TPU v7x, 1024 devices: a whole 4x8x16 slice. The times are simulated.
1024 devices in a mesh: rep: 8 (over x, core), own: 32 (over z_lo, y), blk: 4 (over z_hi).
Axes of the slice: x: 4, y: 8, z: 16 (z_hi: 4, z_lo: 4; z = z_hi * 4 + z_lo), core: 2. Of those that a mesh axis runs over, the one named last changes fastest.
Arguments:
- partial_grads: bfloat16 [8, 64, 1024, 1024], P('rep', 'own', None, 'blk'), may hold values from -6 to 6
- owner_map: int32 [64], replicated, may hold values from 0 to 31, as said below
- iterations: int32 [64], replicated, may hold values from 1 to 2
- slot_history: bfloat16 [32, 4, 1024, 1024], P('own', 'blk'), may hold values from -0.02 to 0.5, as said below
Outputs:
- directions: bfloat16 [64, 1024, 1024], P('own', 'rep', 'blk')
- new_statistic: bfloat16 [32, 4, 1024, 1024], P('own', 'blk', 'rep')
Inputs may be any that keep to these rules, and one draw needn't show every extreme that they name: `owner_map`: the 2 blocks of one home group name different owners; no owner is named by more than 4 blocks in all, and some owner by exactly 4. `slot_history`: each matrix is symmetric.
All inputs are finite; a program needn't handle non-finite values.
Results may differ from a plain program's by a relative error of at most 0.02.
Values may be sent and summed in bfloat16 or wider, within the bound.
No kernel may reach another device: no remote copies, remote signals or barrier semaphores. Data moves between devices by JAX's collectives and lax.ppermute only.
A program may use at most 64 MiB of HBM per device.

v0:
```python
import math

import jax
import jax.numpy as jnp
from jax import lax
from jax.sharding import PartitionSpec as P

ITERS = 2


DECAY = 0.5
DAMPING = 0.05


def statistic_of(grad_full, history_full):
    order_full = grad_full.shape[0]
    gram = jnp.einsum("ik,jk->ij", grad_full, grad_full, preferred_element_type=jnp.float32)
    identity = jnp.eye(order_full, dtype=jnp.float32)
    return (
        DECAY * history_full.astype(jnp.float32)
        + (1.0 - DECAY) * gram / order_full
        + DAMPING * identity
    )


def newton_band(statistic, grad_full, column, width, iter_need):
    order_full = statistic.shape[0]
    frobenius = jnp.sqrt(jnp.sum(statistic * statistic))
    norm_scale = math.sqrt(order_full) / (2.0 * frobenius)
    scaled_half = (statistic * norm_scale).astype(jnp.bfloat16)
    identity = jnp.eye(order_full, dtype=jnp.float32)
    factor_half = (1.5 * identity - 0.5 * scaled_half.astype(jnp.float32)).astype(jnp.bfloat16)
    row_ids = lax.iota(jnp.int32, order_full)[:, None]
    col_ids = column + lax.iota(jnp.int32, width)[None, :]
    eye_band = jnp.where(row_ids == col_ids, 1.0, 0.0).astype(jnp.float32)
    scaled_cols = lax.dynamic_slice_in_dim(scaled_half, column, width, 1).astype(jnp.float32)
    factor_cols = 1.5 * eye_band - 0.5 * scaled_cols
    factor_half_cols = lax.dynamic_slice_in_dim(factor_half, column, width, 1)
    y_cols = jnp.dot(scaled_half, factor_half_cols, preferred_element_type=jnp.float32)
    product = jnp.dot(factor_half, y_cols.astype(jnp.bfloat16), preferred_element_type=jnp.float32)
    update = 1.5 * eye_band - 0.5 * product
    z_cols = jnp.dot(factor_half, update.astype(jnp.bfloat16), preferred_element_type=jnp.float32)
    chosen = jnp.where(iter_need >= ITERS, z_cols, factor_cols)
    raw_band = jnp.einsum(
        "ij,ik->jk", chosen.astype(jnp.bfloat16), grad_full, preferred_element_type=jnp.float32
    )
    return raw_band.astype(jnp.bfloat16)


def body(partial_grads, owner_map, iterations, slot_history):
    summed = lax.psum_scatter(
        partial_grads[0].astype(jnp.float32).astype(jnp.bfloat16),
        "rep",
        scatter_dimension=1,
        tiled=True,
    )
    home_count, band_rows, band_cols = summed.shape
    owners = lax.axis_size("own")
    replicas = lax.axis_size("rep")
    shards = lax.axis_size("blk")
    my_group = lax.axis_index("own")
    my_owners = lax.dynamic_slice_in_dim(owner_map, my_group * home_count, home_count)
    owner_ids = jnp.arange(owners, dtype=jnp.int32)
    send_table = owner_ids[:, None] == my_owners[None, :]
    send_half = send_table.astype(jnp.bfloat16)
    outgoing = jnp.einsum(
        "oi,ixy->oxy", send_half, summed, preferred_element_type=jnp.float32
    ).astype(jnp.bfloat16)
    arrived = lax.all_to_all(outgoing, "own", split_axis=0, concat_axis=0, tiled=True)
    grid_owner = owner_map.reshape(owners, home_count)
    grid_need = iterations.reshape(owners, home_count)
    aimed_here = grid_owner == my_group
    occupied = jnp.sum(jnp.where(aimed_here, 1, 0), axis=1) > 0
    need_from = jnp.sum(jnp.where(aimed_here, grid_need, 0), axis=1)
    occupied_count = jnp.where(occupied, 1, 0)
    earlier = owner_ids[None, :] < owner_ids[:, None]
    slot_rank = jnp.sum(jnp.where(earlier, occupied_count[None, :], 0), axis=1).astype(jnp.int32)
    slot_ids = jnp.arange(shards, dtype=jnp.int32)
    keep_table = (slot_rank[None, :] == slot_ids[:, None]) & occupied[None, :]
    keep_half = keep_table.astype(jnp.bfloat16)
    compacted = jnp.einsum(
        "kh,hxy->kxy", keep_half, arrived, preferred_element_type=jnp.float32
    ).astype(jnp.bfloat16)
    slot_need = jnp.sum(jnp.where(keep_table, need_from[None, :], 0), axis=1)
    iter_need = lax.dynamic_slice_in_dim(slot_need, lax.axis_index("blk"), 1)[0]
    fanned = jnp.broadcast_to(compacted[None], (replicas,) + compacted.shape).reshape(
        replicas * shards, band_rows, band_cols
    )
    received = lax.all_to_all(fanned, ("rep", "blk"), split_axis=0, concat_axis=0, tiled=True)
    grad_full = (
        received.reshape(replicas, shards, band_rows, band_cols)
        .transpose(0, 2, 1, 3)
        .reshape(replicas * band_rows, shards * band_cols)
    )
    history_full = slot_history[0, 0]
    column = lax.axis_index("rep") * band_rows
    statistic = statistic_of(grad_full, history_full)
    stat_rows = lax.dynamic_slice_in_dim(statistic, column, band_rows, 0).astype(jnp.bfloat16)
    history_rows = lax.dynamic_slice_in_dim(history_full, column, band_rows, 0)
    new_rows = jnp.where(iter_need > 0, stat_rows, history_rows)
    raw_half = newton_band(statistic, grad_full, column, band_rows, iter_need)
    dispersed = lax.all_to_all(raw_half[None], "blk", split_axis=2, concat_axis=0, tiled=True)
    going_back = jnp.einsum(
        "kh,kxy->hxy", keep_half, dispersed, preferred_element_type=jnp.float32
    ).astype(jnp.bfloat16)
    homeward = lax.all_to_all(going_back, "own", split_axis=0, concat_axis=0, tiled=True)
    directions = jnp.einsum(
        "oi,oxy->ixy", send_half, homeward, preferred_element_type=jnp.float32
    ).astype(jnp.bfloat16)
    return (directions, new_rows[None, None])


def solution(mesh):
    return jax.shard_map(
        body,
        mesh=mesh,
        in_specs=(P("rep", "own", None, "blk"), P(), P(), P("own", "blk", None, None)),
        out_specs=(P("own", "rep", "blk"), P("own", "blk", "rep", None)),
        check_vma=False,
    )
```

profile of v0, /device:TPU:1, one launch (start us, length us, event | category | flops | bytes accessed | tf_op | source)
XLA Modules:
  0.0 382.6 jit_solution(16991300654298975958)
XLA Ops:
  7.2 0.0 reduce-scatter.2.cloned.1.call-start
  7.2 0.7 reduce-scatter.2.cloned.1.call-update
  7.9 0.7 dynamic_slice.20
  8.6 53.7 %reduce-scatter.2.cloned.1.call-done = bf16[2,128,256]{2,1,0:T(8,128)(2,1)} async-done(((bf16[2,1024,256]{2,1,0:T(8,128)(2,1)}), bf16[2,128,256]{2,1,0:T(8,128)(2,1)}) %reduce-scatter.2.cloned.1.call-update) | async-done | bytes 131088 | tf_op jit(solution)/shard_map/reduce_scatter | solution.py:51
  62.4 1.7 convolution_convert_fusion.1
  64.1 2.5 copy.25
  66.7 0.0 copy-start.1
  66.7 0.0 copy-start.2
  66.7 7.9 %all-to-all-start = ((bf16[32,128,256]{2,1,0:T(8,128)(2,1)}), bf16[32,128,256]{2,1,0:T(8,128)(2,1)S(1)}, u32[]{:S(2)}, u32[]{:S(2)}) async-start(bf16[32,128,256]{2,1,0:T(8,128)(2,1)} %copy.25), calls=%async_computation.1 | async-start | bytes 4194304 | tf_op jit(solution)/shard_map/all_to_all | solution.py:69
  74.5 0.0 copy-done.1
  74.5 0.0 copy-done.2
  74.6 0.1 select_n.64
  74.7 0.1 reduce_sum.45
  74.8 0.1 select_reduce_fusion
  74.9 50.0 %all-to-all-done = bf16[32,128,256]{2,1,0:T(8,128)(2,1)S(1)} async-done(((bf16[32,128,256]{2,1,0:T(8,128)(2,1)}), bf16[32,128,256]{2,1,0:T(8,128)(2,1)S(1)}, u32[]{:S(2)}, u32[]{:S(2)}) %all-to-all-start) | async-done | bytes 2097184 | tf_op jit(solution)/shard_map/all_to_all | solution.py:69
  124.9 1.3 fusion.16
  126.2 1.6 broadcast_in_dim.78
  127.8 30.7 %all-to-all-start.1 = ((bf16[32,128,256]{2,1,0:T(8,128)(2,1)}), bf16[32,128,256]{2,1,0:T(8,128)(2,1)S(1)}, u32[]{:S(2)}, u32[]{:S(2)}) async-start(bf16[32,128,256]{2,1,0:T(8,128)(2,1)} %bitcast.54), calls=%async_computation.2 | async-start | bytes 4194304 | tf_op jit(solution)/shard_map/all_to_all | solution.py:89
  158.6 0.1 select_n.68
  158.7 0.1 reduce_sum.47
  158.8 0.1 select_reduce_fusion.1
  158.9 0.6 dynamic_slice.21
  160.2 89.8 %all-to-all-done.1 = bf16[32,128,256]{2,1,0:T(8,128)(2,1)S(1)} async-done(((bf16[32,128,256]{2,1,0:T(8,128)(2,1)}), bf16[32,128,256]{2,1,0:T(8,128)(2,1)S(1)}, u32[]{:S(2)}, u32[]{:S(2)}) %all-to-all-start.1) | async-done | bytes 2097184 | tf_op jit(solution)/shard_map/all_to_all | solution.py:89
  250.0 2.6 copy.28
  252.6 8.2 %multiply_reduce_fusion = (f32[]{:T(128)}, f32[1024,1024]{1,0:T(8,128)}) fusion(bf16[128,8,8,128]{3,2,1,0:T(8,128)(2,1)} %bitcast.56, bf16[1,1,1024,1024]{3,2,1,0:T(8,128)(2,1)} %param.7), kind=kOutput, calls=%fused_computation.4 | convolution fusion | flops 2156920832 | bytes 8388612 | tf_op jit(solution)/shard_map/ik,jk->ij/dot_general | solution.py:17
  261.5 5.2 %subtract_convert_fusion = (bf16[1024,1024]{1,0:T(8,128)(2,1)}, bf16[1024,1024]{1,0:T(8,128)(2,1)}) fusion(f32[1024,1024]{1,0:T(8,128)} %get-tuple-element.17, f32[]{:T(128)S(6)} %div.11), kind=kLoop, calls=%fused_computation.2 | loop fusion | flops 8388608 | bytes 8388612 | tf_op jit(solution)/shard_map/convert_element_type | solution.py:32
  266.7 0.0 copy-start
  266.7 4.6 %fusion.11 = bf16[1024,128]{1,0:T(8,128)(2,1)S(1)} fusion(bf16[1024,1024]{1,0:T(8,128)(2,1)} %get-tuple-element.12, bf16[1024,1024]{1,0:T(8,128)(2,1)} %get-tuple-element.13, s32[]{:T(128)S(6)} %select_n.73, s32[128]{0:T(128)S(1)} %iota_add_fusion), kind=kOutput, calls=%fused_computation.20 | convolution fusion | flops 537788416 | bytes 4719108 | tf_op jit(solution)/shard_map/dot_general | solution.py:40
  271.3 0.0 copy-done
  271.3 3.9 %fusion.19 = bf16[1,128,1024]{2,1,0:T(8,128)(2,1)S(1)} fusion(bf16[128,8,8,128]{3,2,1,0:T(8,128)(2,1)S(1)} %bitcast.57, bf16[1024,128]{1,0:T(8,128)(2,1)S(1)} %fusion.11, bf16[1024,1024]{1,0:T(8,128)(2,1)} %get-tuple-element.13, s32[]{:T(128)S(6)} %select_n.73, s32[128]{0:T(128)S(1)} %iota_add_fusion, pred[]{:T(512)} %bitcast.2), kind=kOutput, calls=%fused_computation.25 | convolution fusion | flops 544342016 | bytes 4981764 | tf_op jit(solution)/shard_map/ij,ik->jk/dot_general | solution.py:44
  275.2 0.4 copy.29
  275.6 0.5 broadcast.73
  276.1 2.2 reduce
  278.3 0.1 reshape.51
  278.4 19.6 %all_to_all.33 = bf16[4,2,16384]{2,1,0:T(2,128)(2,1)S(1)} all-to-all(bf16[4,2,16384]{2,1,0:T(2,128)(2,1)S(1)} %reshape.51), channel_id=1, replica_groups=mesh['rep'=8,'own'=32,'blk'=4] {'blk'}, dimensions={0} | all-to-all | bytes 524288 | tf_op jit(solution)/shard_map/all_to_all | solution.py:102
  298.0 0.3 reshape.52
  298.4 0.2 copy.34
  298.6 0.8 convolution_convert_fusion
  299.3 2.5 copy.31
  301.9 17.6 %all-to-all-start.3 = ((bf16[32,128,256]{2,1,0:T(8,128)(2,1)}), bf16[32,128,256]{2,1,0:T(8,128)(2,1)S(1)}, u32[]{:S(2)}, u32[]{:S(2)}) async-start(bf16[32,128,256]{2,1,0:T(8,128)(2,1)} %copy.31), calls=%async_computation.4 | async-start | bytes 4194304 | tf_op jit(solution)/shard_map/all_to_all | solution.py:106
  320.1 1.9 fusion.29
  321.9 51.9 %all-to-all-done.3 = bf16[32,128,256]{2,1,0:T(8,128)(2,1)S(1)} async-done(((bf16[32,128,256]{2,1,0:T(8,128)(2,1)}), bf16[32,128,256]{2,1,0:T(8,128)(2,1)S(1)}, u32[]{:S(2)}, u32[]{:S(2)}) %all-to-all-start.3) | async-done | bytes 2097184 | tf_op jit(solution)/shard_map/all_to_all | solution.py:106
  373.9 1.3 fusion.22
  375.1 0.7 copy.33
  (6 shorter events, 0.1 us)
Async XLA Ops:
  7.2 55.2 %reduce-scatter.2.cloned.1.call-start = ((), (), s32[]{:S(2)}) async-start(), calls=%async_computation.5 | async-start | bytes 1179648 | tf_op jit(solution)/shard_map/reduce_scatter | solution.py:51
  66.7 7.9 %copy-start.1 = (s32[64]{0:T(128)S(1)}, s32[64]{0:T(128)}, u32[]{:S(2)}) copy-start(s32[64]{0:T(128)} %param.5) | copy-start | bytes 772
  66.7 7.9 %copy-start.2 = (s32[64]{0:T(128)S(1)}, s32[64]{0:T(128)}, u32[]{:S(2)}) copy-start(s32[64]{0:T(128)} %param.6) | copy-start | bytes 772
  66.7 58.3 %all-to-all-start = ((bf16[32,128,256]{2,1,0:T(8,128)(2,1)}), bf16[32,128,256]{2,1,0:T(8,128)(2,1)S(1)}, u32[]{:S(2)}, u32[]{:S(2)}) async-start(bf16[32,128,256]{2,1,0:T(8,128)(2,1)} %copy.25), calls=%async_computation.1 | async-start | bytes 4194304 | tf_op jit(solution)/shard_map/all_to_all | solution.py:69
  127.8 122.1 %all-to-all-start.1 = ((bf16[32,128,256]{2,1,0:T(8,128)(2,1)}), bf16[32,128,256]{2,1,0:T(8,128)(2,1)S(1)}, u32[]{:S(2)}, u32[]{:S(2)}) async-start(bf16[32,128,256]{2,1,0:T(8,128)(2,1)} %bitcast.54), calls=%async_computation.2 | async-start | bytes 4194304 | tf_op jit(solution)/shard_map/all_to_all | solution.py:89
  266.7 4.6 %copy-start = (bf16[8,128,4,256]{1,0,3,2:T(8,128)(2,1)S(1)}, bf16[8,128,4,256]{1,0,3,2:T(8,128)(2,1)}, u32[]{:S(2)}) copy-start(bf16[8,128,4,256]{1,0,3,2:T(8,128)(2,1)} %copy.28) | copy-start | bytes 6291460
  301.9 72.0 %all-to-all-start.3 = ((bf16[32,128,256]{2,1,0:T(8,128)(2,1)}), bf16[32,128,256]{2,1,0:T(8,128)(2,1)S(1)}, u32[]{:S(2)}, u32[]{:S(2)}) async-start(bf16[32,128,256]{2,1,0:T(8,128)(2,1)} %copy.31), calls=%async_computation.4 | async-start | bytes 4194304 | tf_op jit(solution)/shard_map/all_to_all | solution.py:106
Sparse Core Ops, SparseCore 0:
  11.4 50.9 reduce-scatter.1
where the time goes:
time: 384 us; the launch traced here: 383 us
  waiting for transfers between devices  246 us (64%)
  starting transfers between devices  56.2 us (15%)
  matrix products  21.7 us (6%)
  blocking collectives  19.6 us (5%)
  between operations  16.3 us (4%)
  local copies, waits for them, and re-layouts  13 us (3%)
  other arithmetic  9.74 us (3%)
    all_to_all x1, waiting for transfers between devices, body(): lax.all_to_all(fanned, ('rep', 'blk'), split_axis=0, concat_axis=0, tiled...  89.8 us
    reduce_scatter x1, waiting for transfers between devices, body(): lax.psum_scatter(partial_grads[0].astype(jnp.float32).astype(jnp.bfloat16...  53.7 us
    all_to_all x1, waiting for transfers between devices, body(): lax.all_to_all(going_back, 'own', split_axis=0, concat_axis=0, tiled=True)  51.9 us
    all_to_all x1, waiting for transfers between devices, body(): lax.all_to_all(outgoing, 'own', split_axis=0, concat_axis=0, tiled=True)  50 us
    all_to_all x1, starting transfers between devices, body(): lax.all_to_all(fanned, ('rep', 'blk'), split_axis=0, concat_axis=0, tiled...  30.7 us
    all_to_all x1, blocking collectives, body(): lax.all_to_all(raw_half[None], 'blk', split_axis=2, concat_axis=0, tiled=...  19.6 us
    all_to_all x1, starting transfers between devices, body(): lax.all_to_all(going_back, 'own', split_axis=0, concat_axis=0, tiled=True)  17.6 us
    dot_general x1, matrix products, statistic_of(): jnp.einsum('ik,jk->ij', grad_full, grad_full, preferred_element_type=jnp....  8.24 us
  transfers between devices with their start and end apart: 4, of which 4 were waited for; matrix products, arithmetic and copies ran while one was open for 1% of the time, Pallas kernels for 0%

commit v1 on v0

v1 whole, which is shorter than its diff:
```python
import functools
import math

import jax
import jax.numpy as jnp
from jax import lax
from jax.experimental import pallas as pl
from jax.experimental.pallas import tpu as pltpu
from jax.sharding import PartitionSpec as P

ITERS = 2


DECAY = 0.5
DAMPING = 0.05


def gram_kernel(place, mine, other, out):
    shards = mine.shape[0]
    home_count, band_rows = out.shape[0], out.shape[1]
    for block in range(home_count):
        parts = []
        for half in range(other.shape[0]):
            total = jnp.zeros((band_rows, band_rows), jnp.float32)
            for shard in range(shards):
                total = total + lax.dot_general(
                    mine[shard, block],
                    other[half, shard, block],
                    (((1,), (1,)), ((), ())),
                    preferred_element_type=jnp.float32,
                )
            parts.append(total)
        out[block] = jnp.concatenate(parts, axis=1)


def gram_tile(place, mine, gathered):
    replicas, shards, home_count, band_rows, band_cols = gathered.shape
    span = band_cols // band_rows
    return pl.pallas_call(
        gram_kernel,
        out_shape=jax.ShapeDtypeStruct((home_count, band_rows, band_cols), jnp.float32),
        grid_spec=pltpu.PrefetchScalarGridSpec(
            num_scalar_prefetch=1,
            grid=(1,),
            in_specs=[
                pl.BlockSpec(mine.shape, lambda i, place: (0, 0, 0, 0)),
                pl.BlockSpec(
                    (span, shards, home_count, band_rows, band_cols),
                    lambda i, place: (place[1], 0, 0, 0, 0),
                ),
            ],
            out_specs=pl.BlockSpec((home_count, band_rows, band_cols), lambda i, place: (0, 0, 0)),
        ),
        compiler_params=pltpu.CompilerParams(vmem_limit_bytes=32 * 1024 * 1024),
    )(place, mine, gathered)


def newton_kernel(place, need, stat, cols, out, scaled, factor):
    replicas, shards, _, band_rows, band_cols = stat.shape
    order_full = replicas * band_rows
    block = pl.program_id(0)
    squares = jnp.zeros((8, band_cols), jnp.float32)
    for band in range(replicas):
        for shard in range(shards):
            tile = stat[band, shard, 0].astype(jnp.float32)
            squares = squares + jnp.sum((tile * tile).reshape(-1, 8, band_cols), axis=0)
    frobenius = jnp.sqrt(jnp.sum(squares, keepdims=True)[:1, :1])
    norm_scale = math.sqrt(order_full) / (2.0 * frobenius)
    row_ids = lax.broadcasted_iota(jnp.int32, (band_rows, band_cols), 0)
    col_ids = lax.broadcasted_iota(jnp.int32, (band_rows, band_cols), 1)
    for band in range(replicas):
        for shard in range(shards):
            tile = (stat[band, shard, 0].astype(jnp.float32) * norm_scale).astype(jnp.bfloat16)
            rows, columns = pl.ds(band * band_rows, band_rows), pl.ds(shard * band_cols, band_cols)
            scaled[rows, columns] = tile
            rest = -0.5 * tile.astype(jnp.float32)
            if (band * band_rows) // band_cols == shard:
                diagonal = row_ids + (band * band_rows - shard * band_cols) == col_ids
                rest = rest + jnp.where(diagonal, 1.5, 0.0)
            factor[rows, columns] = rest.astype(jnp.bfloat16)
    first = pl.multiple_of(place[0] * band_rows, band_rows)
    mine = factor[pl.ds(first, band_rows), :]
    product = jnp.dot(mine, scaled[...], preferred_element_type=jnp.float32).astype(jnp.bfloat16)
    product = jnp.dot(product, factor[...], preferred_element_type=jnp.float32)
    wide_rows = lax.broadcasted_iota(jnp.int32, (band_rows, order_full), 0) + first
    wide_cols = lax.broadcasted_iota(jnp.int32, (band_rows, order_full), 1)
    update = jnp.where(wide_rows == wide_cols, 1.5, 0.0) - 0.5 * product
    second = jnp.dot(update.astype(jnp.bfloat16), factor[...], preferred_element_type=jnp.float32)
    root = jnp.where(need[block] >= ITERS, second, mine.astype(jnp.float32)).astype(jnp.bfloat16)
    total = jnp.zeros((band_rows, band_cols), jnp.float32)
    for band in range(replicas):
        total = total + jnp.dot(
            root[:, band * band_rows : (band + 1) * band_rows],
            cols[band, 0, 0],
            preferred_element_type=jnp.float32,
        )
    out[0] = total.astype(jnp.bfloat16)


def newton_tile(place, need, stat, gathered):
    replicas, shards, home_count, band_rows, band_cols = stat.shape
    order_full = replicas * band_rows
    return pl.pallas_call(
        newton_kernel,
        out_shape=jax.ShapeDtypeStruct((home_count, band_rows, band_cols), jnp.bfloat16),
        grid_spec=pltpu.PrefetchScalarGridSpec(
            num_scalar_prefetch=2,
            grid=(home_count,),
            in_specs=[
                pl.BlockSpec(
                    (replicas, shards, 1, band_rows, band_cols),
                    lambda i, place, need: (0, 0, i, 0, 0),
                ),
                pl.BlockSpec(
                    (replicas, 1, 1, band_rows, band_cols),
                    lambda i, place, need: (0, place[1], i, 0, 0),
                ),
            ],
            out_specs=pl.BlockSpec((1, band_rows, band_cols), lambda i, place, need: (i, 0, 0)),
            scratch_shapes=[
                pltpu.VMEM((order_full, order_full), jnp.bfloat16),
                pltpu.VMEM((order_full, order_full), jnp.bfloat16),
            ],
        ),
        compiler_params=pltpu.CompilerParams(vmem_limit_bytes=40 * 1024 * 1024),
    )(place, need, stat, gathered)


def exchange(array, axis):
    return lax.all_to_all(array, axis, split_axis=0, concat_axis=0, tiled=True)


def spread(tiles, targets, count):
    ids = lax.broadcasted_iota(jnp.int32, (count, 1, 1), 0)
    out = jnp.zeros((count,) + tiles.shape[1:], tiles.dtype)
    for index in range(tiles.shape[0]):
        out = jnp.where(ids == targets[index], tiles[index][None], out)
    return out


def pick(tiles, index):
    return lax.dynamic_index_in_dim(tiles, index, 0, keepdims=False)


def body(partial_grads, owner_map, iterations, slot_history):
    owners = lax.axis_size("own")
    replicas = lax.axis_size("rep")
    shards = lax.axis_size("blk")
    my_rep, my_own, my_blk = lax.axis_index("rep"), lax.axis_index("own"), lax.axis_index("blk")
    _, home_count, order_full, band_cols = partial_grads.shape
    band_rows = order_full // replicas
    total_blocks = owner_map.shape[0]
    history = slot_history[0, 0]

    outgoing = (
        partial_grads[0]
        .reshape(home_count, replicas, band_rows, band_cols)
        .transpose(1, 0, 2, 3)
    )
    partials = exchange(outgoing, "rep")
    grad_tile = jnp.sum(partials.astype(jnp.float32), axis=0).astype(jnp.bfloat16)

    grad_band = lax.all_gather(grad_tile, "blk", axis=0, tiled=False)
    grad_full = lax.all_gather(grad_band, "rep", axis=0, tiled=False)

    position = jnp.arange(total_blocks, dtype=jnp.int32)
    same = owner_map[:, None] == owner_map[None, :]
    slot = jnp.sum(jnp.where(same & (position[None, :] < position[:, None]), 1, 0), axis=1)
    slot_ids = jnp.arange(shards, dtype=jnp.int32)
    held = (owner_map[None, :] == my_own) & (slot[None, :] == slot_ids[:, None])
    holder = jnp.sum(jnp.where(held, position[None, :] + 1, 0), axis=1)
    home_of = jnp.where(holder > 0, (holder - 1) // home_count, -1)
    my_owners = lax.dynamic_slice_in_dim(owner_map, my_own * home_count, home_count)
    my_need = lax.dynamic_slice_in_dim(iterations, my_own * home_count, home_count)

    history_rows = lax.dynamic_slice_in_dim(history, my_rep * band_rows, band_rows, 0)
    history_rows, _ = lax.optimization_barrier((history_rows, grad_tile))
    history_parts = history_rows.reshape(band_rows, shards, band_cols).transpose(1, 0, 2)
    history_tiles = exchange(history_parts, "blk")
    history_sent = spread(history_tiles, home_of, owners)
    history_came = exchange(history_sent, "own")
    history_mine = jnp.stack([pick(history_came, my_owners[i]) for i in range(home_count)])

    place = jnp.stack([my_rep, my_blk]).astype(jnp.int32)
    gram = gram_tile(place, grad_band, grad_full) * ((1.0 - DECAY) / order_full)
    row_ids = my_rep * band_rows + lax.broadcasted_iota(jnp.int32, (band_rows, band_cols), 0)
    col_ids = my_blk * band_cols + lax.broadcasted_iota(jnp.int32, (band_rows, band_cols), 1)
    damping = jnp.where(row_ids == col_ids, DAMPING, 0.0)
    stat_tile = (DECAY * history_mine.astype(jnp.float32) + gram + damping).astype(jnp.bfloat16)

    stat_band = lax.all_gather(stat_tile, "blk", axis=0, tiled=False)
    stat_full = lax.all_gather(stat_band, "rep", axis=0, tiled=False)

    gram_sent = spread(gram.astype(jnp.bfloat16), my_owners, owners)
    gram_came = exchange(gram_sent, "own")
    gram_slots = jnp.stack([pick(gram_came, jnp.maximum(home_of[i], 0)) for i in range(shards)])
    gram_rows = exchange(gram_slots, "blk").transpose(1, 0, 2).reshape(band_rows, order_full)
    own_rows = lax.dynamic_slice_in_dim(history, my_rep * band_rows, band_rows, 0)
    wide_rows = my_rep * band_rows + lax.broadcasted_iota(jnp.int32, (band_rows, order_full), 0)
    wide_cols = lax.broadcasted_iota(jnp.int32, (band_rows, order_full), 1)
    fresh = (
        DECAY * own_rows.astype(jnp.float32)
        + gram_rows.astype(jnp.float32)
        + jnp.where(wide_rows == wide_cols, DAMPING, 0.0)
    ).astype(jnp.bfloat16)
    occupied = lax.dynamic_index_in_dim(holder, my_blk, 0, keepdims=False) > 0
    new_rows = jnp.where(occupied, fresh, own_rows)

    directions = newton_tile(place, my_need, stat_full, grad_full)
    return (directions, new_rows[None, None])


def solution(mesh):
    return jax.shard_map(
        body,
        mesh=mesh,
        in_specs=(P("rep", "own", None, "blk"), P(), P(), P("own", "blk", None, None)),
        out_specs=(P("own", "rep", "blk"), P("own", "blk", "rep", None)),
        check_vma=False,
    )
```

time: 384 us -> 368 us (0.958)
  waiting for transfers between devices: 246 us -> 142 us
  blocking collectives: 19.6 us -> 107 us
  matrix products: 21.7 us -> 0 us
  Pallas kernels: 0 us -> 7.64 us
  starting transfers between devices: 56.2 us -> 62.8 us
  between operations: 16.3 us -> 21 us
    all_to_all x3 -> x5, waiting for transfers between devices: 192 us -> 24.2 us  [exchange(): return lax.all_to_all(array, axis, split_axis=0, concat_axis=0, tiled=True)]
    all_gather x0 -> x2, waiting for transfers between devices: none -> 118 us  [the longest x1 61.8 us: body(): grad_full = lax.all_gather(grad_band, 'rep', axis=0, tiled=False)]
    all_gather x0 -> x2, blocking collectives: none -> 107 us  [the longest x1 55.7 us: body(): stat_band = lax.all_gather(stat_tile, 'blk', axis=0, tiled=False)]
    reduce_scatter x1 -> x0, waiting for transfers between devices: 53.7 us -> none  [body(): lax.psum_scatter(partial_grads[0].astype(jnp.float32).astype(jnp.bfloat16...]
    dot_general x7 -> x0, matrix products: 21.7 us -> none  [the longest x1 8.24 us: statistic_of(): jnp.einsum('ik,jk->ij', grad_full, grad_full, preferred_element_type=jnp....]
    all_to_all x1 -> x0, blocking collectives: 19.6 us -> none  [body(): lax.all_to_all(raw_half[None], 'blk', split_axis=2, concat_axis=0, tiled=...]
    unnamed x11 -> x16, local copies, waits for them, and re-layouts: 1.57 us -> 9.31 us
    pallas_call x0 -> x2, Pallas kernels: none -> 7.64 us  [the longest x1 6.67 us: newton_tile(): pl.pallas_call(newton_kernel, out_shape=jax.ShapeDtypeStruct((home_count,...]
  transfers between devices with their start and end apart: 4 -> 7, of which waited for: 4 -> 4; matrix products, arithmetic and copies ran while one was open for 1% -> 2% of each run, Pallas kernels for 0% -> 2%
where the time goes in v1:
time: 368 us; the launch traced here: 367 us
  waiting for transfers between devices  142 us (39%)
  blocking collectives  107 us (29%)
  starting transfers between devices  62.8 us (17%)
  between operations  21 us (6%)
  local copies, waits for them, and re-layouts  16.3 us (4%)
  other arithmetic  9.85 us (3%)
  Pallas kernels  7.64 us (2%)
    all_to_all x5, starting transfers between devices, exchange(): return lax.all_to_all(array, axis, split_axis=0, concat_axis=0, tiled=True)  62.7 us
    all_gather x1, waiting for transfers between devices, body(): grad_full = lax.all_gather(grad_band, 'rep', axis=0, tiled=False)  61.8 us
    all_gather x1, waiting for transfers between devices, body(): stat_full = lax.all_gather(stat_band, 'rep', axis=0, tiled=False)  56.1 us
    all_gather x1, blocking collectives, body(): stat_band = lax.all_gather(stat_tile, 'blk', axis=0, tiled=False)  55.7 us
    all_gather x1, blocking collectives, body(): grad_band = lax.all_gather(grad_tile, 'blk', axis=0, tiled=False)  51.6 us
    all_to_all x5, waiting for transfers between devices, exchange(): return lax.all_to_all(array, axis, split_axis=0, concat_axis=0, tiled=True)  24.2 us
    unnamed x16, local copies, waits for them, and re-layouts  9.31 us
  transfers between devices with their start and end apart: 7, of which 4 were waited for; matrix products, arithmetic and copies ran while one was open for 2% of the time, Pallas kernels for 2%

profile of v1, /device:TPU:1, one launch (start us, length us, event | category | flops | bytes accessed | tf_op | source)
XLA Modules:
  0.0 367.0 jit_solution(4907904947408598860)
XLA Ops:
  7.2 2.5 copy.29
  9.6 17.7 %all-to-all-start = ((bf16[8,2,128,256]{3,2,1,0:T(8,128)(2,1)}), bf16[8,2,128,256]{3,2,1,0:T(8,128)(2,1)S(1)}, u32[]{:S(2)}, u32[]{:S(2)}) async-start(bf16[8,2,128,256]{3,2,1,0:T(8,128)(2,1)} %copy.29), calls=%async_computation | async-start | bytes 2097152 | tf_op jit(solution)/shard_map/all_to_all | solution.py:130
  27.4 0.8 copy.36
  28.3 14.2 %all-to-all-done = bf16[8,2,128,256]{3,2,1,0:T(8,128)(2,1)S(1)} async-done(((bf16[8,2,128,256]{3,2,1,0:T(8,128)(2,1)}), bf16[8,2,128,256]{3,2,1,0:T(8,128)(2,1)S(1)}, u32[]{:S(2)}, u32[]{:S(2)}) %all-to-all-start) | async-done | bytes 1048608 | tf_op jit(solution)/shard_map/all_to_all | solution.py:130
  42.5 0.1 reduce_sum.32
  42.6 6.6 %all-to-all-start.1 = ((bf16[4,128,256]{1,2,0:T(8,128)(2,1)}), bf16[4,128,256]{1,2,0:T(8,128)(2,1)S(1)}, u32[]{:S(2)}, u32[]{:S(2)}) async-start(bf16[4,128,256]{1,2,0:T(8,128)(2,1)} %bitcast.7), calls=%async_computation.1 | async-start | bytes 524288 | tf_op jit(solution)/shard_map/all_to_all | solution.py:130
  49.3 0.2 select_reduce_fusion
  49.4 0.1 select_reduce_fusion.1
  49.6 0.6 fusion.4
  50.2 1.2 iota_compare_fusion.5
  51.4 1.1 iota_compare_fusion.7
  52.5 9.9 %all-to-all-done.1 = bf16[4,128,256]{1,2,0:T(8,128)(2,1)S(1)} async-done(((bf16[4,128,256]{1,2,0:T(8,128)(2,1)}), bf16[4,128,256]{1,2,0:T(8,128)(2,1)S(1)}, u32[]{:S(2)}, u32[]{:S(2)}) %all-to-all-start.1) | async-done | bytes 262176 | tf_op jit(solution)/shard_map/all_to_all | solution.py:130
  62.4 0.1 copy.30
  62.6 0.1 copy.31
  62.7 0.1 copy.32
  62.8 0.1 copy.33
  62.9 1.9 select_select_fusion.1
  64.8 15.4 %all-to-all-start.2 = ((bf16[32,128,256]{2,1,0:T(8,128)(2,1)}), bf16[32,128,256]{2,1,0:T(8,128)(2,1)}, u32[]{:S(2)}, u32[]{:S(2)}) async-start(bf16[32,128,256]{2,1,0:T(8,128)(2,1)} %select_select_fusion.1), calls=%async_computation.2 | async-start | bytes 4194304 | tf_op jit(solution)/shard_map/all_to_all | solution.py:130
  80.2 0.0 all-gather.7.cloned.1.call-start
  80.3 51.6 %all-gather = bf16[8,128,256]{2,1,0:T(8,128)(2,1)} all-gather(bf16[2,128,256]{2,1,0:T(8,128)(2,1)S(1)} %reduce_sum.32), channel_id=2, replica_groups=mesh['rep'=8,'own'=32,'blk'=4] {'blk'}, dimensions={0}, use_global_device_ids=true | all-gather | bytes 655360 | tf_op jit(solution)/shard_map/all_gather | solution.py:163
  131.9 0.0 all-gather.7.cloned.1.call-update
  132.0 0.1 dynamic_slice.38
  132.0 0.7 fusion.3
  136.5 0.1 pad_add_fusion.place
  136.6 1.3 iota_compare_fusion.3
  137.9 0.1 compare_select_fusion
  138.0 61.8 %all-gather.7.cloned.1.call-done = bf16[32,2,128,256]{3,2,1,0:T(8,128)(2,1)} async-done(((bf16[4,2,128,256]{3,2,1,0:T(8,128)(2,1)}), bf16[32,2,128,256]{3,2,1,0:T(8,128)(2,1)}) %all-gather.7.cloned.1.call-update) | async-done | bytes 4194320 | tf_op jit(solution)/shard_map/all_gather | solution.py:164
  199.7 2.2 copy-done.1
  201.9 1.0 copy-done.3
  203.0 1.0 shard_map.59
  204.0 0.9 constant_dynamic-slice_fusion.5
  204.8 0.1 multiply_convert_fusion
  204.9 1.7 select_select_fusion
  206.6 10.2 %all-to-all-start.3 = ((bf16[32,128,256]{2,1,0:T(8,128)(2,1)}), bf16[32,128,256]{2,1,0:T(8,128)(2,1)}, u32[]{:S(2)}, u32[]{:S(2)}) async-start(bf16[32,128,256]{2,1,0:T(8,128)(2,1)} %select_select_fusion), calls=%async_computation.3 | async-start | bytes 4194304 | tf_op jit(solution)/shard_map/all_to_all | solution.py:130
  216.8 0.0 all-gather.9.cloned.1.call-start
  216.9 55.7 %all-gather.2 = bf16[8,128,256]{2,1,0:T(8,128)(2,1)} all-gather(bf16[2,128,256]{2,1,0:T(8,128)(2,1)S(1)} %get-tuple-element.19), channel_id=4, replica_groups=mesh['rep'=8,'own'=32,'blk'=4] {'blk'}, dimensions={0}, use_global_device_ids=true | all-gather | bytes 655360 | tf_op jit(solution)/shard_map/all_gather | solution.py:191
  274.9 1.0 constant_dynamic-slice_fusion.3
  275.9 0.7 pad_maximum_fusion
  276.7 12.7 %all-to-all-start.4 = ((bf16[4,128,256]{2,1,0:T(8,128)(2,1)}), bf16[4,128,256]{2,1,0:T(8,128)(2,1)S(1)}, u32[]{:S(2)}, u32[]{:S(2)}) async-start(bf16[4,128,256]{2,1,0:T(8,128)(2,1)} %pad_maximum_fusion), calls=%async_computation.4 | async-start | bytes 524288 | tf_op jit(solution)/shard_map/all_to_all | solution.py:130
  289.4 0.6 dynamic_slice.41
  290.0 0.1 dynamic_slice.35.need
  290.7 56.1 %all-gather.9.cloned.1.call-done = bf16[32,2,128,256]{3,2,1,0:T(8,128)(2,1)} async-done(((bf16[4,2,128,256]{3,2,1,0:T(8,128)(2,1)}), bf16[32,2,128,256]{3,2,1,0:T(8,128)(2,1)}) %all-gather.9.cloned.1.call-update) | async-done | bytes 4194320 | tf_op jit(solution)/shard_map/all_gather | solution.py:192
  346.8 2.2 copy-done.2
  349.0 2.2 copy-done.4
  351.2 6.7 %shard_map.60 = bf16[2,128,256]{2,1,0:T(8,128)(2,1)} custom-call(s32[2]{0:T(128)S(1)} %pad_add_fusion.place, s32[2]{0:T(128)S(1)} %dynamic_slice.35.need, bf16[8,4,2,128,256]{4,3,2,1,0:T(8,128)(2,1)S(1)} %bitcast.39, bf16[8,4,2,128,256]{4,3,2,1,0:T(8,128)(2,1)S(1)} %bitcast.36), custom_call_target="tpu_custom_call" | custom-call | tf_op jit(solution)/shard_map/pallas_call | solution.py:103
  357.9 0.2 copy.34
  358.1 1.2 fusion
  359.3 0.9 copy.35
  (23 shorter events, 0.2 us)
Async XLA Ops:
  7.2 20.2 %copy-start = (bf16[1,1,1024,1024]{3,2,1,0:T(8,128)(2,1)S(1)}, bf16[1,1,1024,1024]{3,2,1,0:T(8,128)(2,1)}, u32[]{:S(2)}) copy-start(bf16[1,1,1024,1024]{3,2,1,0:T(8,128)(2,1)} %param.7) | copy-start | bytes 6291460
  9.6 18.6 %copy-start.5 = (s32[64]{0:T(128)S(1)}, s32[64]{0:T(128)}, u32[]{:S(2)}) copy-start(s32[64]{0:T(128)} %param.5) | copy-start | bytes 772
  9.6 32.9 %all-to-all-start = ((bf16[8,2,128,256]{3,2,1,0:T(8,128)(2,1)}), bf16[8,2,128,256]{3,2,1,0:T(8,128)(2,1)S(1)}, u32[]{:S(2)}, u32[]{:S(2)}) async-start(bf16[8,2,128,256]{3,2,1,0:T(8,128)(2,1)} %copy.29), calls=%async_computation | async-start | bytes 2097152 | tf_op jit(solution)/shard_map/all_to_all | solution.py:130
  42.6 19.8 %all-to-all-start.1 = ((bf16[4,128,256]{1,2,0:T(8,128)(2,1)}), bf16[4,128,256]{1,2,0:T(8,128)(2,1)S(1)}, u32[]{:S(2)}, u32[]{:S(2)}) async-start(bf16[4,128,256]{1,2,0:T(8,128)(2,1)} %bitcast.7), calls=%async_computation.1 | async-start | bytes 524288 | tf_op jit(solution)/shard_map/all_to_all | solution.py:130
  64.8 139.1 %all-to-all-start.2 = ((bf16[32,128,256]{2,1,0:T(8,128)(2,1)}), bf16[32,128,256]{2,1,0:T(8,128)(2,1)}, u32[]{:S(2)}, u32[]{:S(2)}) async-start(bf16[32,128,256]{2,1,0:T(8,128)(2,1)} %select_select_fusion.1), calls=%async_computation.2 | async-start | bytes 4194304 | tf_op jit(solution)/shard_map/all_to_all | solution.py:130
  80.2 119.5 %all-gather.7.cloned.1.call-start = ((), (), s32[]{:S(2)}) async-start(), calls=%async_computation.5 | async-start | bytes 4718592 | tf_op jit(solution)/shard_map/all_gather | solution.py:164
  199.7 2.2 copy-start.1
  201.9 1.0 copy-start.3
  206.6 68.3 %all-to-all-start.3 = ((bf16[32,128,256]{2,1,0:T(8,128)(2,1)}), bf16[32,128,256]{2,1,0:T(8,128)(2,1)}, u32[]{:S(2)}, u32[]{:S(2)}) async-start(bf16[32,128,256]{2,1,0:T(8,128)(2,1)} %select_select_fusion), calls=%async_computation.3 | async-start | bytes 4194304 | tf_op jit(solution)/shard_map/all_to_all | solution.py:130
  216.8 73.1 %copy-start.6 = (s32[64]{0:T(128)S(1)}, s32[64]{0:T(128)}, u32[]{:S(2)}) copy-start(s32[64]{0:T(128)} %param.6) | copy-start | bytes 772
  216.8 130.0 %all-gather.9.cloned.1.call-start = ((), (), s32[]{:S(2)}) async-start(), calls=%async_computation.6 | async-start | bytes 4718592 | tf_op jit(solution)/shard_map/all_gather | solution.py:192
  276.7 81.2 %all-to-all-start.4 = ((bf16[4,128,256]{2,1,0:T(8,128)(2,1)}), bf16[4,128,256]{2,1,0:T(8,128)(2,1)S(1)}, u32[]{:S(2)}, u32[]{:S(2)}) async-start(bf16[4,128,256]{2,1,0:T(8,128)(2,1)} %pad_maximum_fusion), calls=%async_computation.4 | async-start | bytes 524288 | tf_op jit(solution)/shard_map/all_to_all | solution.py:130
  346.8 2.2 copy-start.2
  349.0 2.2 copy-start.4
Sparse Core Ops, SparseCore 0:
  132.1 67.6 all-gather.6
  272.8 74.0 all-gather.8

commit v2 on v1

v2 whole, which is shorter than its diff:
```python
import functools
import math

import jax
import jax.numpy as jnp
from jax import lax
from jax.experimental import pallas as pl
from jax.experimental.pallas import tpu as pltpu
from jax.sharding import Mesh, PartitionSpec as P

ITERS = 2


DECAY = 0.5
DAMPING = 0.05

REP = ("x", "core")
OWN = ("zl", "y")
BLK = "zh"
RING = ("zl", "zh")
BIG = pltpu.CompilerParams(vmem_limit_bytes=40 * 1024 * 1024)


def take_kernel(index, tiles, out):
    for place in range(out.shape[0]):
        out[place] = tiles[index[place]]


def take(tiles, index):
    return pl.pallas_call(
        take_kernel,
        out_shape=jax.ShapeDtypeStruct((index.shape[0],) + tiles.shape[1:], tiles.dtype),
        in_specs=[
            pl.BlockSpec(memory_space=pltpu.SMEM),
            pl.BlockSpec(memory_space=pltpu.VMEM),
        ],
        out_specs=pl.BlockSpec(memory_space=pltpu.VMEM),
        compiler_params=BIG,
    )(index, tiles)


def cut_kernel(place, rows, out):
    width = out.shape[2]
    for shard in range(out.shape[0]):
        out[shard] = rows[:, shard * width : (shard + 1) * width]


def cut_rows(place, history, shards, band_rows):
    order_full = history.shape[1]
    shape = (shards, band_rows, order_full // shards)
    return pl.pallas_call(
        cut_kernel,
        out_shape=jax.ShapeDtypeStruct(shape, history.dtype),
        grid_spec=pltpu.PrefetchScalarGridSpec(
            num_scalar_prefetch=1,
            grid=(1,),
            in_specs=[pl.BlockSpec((band_rows, order_full), lambda i, place: (place[0], 0))],
            out_specs=pl.BlockSpec(shape, lambda i, place: (0, 0, 0)),
        ),
        compiler_params=BIG,
    )(place, history)


def gram_kernel(place, mine, other, out, half_out):
    shards = mine.shape[0]
    home_count, band_rows = out.shape[0], out.shape[1]
    order_full = shards * out.shape[2]
    for block in range(home_count):
        for half in range(other.shape[0]):
            total = jnp.zeros((band_rows, band_rows), jnp.float32)
            for shard in range(shards):
                total = total + lax.dot_general(
                    mine[shard, block],
                    other[half, shard, block],
                    (((1,), (1,)), ((), ())),
                    preferred_element_type=jnp.float32,
                )
            total = total * ((1.0 - DECAY) / order_full)
            columns = slice(half * band_rows, (half + 1) * band_rows)
            out[block, :, columns] = total
            half_out[block, :, columns] = total.astype(jnp.bfloat16)


def gram_tile(place, mine, gathered):
    replicas, shards, home_count, band_rows, band_cols = gathered.shape
    span = band_cols // band_rows
    shape = (home_count, band_rows, band_cols)
    return pl.pallas_call(
        gram_kernel,
        out_shape=(
            jax.ShapeDtypeStruct(shape, jnp.float32),
            jax.ShapeDtypeStruct(shape, jnp.bfloat16),
        ),
        grid_spec=pltpu.PrefetchScalarGridSpec(
            num_scalar_prefetch=1,
            grid=(1,),
            in_specs=[
                pl.BlockSpec(mine.shape, lambda i, place: (0, 0, 0, 0)),
                pl.BlockSpec(
                    (span, shards, home_count, band_rows, band_cols),
                    lambda i, place: (place[1], 0, 0, 0, 0),
                ),
            ],
            out_specs=[pl.BlockSpec(shape, lambda i, place: (0, 0, 0))] * 2,
        ),
        compiler_params=BIG,
    )(place, mine, gathered)


def stat_kernel(place, owners, gram, came, out):
    home_count, band_rows, band_cols = out.shape
    row_ids = place[0] * band_rows + lax.broadcasted_iota(jnp.int32, (band_rows, band_cols), 0)
    col_ids = place[1] * band_cols + lax.broadcasted_iota(jnp.int32, (band_rows, band_cols), 1)
    damping = jnp.where(row_ids == col_ids, DAMPING, 0.0)
    for block in range(home_count):
        history = came[owners[block]].astype(jnp.float32)
        out[block] = (DECAY * history + gram[block] + damping).astype(jnp.bfloat16)


def stat_tile(place, owners, gram, came):
    return pl.pallas_call(
        stat_kernel,
        out_shape=jax.ShapeDtypeStruct(gram.shape, jnp.bfloat16),
        in_specs=[pl.BlockSpec(memory_space=pltpu.SMEM)] * 2
        + [pl.BlockSpec(memory_space=pltpu.VMEM)] * 2,
        out_specs=pl.BlockSpec(memory_space=pltpu.VMEM),
        compiler_params=BIG,
    )(place, owners, gram, came)


def fresh_kernel(place, rows, gram, out):
    shards, band_rows, band_cols = gram.shape
    row_ids = place[0] * band_rows + lax.broadcasted_iota(jnp.int32, (band_rows, band_cols), 0)
    col_ids = lax.broadcasted_iota(jnp.int32, (band_rows, band_cols), 1)
    for shard in range(shards):
        columns = slice(shard * band_cols, (shard + 1) * band_cols)
        history = rows[:, columns].astype(jnp.float32)
        came = gram[lax.rem(shard + place[1], shards)].astype(jnp.float32)
        damping = jnp.where(row_ids == col_ids + shard * band_cols, DAMPING, 0.0)
        fresh = DECAY * history + came + damping
        out[:, columns] = jnp.where(place[2] > 0, fresh, history).astype(jnp.bfloat16)


def fresh_rows(place, history, gram):
    shards, band_rows, _ = gram.shape
    order_full = history.shape[1]
    return pl.pallas_call(
        fresh_kernel,
        out_shape=jax.ShapeDtypeStruct((band_rows, order_full), jnp.bfloat16),
        grid_spec=pltpu.PrefetchScalarGridSpec(
            num_scalar_prefetch=1,
            grid=(1,),
            in_specs=[
                pl.BlockSpec((band_rows, order_full), lambda i, place: (place[0], 0)),
                pl.BlockSpec(gram.shape, lambda i, place: (0, 0, 0)),
            ],
            out_specs=pl.BlockSpec((band_rows, order_full), lambda i, place: (0, 0)),
        ),
        compiler_params=BIG,
    )(place, history, gram)


def newton_kernel(place, need, stat, cols, out, scaled, factor):
    replicas, shards, _, band_rows, band_cols = stat.shape
    order_full = replicas * band_rows
    block = pl.program_id(0)
    squares = jnp.zeros((8, band_cols), jnp.float32)
    for band in range(replicas):
        for shard in range(shards):
            tile = stat[band, shard, 0].astype(jnp.float32)
            squares = squares + jnp.sum((tile * tile).reshape(-1, 8, band_cols), axis=0)
    frobenius = jnp.sqrt(jnp.sum(squares, keepdims=True)[:1, :1])
    norm_scale = math.sqrt(order_full) / (2.0 * frobenius)
    row_ids = lax.broadcasted_iota(jnp.int32, (band_rows, band_cols), 0)
    col_ids = lax.broadcasted_iota(jnp.int32, (band_rows, band_cols), 1)
    for band in range(replicas):
        for shard in range(shards):
            tile = (stat[band, shard, 0].astype(jnp.float32) * norm_scale).astype(jnp.bfloat16)
            rows, columns = pl.ds(band * band_rows, band_rows), pl.ds(shard * band_cols, band_cols)
            scaled[rows, columns] = tile
            rest = -0.5 * tile.astype(jnp.float32)
            if (band * band_rows) // band_cols == shard:
                diagonal = row_ids + (band * band_rows - shard * band_cols) == col_ids
                rest = rest + jnp.where(diagonal, 1.5, 0.0)
            factor[rows, columns] = rest.astype(jnp.bfloat16)
    first = pl.multiple_of(place[0] * band_rows, band_rows)
    mine = factor[pl.ds(first, band_rows), :]
    product = jnp.dot(mine, scaled[...], preferred_element_type=jnp.float32).astype(jnp.bfloat16)
    product = jnp.dot(product, factor[...], preferred_element_type=jnp.float32)
    wide_rows = lax.broadcasted_iota(jnp.int32, (band_rows, order_full), 0) + first
    wide_cols = lax.broadcasted_iota(jnp.int32, (band_rows, order_full), 1)
    update = jnp.where(wide_rows == wide_cols, 1.5, 0.0) - 0.5 * product
    second = jnp.dot(update.astype(jnp.bfloat16), factor[...], preferred_element_type=jnp.float32)
    root = jnp.where(need[block] >= ITERS, second, mine.astype(jnp.float32)).astype(jnp.bfloat16)
    total = jnp.zeros((band_rows, band_cols), jnp.float32)
    for band in range(replicas):
        total = total + jnp.dot(
            root[:, band * band_rows : (band + 1) * band_rows],
            cols[band, 0, 0],
            preferred_element_type=jnp.float32,
        )
    out[0] = total.astype(jnp.bfloat16)


def newton_tile(place, need, stat, gathered):
    replicas, shards, home_count, band_rows, band_cols = stat.shape
    order_full = replicas * band_rows
    return pl.pallas_call(
        newton_kernel,
        out_shape=jax.ShapeDtypeStruct((home_count, band_rows, band_cols), jnp.bfloat16),
        grid_spec=pltpu.PrefetchScalarGridSpec(
            num_scalar_prefetch=2,
            grid=(home_count,),
            in_specs=[
                pl.BlockSpec(
                    (replicas, shards, 1, band_rows, band_cols),
                    lambda i, place, need: (0, 0, i, 0, 0),
                ),
                pl.BlockSpec(
                    (replicas, 1, 1, band_rows, band_cols),
                    lambda i, place, need: (0, place[1], i, 0, 0),
                ),
            ],
            out_specs=pl.BlockSpec((1, band_rows, band_cols), lambda i, place, need: (i, 0, 0)),
            scratch_shapes=[
                pltpu.VMEM((order_full, order_full), jnp.bfloat16),
                pltpu.VMEM((order_full, order_full), jnp.bfloat16),
            ],
        ),
        compiler_params=BIG,
    )(place, need, stat, gathered)


def exchange(array, axis):
    return lax.all_to_all(array, axis, split_axis=0, concat_axis=0, tiled=True)


def after(array, other):
    return lax.optimization_barrier((array, other))[0]


def body(partial_grads, owner_map, iterations, slot_history):
    owners = lax.axis_size(OWN)
    replicas = lax.axis_size(REP)
    shards = lax.axis_size(BLK)
    levels = lax.axis_size("zl")
    turns = lax.axis_size("y")
    my_rep, my_own, my_blk = lax.axis_index(REP), lax.axis_index(OWN), lax.axis_index(BLK)
    my_level, my_turn = lax.axis_index("zl"), lax.axis_index("y")
    _, home_count, order_full, band_cols = partial_grads.shape
    band_rows = order_full // replicas
    total_blocks = owner_map.shape[0]
    history = slot_history[0, 0]
    place = jnp.stack([my_rep, my_blk]).astype(jnp.int32)

    outgoing = (
        partial_grads[0]
        .reshape(home_count, replicas, band_rows, band_cols)
        .transpose(1, 0, 2, 3)
    )
    partials = exchange(outgoing, REP)
    grad_tile = jnp.sum(partials.astype(jnp.float32), axis=0).astype(jnp.bfloat16)

    position = jnp.arange(total_blocks, dtype=jnp.int32)
    same = owner_map[:, None] == owner_map[None, :]
    slot = jnp.sum(jnp.where(same & (position[None, :] < position[:, None]), 1, 0), axis=1)
    place_ids = jnp.arange(owners * shards, dtype=jnp.int32)
    lands = (owner_map * shards + slot)[None, :] == place_ids[:, None]
    holder = jnp.sum(jnp.where(lands, position[None, :] + 1, 0), axis=1).reshape(owners, shards) - 1
    my_holder = lax.dynamic_index_in_dim(holder, my_own, 0, keepdims=False)
    my_owners = lax.dynamic_slice_in_dim(owner_map, my_own * home_count, home_count)
    my_need = lax.dynamic_slice_in_dim(iterations, my_own * home_count, home_count)
    owner_ids = jnp.arange(owners, dtype=jnp.int32)
    slot_ids = jnp.arange(shards, dtype=jnp.int32)
    sits = (my_holder // home_count)[None, :] == owner_ids[:, None]
    slot_for_home = jnp.sum(jnp.where(sits & (my_holder >= 0)[None, :], slot_ids[None, :], 0), axis=1)

    history_tiles = exchange(cut_rows(place, history, shards, band_rows), BLK)

    grad_band = lax.all_gather(grad_tile, BLK, axis=0, tiled=False)
    grad_full = lax.all_gather(grad_band, REP, axis=0, tiled=False)

    history_sent = take(after(history_tiles, grad_band), slot_for_home)
    history_came = exchange(history_sent, OWN)

    gram, gram_half = gram_tile(place, grad_band, grad_full)
    tile = stat_tile(place, my_owners, gram, history_came)
    stat_band = lax.all_gather(tile, BLK, axis=0, tiled=False)
    stat_full = lax.all_gather(stat_band, REP, axis=0, tiled=False)

    column = lax.all_gather(gram_half, "y", axis=0, tiled=True)
    ring_size = shards * levels
    steps = (0, 1, -1, 2)

    def spot(height):
        height = height % ring_size
        return (height % levels) * shards + height // levels

    wanted = holder.reshape(levels, turns, shards)[:, my_turn]
    wanted_home = jnp.maximum(wanted, 0) // home_count
    in_column = (wanted_home % turns) * home_count + jnp.maximum(wanted, 0) % home_count
    arrivals = []
    for step in steps:
        level = lax.rem(my_level + step + levels, levels)
        sent = take(column, lax.dynamic_index_in_dim(in_column, level, 0, keepdims=False))
        if step:
            ring = [(spot(i), spot(i + step)) for i in range(ring_size)]
            sent = lax.ppermute(sent, RING, ring)
        arrivals.append(sent)
    my_from = jnp.maximum(my_holder, 0) // home_count // turns
    way = lax.rem(my_level - my_from + levels, levels)
    slot_step = jnp.where(way == 0, 0, jnp.where(way == 1, 1, jnp.where(way == 2, 3, 2)))
    slot_gram = take(jnp.concatenate(arrivals, axis=0), slot_step * shards + slot_ids)
    rows_gram = exchange(slot_gram, BLK)
    my_way = lax.dynamic_index_in_dim(way, my_blk, 0, keepdims=False)
    signed = jnp.where(my_way == levels - 1, -1, my_way)
    source = my_level - signed
    carry = jnp.where(source < 0, -1, jnp.where(source >= levels, 1, 0))
    occupied = jnp.where(lax.dynamic_index_in_dim(my_holder, my_blk, 0, keepdims=False) >= 0, 1, 0)
    turn = lax.rem(shards - carry, shards)
    new_rows = fresh_rows(jnp.stack([my_rep, turn, occupied]).astype(jnp.int32), history, rows_gram)

    directions = newton_tile(place, my_need, stat_full, grad_full)
    return (directions, new_rows[None, None])


def solution(mesh):
    fine = Mesh(mesh.devices.reshape(4, 2, 4, 8, 4), ("x", "core", "zl", "y", "zh"))
    return jax.shard_map(
        body,
        mesh=fine,
        in_specs=(P(REP, OWN, None, BLK), P(), P(), P(OWN, BLK, None, None)),
        out_specs=(P(OWN, REP, BLK), P(OWN, BLK, REP, None)),
        check_vma=False,
    )
```

time: 368 us -> 255 us (0.69)
  the two profiles are of different devices: /device:TPU:1 before, /device:TPU:8 now
where the time goes in v2:
time: 255 us; the launch traced here: 254 us
  waiting for transfers between devices  82.1 us (32%)
  blocking collectives  70 us (27%)
  starting transfers between devices  52.9 us (21%)
  Pallas kernels  16.8 us (7%)
  between operations  16 us (6%)
  local copies, waits for them, and re-layouts  14.3 us (6%)
    all_to_all x4, waiting for transfers between devices, exchange(): return lax.all_to_all(array, axis, split_axis=0, concat_axis=0, tiled=True)  49.6 us
    all_to_all x4, starting transfers between devices, exchange(): return lax.all_to_all(array, axis, split_axis=0, concat_axis=0, tiled=True)  38.9 us
    all_gather x1, blocking collectives, body(): grad_band = lax.all_gather(grad_tile, BLK, axis=0, tiled=False)  37.7 us
    all_gather x1, blocking collectives, body(): stat_band = lax.all_gather(tile, BLK, axis=0, tiled=False)  32.3 us
    all_gather x1, waiting for transfers between devices, body(): grad_full = lax.all_gather(grad_band, REP, axis=0, tiled=False)  25.4 us
    ppermute x3, starting transfers between devices, body(): sent = lax.ppermute(sent, RING, ring)  13.9 us
    unnamed x20, local copies, waits for them, and re-layouts  10.4 us
    ppermute x3, waiting for transfers between devices, body(): sent = lax.ppermute(sent, RING, ring)  6.92 us
  transfers between devices with their start and end apart: 10, of which 6 were waited for; matrix products, arithmetic and copies ran while one was open for 1% of the time, Pallas kernels for 4%

profile of v2, /device:TPU:8, one launch (start us, length us, event | category | flops | bytes accessed | tf_op | source)
XLA Modules:
  0.0 254.3 jit_solution(5975737111981123983)
XLA Ops:
  7.2 2.4 copy.7
  9.6 4.4 %all-to-all-start = ((bf16[8,2,128,256]{3,2,1,0:T(8,128)(2,1)}), bf16[8,2,128,256]{3,2,1,0:T(8,128)(2,1)}, u32[]{:S(2)}, u32[]{:S(2)}) async-start(bf16[8,2,128,256]{3,2,1,0:T(8,128)(2,1)} %copy.7), calls=%async_computation | async-start | bytes 2097152 | tf_op jit(solution)/shard_map/all_to_all | solution.py:235
  14.0 0.1 pad_add_fusion.place
  14.1 1.3 shard_map.60
  15.4 0.2 select_reduce_fusion.1
  15.6 14.6 %all-to-all-done = bf16[8,2,128,256]{3,2,1,0:T(8,128)(2,1)} async-done(((bf16[8,2,128,256]{3,2,1,0:T(8,128)(2,1)}), bf16[8,2,128,256]{3,2,1,0:T(8,128)(2,1)}, u32[]{:S(2)}, u32[]{:S(2)}) %all-to-all-start) | async-done | bytes 1048608 | tf_op jit(solution)/shard_map/all_to_all | solution.py:235
  30.1 18.7 %all-to-all-start.1 = ((bf16[4,128,256]{2,1,0:T(8,128)(2,1)}), bf16[4,128,256]{2,1,0:T(8,128)(2,1)S(1)}, u32[]{:S(2)}, u32[]{:S(2)}) async-start(bf16[4,128,256]{2,1,0:T(8,128)(2,1)} %shard_map.60), calls=%async_computation.1 | async-start | bytes 524288 | tf_op jit(solution)/shard_map/all_to_all | solution.py:235
  48.8 1.4 reduce_sum.39
  50.2 37.7 %all-gather = bf16[8,128,256]{2,1,0:T(8,128)(2,1)} all-gather(bf16[2,128,256]{2,1,0:T(8,128)(2,1)S(1)} %reduce_sum.39), channel_id=2, replica_groups=mesh['x'=4,'core'=2,'zl'=4,'y'=8,'zh'=4] {'zh'}, dimensions={0}, use_global_device_ids=true | all-gather | bytes 655360 | tf_op jit(solution)/shard_map/all_gather | solution.py:280
  87.9 0.1 select_reduce_fusion
  88.0 0.1 sub.35
  88.2 0.1 select_reduce_fusion.2.index
  88.3 0.7 shard_map.61
  89.0 1.4 copy-done.5
  90.4 9.2 %all-to-all-start.2 = ((bf16[32,128,256]{2,1,0:T(8,128)(2,1)}), bf16[32,128,256]{2,1,0:T(8,128)(2,1)}, u32[]{:S(2)}, u32[]{:S(2)}) async-start(bf16[32,128,256]{2,1,0:T(8,128)(2,1)} %copy-done.5), calls=%async_computation.2 | async-start | bytes 4194304 | tf_op jit(solution)/shard_map/all_to_all | solution.py:235
  99.6 0.0 all-gather.8.cloned.1.call-start
  99.6 25.4 %all-gather.10.cloned.1.call-done = bf16[32,2,128,256]{3,2,1,0:T(8,128)(2,1)} async-done(((bf16[4,2,128,256]{3,2,1,0:T(8,128)(2,1)}), bf16[32,2,128,256]{3,2,1,0:T(8,128)(2,1)}) %all-gather.10.cloned.1.call-update) | async-done | bytes 4194320 | tf_op jit(solution)/shard_map/all_gather | solution.py:281
  125.1 2.2 copy-done.2
  127.2 1.6 shard_map.59
  128.9 0.0 all-gather.12.cloned.1.call-start
  129.0 0.1 dynamic_slice.34.owners
  129.0 23.8 %all-to-all-done.2.came = bf16[32,128,256]{2,1,0:T(8,128)(2,1)} async-done(((bf16[32,128,256]{2,1,0:T(8,128)(2,1)}), bf16[32,128,256]{2,1,0:T(8,128)(2,1)}, u32[]{:S(2)}, u32[]{:S(2)}) %all-to-all-start.2) | async-done | bytes 2097184 | tf_op jit(solution)/shard_map/all_to_all | solution.py:235
  152.8 1.7 shard_map.62
  154.5 32.3 %all-gather.2 = bf16[8,128,256]{2,1,0:T(8,128)(2,1)} all-gather(bf16[2,128,256]{2,1,0:T(8,128)(2,1)S(1)} %shard_map.62), channel_id=4, replica_groups=mesh['x'=4,'core'=2,'zl'=4,'y'=8,'zh'=4] {'zh'}, dimensions={0}, use_global_device_ids=true | all-gather | bytes 655360 | tf_op jit(solution)/shard_map/all_gather | solution.py:288
  186.9 0.1 sub.43
  187.1 1.2 copy-done
  188.4 0.6 shard_map.67
  188.9 1.9 collective-permute-start.2
  190.9 1.2 copy-done.1
  192.1 0.6 shard_map.66
  192.7 10.1 %collective-permute-start.1 = (bf16[4,128,256]{2,1,0:T(8,128)(2,1)S(1)}, bf16[4,128,256]{2,1,0:T(8,128)(2,1)S(1)}, u32[]{:S(2)}, u32[]{:S(2)}) collective-permute-start(bf16[4,128,256]{2,1,0:T(8,128)(2,1)S(1)} %shard_map.66), channel_id=1, source_target_pairs={{0,99},{32,0},{64,32},{96,64},{1,96},{33,1},{65,33},{97,65},{2,97}... | collective-permute-start | bytes 786440 | tf_op jit(solution)/shard_map/ppermute | solution.py:308
  202.7 0.6 shard_map.65
  203.3 1.9 collective-permute-start
  205.3 0.6 shard_map.64
  205.9 0.7 collective-permute-done.1
  206.6 6.2 %collective-permute-done = bf16[4,128,256]{2,1,0:T(8,128)(2,1)S(1)} collective-permute-done((bf16[4,128,256]{2,1,0:T(8,128)(2,1)S(1)}, bf16[4,128,256]{2,1,0:T(8,128)(2,1)S(1)}, u32[]{:S(2)}, u32[]{:S(2)}) %collective-permute-start) | collective-permute-done | bytes 262176 | tf_op jit(solution)/shard_map/ppermute | solution.py:308
  212.8 0.1 pad_maximum_fusion.tiles
  212.9 1.3 shard_map.68
  214.2 6.6 %all-to-all-start.3 = ((bf16[4,128,256]{2,1,0:T(8,128)(2,1)}), bf16[4,128,256]{2,1,0:T(8,128)(2,1)S(1)}, u32[]{:S(2)}, u32[]{:S(2)}) async-start(bf16[4,128,256]{2,1,0:T(8,128)(2,1)} %shard_map.68), calls=%async_computation.3 | async-start | bytes 524288 | tf_op jit(solution)/shard_map/all_to_all | solution.py:235
  220.7 0.6 dynamic_slice.36
  222.7 0.1 dynamic_slice.33.need
  222.7 0.6 dynamic_slice.37
  224.0 0.1 pad_add_fusion.1.place
  224.1 11.3 %all-to-all-done.3.gram = bf16[4,128,256]{2,1,0:T(8,128)(2,1)S(1)} async-done(((bf16[4,128,256]{2,1,0:T(8,128)(2,1)}), bf16[4,128,256]{2,1,0:T(8,128)(2,1)S(1)}, u32[]{:S(2)}, u32[]{:S(2)}) %all-to-all-start.3) | async-done | bytes 262176 | tf_op jit(solution)/shard_map/all_to_all | solution.py:235
  235.3 1.4 shard_map.69
  236.7 2.2 copy-done.3
  238.9 2.2 copy-done.7
  241.1 6.7 %shard_map.63 = bf16[2,128,256]{2,1,0:T(8,128)(2,1)} custom-call(s32[2]{0:T(128)S(1)} %pad_add_fusion.place, s32[2]{0:T(128)S(1)} %dynamic_slice.33.need, bf16[8,4,2,128,256]{4,3,2,1,0:T(8,128)(2,1)S(1)} %bitcast.50, bf16[8,4,2,128,256]{4,3,2,1,0:T(8,128)(2,1)S(1)} %bitcast.45), custom_call_target="tpu_custom_call" | custom-call | tf_op jit(solution)/shard_map/pallas_call | solution.py:208
  (31 shorter events, 0.2 us)
Async XLA Ops:
  7.2 7.0 %copy-start.4 = (bf16[1,1,1024,1024]{3,2,1,0:T(8,128)(2,1)S(1)}, bf16[1,1,1024,1024]{3,2,1,0:T(8,128)(2,1)}, u32[]{:S(2)}) copy-start(bf16[1,1,1024,1024]{3,2,1,0:T(8,128)(2,1)} %param.7) | copy-start | bytes 6291460
  9.6 5.8 %copy-start.8 = (s32[64]{0:T(128)S(1)}, s32[64]{0:T(128)}, u32[]{:S(2)}) copy-start(s32[64]{0:T(128)} %param.5) | copy-start | bytes 772
  9.6 20.5 %all-to-all-start = ((bf16[8,2,128,256]{3,2,1,0:T(8,128)(2,1)}), bf16[8,2,128,256]{3,2,1,0:T(8,128)(2,1)}, u32[]{:S(2)}, u32[]{:S(2)}) async-start(bf16[8,2,128,256]{3,2,1,0:T(8,128)(2,1)} %copy.7), calls=%async_computation | async-start | bytes 2097152 | tf_op jit(solution)/shard_map/all_to_all | solution.py:235
  30.1 58.2 %all-to-all-start.1 = ((bf16[4,128,256]{2,1,0:T(8,128)(2,1)}), bf16[4,128,256]{2,1,0:T(8,128)(2,1)S(1)}, u32[]{:S(2)}, u32[]{:S(2)}) async-start(bf16[4,128,256]{2,1,0:T(8,128)(2,1)} %shard_map.60), calls=%async_computation.1 | async-start | bytes 524288 | tf_op jit(solution)/shard_map/all_to_all | solution.py:235
  48.8 76.2 %all-gather.10.cloned.1.call-start = ((), (), s32[]{:S(2)}) async-start(), calls=%async_computation.5 | async-start | bytes 4718592 | tf_op jit(solution)/shard_map/all_gather | solution.py:281
  89.0 1.4 copy-start.5
  90.4 34.7 %copy-start.6 = (bf16[8,128,256]{2,1,0:T(8,128)(2,1)S(1)}, bf16[8,128,256]{2,1,0:T(8,128)(2,1)}, u32[]{:S(2)}) copy-start(bf16[8,128,256]{2,1,0:T(8,128)(2,1)} %all-gather) | copy-start | bytes 1572868
  90.4 62.5 %all-to-all-start.2 = ((bf16[32,128,256]{2,1,0:T(8,128)(2,1)}), bf16[32,128,256]{2,1,0:T(8,128)(2,1)}, u32[]{:S(2)}, u32[]{:S(2)}) async-start(bf16[32,128,256]{2,1,0:T(8,128)(2,1)} %copy-done.5), calls=%async_computation.2 | async-start | bytes 4194304 | tf_op jit(solution)/shard_map/all_to_all | solution.py:235
  99.6 87.5 %all-gather.8.cloned.1.call-start = ((), (), s32[]{:S(2)}) async-start(), calls=%async_computation.4 | async-start | bytes 1179648 | tf_op jit(solution)/shard_map/all_gather | solution.py:291
  125.1 2.2 copy-start.2
  128.9 107.8 %all-gather.12.cloned.1.call-start = ((), (), s32[]{:S(2)}) async-start(), calls=%async_computation.6 | async-start | bytes 4718592 | tf_op jit(solution)/shard_map/all_gather | solution.py:289
  187.1 1.2 copy-start
  188.9 16.9 %collective-permute-start.2 = (bf16[4,128,256]{2,1,0:T(8,128)(2,1)S(1)}, bf16[4,128,256]{2,1,0:T(8,128)(2,1)S(1)}, u32[]{:S(2)}, u32[]{:S(2)}) collective-permute-start(bf16[4,128,256]{2,1,0:T(8,128)(2,1)S(1)} %shard_map.67), channel_id=1, source_target_pairs={{0,64},{32,96},{64,1},{96,33},{1,65},{33,97},{65,2},{97,34},{2,66}... | collective-permute-start | bytes 786440 | tf_op jit(solution)/shard_map/ppermute | solution.py:308
  190.9 1.2 copy-start.1
  192.7 13.9 %collective-permute-start.1 = (bf16[4,128,256]{2,1,0:T(8,128)(2,1)S(1)}, bf16[4,128,256]{2,1,0:T(8,128)(2,1)S(1)}, u32[]{:S(2)}, u32[]{:S(2)}) collective-permute-start(bf16[4,128,256]{2,1,0:T(8,128)(2,1)S(1)} %shard_map.66), channel_id=1, source_target_pairs={{0,99},{32,0},{64,32},{96,64},{1,96},{33,1},{65,33},{97,65},{2,97}... | collective-permute-start | bytes 786440 | tf_op jit(solution)/shard_map/ppermute | solution.py:308
  203.3 9.5 %collective-permute-start = (bf16[4,128,256]{2,1,0:T(8,128)(2,1)S(1)}, bf16[4,128,256]{2,1,0:T(8,128)(2,1)S(1)}, u32[]{:S(2)}, u32[]{:S(2)}) collective-permute-start(bf16[4,128,256]{2,1,0:T(8,128)(2,1)S(1)} %shard_map.65), channel_id=1, source_target_pairs={{0,32},{32,64},{64,96},{96,1},{1,33},{33,65},{65,97},{97,2},{2,34}... | collective-permute-start | bytes 786440 | tf_op jit(solution)/shard_map/ppermute | solution.py:308
  205.8 16.8 %copy-start.9 = (s32[64]{0:T(128)S(1)}, s32[64]{0:T(128)}, u32[]{:S(2)}) copy-start(s32[64]{0:T(128)} %param.6) | copy-start | bytes 772
  214.2 21.2 %all-to-all-start.3 = ((bf16[4,128,256]{2,1,0:T(8,128)(2,1)}), bf16[4,128,256]{2,1,0:T(8,128)(2,1)S(1)}, u32[]{:S(2)}, u32[]{:S(2)}) async-start(bf16[4,128,256]{2,1,0:T(8,128)(2,1)} %shard_map.68), calls=%async_computation.3 | async-start | bytes 524288 | tf_op jit(solution)/shard_map/all_to_all | solution.py:235
  236.7 2.2 copy-start.3
  238.9 2.2 copy-start.7
Sparse Core Ops, SparseCore 0:
  88.0 36.9 all-gather.9
  129.0 47.3 all-gather.7
  187.0 42.2 all-gather.11

commit v3 on v0

v3 whole, which is shorter than its diff:
```python
import math

import jax
import jax.numpy as jnp
from jax import lax
from jax.experimental import pallas as pl
from jax.experimental.pallas import tpu as pltpu
from jax.sharding import PartitionSpec as P

ITERS = 2


DECAY = 0.5
DAMPING = 0.05

BIG = pltpu.CompilerParams(vmem_limit_bytes=40 * 1024 * 1024)
SCALARS = pl.BlockSpec(memory_space=pltpu.SMEM)
WHOLE = pl.BlockSpec(memory_space=pltpu.VMEM)

REP_AT, BLK_AT, OWNER_AT, NEED_AT, HOLDER_AT = 0, 1, 2, 4, 6


def ds(start, size, unit):
    return pl.ds(pl.multiple_of(start, unit), size)


def pieces(tile, shards):
    depth = (4 * tile + tile // 2) // shards
    ends = sorted(set(range(0, shards * depth + 1, depth)) | set(range(0, 4 * tile + 1, tile)))
    return [
        (low // depth, low % depth, low // tile, low % tile, high - low)
        for low, high in zip(ends[:-1], ends[1:])
    ]


def call(kernel, ins, outs, in_specs=None, scratch=()):
    many = isinstance(outs, (list, tuple))
    return pl.pallas_call(
        kernel,
        out_shape=outs,
        in_specs=in_specs or [SCALARS] + [WHOLE] * (len(ins) - 1),
        out_specs=[WHOLE] * len(outs) if many else WHOLE,
        scratch_shapes=list(scratch),
        compiler_params=BIG,
    )(*ins)


def like(shape, dtype=jnp.bfloat16):
    return jax.ShapeDtypeStruct(shape, dtype)


def history_kernel(place, column, half, *refs):
    outs, held = refs[:-1], refs[-1]
    shards, depth, tile = held.shape
    for part, row, step, inner, size in pieces(tile, shards):
        if step < 4:
            start = lax.rem(place[0] + step, 8) * tile + inner
            held[part, row : row + size] = column[ds(start, size, 16), :]
        else:
            held[part, row : row + size] = half[inner : inner + size]
    for step in range(shards):
        outs[step][...] = held[lax.rem(place[1] + step, shards)]


def cut_history(place, history, shards, tile):
    depth = (4 * tile + tile // 2) // shards
    order_full = history.shape[0]
    return pl.pallas_call(
        history_kernel,
        out_shape=[like((depth, tile))] * shards,
        grid_spec=pltpu.PrefetchScalarGridSpec(
            num_scalar_prefetch=1,
            grid=(1,),
            in_specs=[
                pl.BlockSpec((order_full, tile), lambda i, place: (0, place[0])),
                pl.BlockSpec(
                    (tile // 2, tile),
                    lambda i, place: (
                        (lax.rem(place[0], 4) + 4) * 2 + place[0] // 4,
                        lax.rem(place[0], 4),
                    ),
                ),
            ],
            out_specs=[pl.BlockSpec((depth, tile), lambda i, place: (0, 0))] * shards,
            scratch_shapes=[pltpu.VMEM((shards, depth, tile), jnp.bfloat16)],
        ),
        compiler_params=BIG,
    )(place, history, history)


def spread_kernel(table, *refs):
    arrived, out = refs[:-1], refs[-1]
    shards = len(arrived)
    out[...] = jnp.zeros_like(out)
    for step in range(shards):
        holder = table[HOLDER_AT + lax.rem(table[BLK_AT] + shards - step, shards)]

        @pl.when(holder >= 0)
        def _(step=step, holder=holder):
            out[lax.div(holder, 2)] = arrived[step][...]


def gram_kernel(place, cols, *refs):
    outs, held = refs[:-1], refs[-1]
    shards, home_count, depth, tile = held.shape
    order_full = cols.shape[0] * tile
    rep = place[0]
    quarter = lax.rem(rep, 4)
    for block in range(home_count):
        mine = cols[rep, block]
        tiles = []
        for step in range(5):
            if step < 4:
                left, right = cols[lax.rem(rep + step, 8), block], mine
            else:
                start = lax.div(rep, 4) * (tile // 2)
                left = cols[quarter + 4, block, ds(start, tile // 2, 16), :]
                right = cols[quarter, block]
            product = lax.dot_general(
                left, right, (((1,), (1,)), ((), ())), preferred_element_type=jnp.float32
            )
            tiles.append((product * ((1.0 - DECAY) / order_full)).astype(jnp.bfloat16))
        for part, row, step, inner, size in pieces(tile, shards):
            held[part, block, row : row + size] = tiles[step][inner : inner + size]
    for step in range(shards):
        outs[step][...] = held[lax.rem(place[1] + step, shards)]


def add_kernel(table, *refs):
    arrived, total_out, sent = refs[:-2], refs[-2], refs[-1]
    total = sum(ref[...].astype(jnp.float32) for ref in arrived)
    total_out[...] = total
    sent[...] = jnp.zeros_like(sent)
    for block in range(total.shape[0]):
        sent[table[OWNER_AT + block]] = total[block].astype(jnp.bfloat16)


def stat_kernel(table, gram, came, out):
    home_count, depth, tile = out.shape
    row_ids = lax.broadcasted_iota(jnp.int32, (depth, tile), 0)
    col_ids = lax.broadcasted_iota(jnp.int32, (depth, tile), 1)
    damping = jnp.where((row_ids + table[BLK_AT] * depth) == col_ids, DAMPING, 0.0)
    for block in range(home_count):
        history = came[table[OWNER_AT + block]].astype(jnp.float32)
        out[block] = (DECAY * history + gram[block] + damping).astype(jnp.bfloat16)


def order_kernel(table, *refs):
    arrived, out = refs[:-1], refs[-1]
    shards = len(arrived)
    for step in range(shards):
        out[lax.rem(table[BLK_AT] + shards - step, shards)] = arrived[step][...]


def choose_kernel(table, came, *outs):
    shards = len(outs)
    for step in range(shards):
        holder = table[HOLDER_AT + lax.rem(table[BLK_AT] + step, shards)]
        outs[step][...] = came[lax.div(jnp.maximum(holder, 0), 2)]


def turn_kernel(table, *refs):
    arrived, band, sent = refs[:-2], refs[-2], refs[-1]
    shards = len(arrived)
    depth, tile = arrived[0].shape
    for step in range(shards):
        part = lax.rem(table[BLK_AT] + shards - step, shards)
        band[ds(part * depth, depth, 16), :] = arrived[step][...]
    sent[...] = jnp.zeros_like(sent)
    for step in range(1, 4):
        sent[lax.rem(table[REP_AT] + step, 8)] = band[step * tile : (step + 1) * tile]
    sent[lax.rem(table[REP_AT] + 4, 8), : tile // 2] = band[4 * tile :]


def finish_kernel(place, rows, band, came, out):
    tile = rows.shape[0]
    rep = place[0]
    first = rep < 4

    def put(column, gram, damping=None):
        columns = ds(column * tile, tile, tile)
        history = rows[:, columns].astype(jnp.float32)
        fresh = DECAY * history + gram
        if damping is not None:
            fresh = fresh + damping
        out[:, columns] = jnp.where(place[1] > 0, fresh, history).astype(jnp.bfloat16)

    row_ids = lax.broadcasted_iota(jnp.int32, (tile, tile), 0)
    col_ids = lax.broadcasted_iota(jnp.int32, (tile, tile), 1)
    put(rep, band[:tile].astype(jnp.float32), jnp.where(row_ids == col_ids, DAMPING, 0.0))
    for step in range(1, 4):
        mine = band[step * tile : (step + 1) * tile].astype(jnp.float32)
        put(lax.rem(rep + step, 8), mine.T)
        other = lax.rem(rep + 8 - step, 8)
        put(other, came[other].astype(jnp.float32))
    other = lax.rem(rep + 4, 8)
    mine = band[4 * tile :].astype(jnp.float32)
    theirs = came[other, : tile // 2].astype(jnp.float32)
    upper, lower = jnp.where(first, mine, theirs), jnp.where(first, theirs, mine)
    whole = jnp.concatenate([upper, lower], axis=0)
    put(other, jnp.where(first, whole.T, whole))


def finish(place, history, band, came):
    tile, order_full = band.shape[1], history.shape[1]
    return pl.pallas_call(
        finish_kernel,
        out_shape=like((tile, order_full)),
        grid_spec=pltpu.PrefetchScalarGridSpec(
            num_scalar_prefetch=1,
            grid=(1,),
            in_specs=[
                pl.BlockSpec((tile, order_full), lambda i, place: (place[0], 0)),
                pl.BlockSpec(band.shape, lambda i, place: (0, 0)),
                pl.BlockSpec(came.shape, lambda i, place: (0, 0, 0)),
            ],
            out_specs=pl.BlockSpec((tile, order_full), lambda i, place: (0, 0)),
        ),
        compiler_params=BIG,
    )(place, history, band, came)


def newton_kernel(table, stat, cols, out, full):
    bands, shards, _, depth, tile = stat.shape
    order_full = bands * tile
    block = pl.program_id(0)
    squares = jnp.zeros((8, tile), jnp.float32)
    for band in range(bands):
        for shard in range(shards):
            part = stat[band, shard, 0].astype(jnp.float32)
            squares = squares + 2.0 * jnp.sum((part * part).reshape(-1, 8, tile), axis=0)
        part = stat[band, 0, 0, :tile].astype(jnp.float32)
        squares = squares - jnp.sum((part * part).reshape(-1, 8, tile), axis=0)
    frobenius = jnp.sqrt(jnp.sum(squares, keepdims=True)[:1, :1])
    norm_scale = math.sqrt(order_full) / (2.0 * frobenius)

    def at(index):
        return slice(index * tile, (index + 1) * tile)

    for band in range(bands):
        for part, row, step, inner, size in pieces(tile, shards):
            if step < 4:
                start, columns = (band + step) % bands * tile + inner, at(band)
            else:
                start = (band % 4 + 4) * tile + band // 4 * (tile // 2) + inner
                columns = at(band % 4)
            piece = stat[band, part, 0, row : row + size].astype(jnp.float32) * norm_scale
            full[start : start + size, columns] = piece.astype(jnp.bfloat16)
    for band in range(bands):
        for step in range(1, 5 if band < 4 else 4):
            other = (band + step) % bands
            full[at(band), at(other)] = full[at(other), at(band)].T

    row_ids = lax.broadcasted_iota(jnp.int32, (tile, tile), 0)
    col_ids = lax.broadcasted_iota(jnp.int32, (tile, tile), 1)
    diagonals = []
    for band in range(bands):
        corner = full[at(band), at(band)].astype(jnp.float32)
        values = jnp.sum(jnp.where(row_ids == col_ids, corner, 0.0), axis=0, keepdims=True)
        rounded = (1.5 - 0.5 * values).astype(jnp.bfloat16).astype(jnp.float32)
        diagonals.append(rounded + 0.5 * values)
    diagonal = jnp.concatenate(diagonals, axis=1)

    def times_scaled(left):
        return jnp.dot(left, full[...], preferred_element_type=jnp.float32)

    def times_factor(left):
        return left.astype(jnp.float32) * diagonal - 0.5 * times_scaled(left)

    first = table[REP_AT] * tile
    wide_rows = lax.broadcasted_iota(jnp.int32, (tile, order_full), 0) + first
    wide_cols = lax.broadcasted_iota(jnp.int32, (tile, order_full), 1)
    identity = jnp.where(wide_rows == wide_cols, 1.5, 0.0)
    mine = full[ds(first, tile, tile), :].astype(jnp.float32)
    mine = (identity - 0.5 * mine).astype(jnp.bfloat16)
    product = times_factor(times_scaled(mine).astype(jnp.bfloat16))
    update = (identity - 0.5 * product).astype(jnp.bfloat16)
    second = times_factor(update).astype(jnp.bfloat16)
    root = jnp.where(table[NEED_AT + block] >= ITERS, second, mine)
    total = jnp.zeros(out.shape[1:], jnp.float32)
    for band in range(bands):
        total = total + jnp.dot(root[:, at(band)], cols[band, 0], preferred_element_type=jnp.float32)
    out[0] = total.astype(jnp.bfloat16)


def newton(table, stat, cols):
    bands, shards, home_count, depth, tile = stat.shape
    width = cols.shape[3]
    return pl.pallas_call(
        newton_kernel,
        out_shape=like((home_count, tile, width)),
        grid_spec=pltpu.PrefetchScalarGridSpec(
            num_scalar_prefetch=1,
            grid=(home_count,),
            in_specs=[
                pl.BlockSpec((bands, shards, 1, depth, tile), lambda i, table: (0, 0, i, 0, 0)),
                pl.BlockSpec((bands, 1, tile, width), lambda i, table: (0, i, 0, 0)),
            ],
            out_specs=pl.BlockSpec((1, tile, width), lambda i, table: (i, 0, 0)),
            scratch_shapes=[pltpu.VMEM((bands * tile, bands * tile), jnp.bfloat16)],
        ),
        compiler_params=BIG,
    )(table, stat, cols)


def exchange(array, axis):
    return lax.all_to_all(array, axis, split_axis=0, concat_axis=0, tiled=True)


def swap(parts, count):
    return [parts[0]] + [
        lax.ppermute(parts[step], "blk", [(i, (i + step) % count) for i in range(count)])
        for step in range(1, count)
    ]


def after(array, other):
    return lax.optimization_barrier((array, other))[0]


def body(partial_grads, owner_map, iterations, slot_history):
    owners = lax.axis_size("own")
    replicas = lax.axis_size("rep")
    shards = lax.axis_size("blk")
    my_rep, my_own, my_blk = lax.axis_index("rep"), lax.axis_index("own"), lax.axis_index("blk")
    _, home_count, order_full, band_cols = partial_grads.shape
    tile = order_full // replicas
    depth = (4 * tile + tile // 2) // shards
    total_blocks = owner_map.shape[0]
    history = slot_history[0, 0]
    place = jnp.stack([my_rep, my_blk]).astype(jnp.int32)

    position = jnp.arange(total_blocks, dtype=jnp.int32)
    same = owner_map[:, None] == owner_map[None, :]
    slot = jnp.sum(jnp.where(same & (position[None, :] < position[:, None]), 1, 0), axis=1)
    slot_ids = jnp.arange(shards, dtype=jnp.int32)
    held = (owner_map[None, :] == my_own) & (slot[None, :] == slot_ids[:, None])
    holder = jnp.sum(jnp.where(held, position[None, :] + 1, 0), axis=1) - 1
    my_owners = lax.dynamic_slice_in_dim(owner_map, my_own * home_count, home_count)
    my_need = lax.dynamic_slice_in_dim(iterations, my_own * home_count, home_count)
    table = jnp.concatenate([place, my_owners, my_need, holder]).astype(jnp.int32)

    outgoing = (
        partial_grads[0].reshape(home_count, replicas, tile, band_cols).transpose(1, 0, 2, 3)
    )
    history_parts = cut_history(place, history, shards, tile)
    history_arrived = swap(history_parts, shards)
    partials = exchange(outgoing, "rep")
    grad_tile = jnp.sum(partials.astype(jnp.float32), axis=0).astype(jnp.bfloat16)
    grad_cols = lax.all_gather(grad_tile, "rep", axis=0, tiled=False)

    history_sent = call(spread_kernel, [table, *history_arrived], like((owners, depth, tile)))
    history_came = exchange(after(history_sent, grad_tile), "own")

    gram_parts = pl.pallas_call(
        gram_kernel,
        out_shape=[like((home_count, depth, tile))] * shards,
        in_specs=[SCALARS, WHOLE],
        out_specs=[WHOLE] * shards,
        scratch_shapes=[pltpu.VMEM((shards, home_count, depth, tile), jnp.bfloat16)],
        compiler_params=BIG,
    )(place, grad_cols)
    gram_arrived = swap(gram_parts, shards)
    gram, gram_sent = call(
        add_kernel,
        [table, *gram_arrived],
        [like((home_count, depth, tile), jnp.float32), like((owners, depth, tile))],
    )
    stat = call(stat_kernel, [table, gram, history_came], like((home_count, depth, tile)))
    stat_band = call(
        order_kernel, [table, *swap([stat] * shards, shards)], like((shards, home_count, depth, tile))
    )
    stat_full = lax.all_gather(stat_band, "rep", axis=0, tiled=False)

    gram_came = exchange(after(gram_sent, stat), "own")
    slot_parts = call(choose_kernel, [table, gram_came], [like((depth, tile))] * shards)
    band, turned = call(
        turn_kernel,
        [table, *swap(slot_parts, shards)],
        [like((shards * depth, tile)), like((replicas, tile, tile))],
    )
    turned = exchange(turned, "rep")
    occupied = jnp.where(lax.dynamic_index_in_dim(holder, my_blk, 0, keepdims=False) >= 0, 1, 0)
    new_rows = finish(jnp.stack([my_rep, occupied]).astype(jnp.int32), history, band, turned)

    directions = newton(table, stat_full, grad_cols)
    return (directions, new_rows[None, None])


def solution(mesh):
    return jax.shard_map(
        body,
        mesh=mesh,
        in_specs=(P("rep", "own", None, "blk"), P(), P(), P("own", "blk", None, None)),
        out_specs=(P("own", "rep", "blk"), P("own", "blk", "rep", None)),
        check_vma=False,
    )
```

time: 384 us -> 236 us (0.61)
  waiting for transfers between devices: 246 us -> 76.8 us
  starting transfers between devices: 56.2 us -> 118 us
  matrix products: 21.7 us -> 0 us
  blocking collectives: 19.6 us -> 0 us
  Pallas kernels: 0 us -> 14.7 us
  other arithmetic: 9.74 us -> 1.27 us
  local copies, waits for them, and re-layouts: 13 us -> 8.94 us
    all_to_all x3 -> x4, waiting for transfers between devices: 192 us -> 7.88 us  [exchange(): return lax.all_to_all(array, axis, split_axis=0, concat_axis=0, tiled=True)]
    ppermute x0 -> x12, starting transfers between devices: none -> 75.3 us  [swap(): lax.ppermute(parts[step], 'blk', [(i, (i + step) % count) for i in range(...]
    reduce_scatter x1 -> x0, waiting for transfers between devices: 53.7 us -> none  [body(): lax.psum_scatter(partial_grads[0].astype(jnp.float32).astype(jnp.bfloat16...]
    all_gather x0 -> x2, waiting for transfers between devices: none -> 38.4 us  [the longest x1 33.6 us: body(): grad_cols = lax.all_gather(grad_tile, 'rep', axis=0, tiled=False)]
    ppermute x0 -> x12, waiting for transfers between devices: none -> 29.8 us  [swap(): lax.ppermute(parts[step], 'blk', [(i, (i + step) % count) for i in range(...]
    dot_general x7 -> x0, matrix products: 21.7 us -> none  [the longest x1 8.24 us: statistic_of(): jnp.einsum('ik,jk->ij', grad_full, grad_full, preferred_element_type=jnp....]
    all_to_all x1 -> x0, blocking collectives: 19.6 us -> none  [body(): lax.all_to_all(raw_half[None], 'blk', split_axis=2, concat_axis=0, tiled=...]
    pallas_call x0 -> x10, Pallas kernels: none -> 14.7 us  [the longest x1 6.18 us: newton(): pl.pallas_call(newton_kernel, out_shape=like((home_count, tile, width)),...]
  transfers between devices with their start and end apart: 4 -> 18, of which waited for: 4 -> 9; matrix products, arithmetic and copies ran while one was open for 1% -> 1% of each run, Pallas kernels for 0% -> 5%
where the time goes in v3:
time: 236 us; the launch traced here: 234 us
  starting transfers between devices  118 us (50%)
  waiting for transfers between devices  76.8 us (33%)
  between operations  14.9 us (6%)
  Pallas kernels  14.7 us (6%)
  local copies, waits for them, and re-layouts  8.94 us (4%)
    ppermute x12, starting transfers between devices, swap(): lax.ppermute(parts[step], 'blk', [(i, (i + step) % count) for i in range(...  75.3 us
    all_to_all x4, starting transfers between devices, exchange(): return lax.all_to_all(array, axis, split_axis=0, concat_axis=0, tiled=True)  42.2 us
    all_gather x1, waiting for transfers between devices, body(): grad_cols = lax.all_gather(grad_tile, 'rep', axis=0, tiled=False)  33.6 us
    ppermute x12, waiting for transfers between devices, swap(): lax.ppermute(parts[step], 'blk', [(i, (i + step) % count) for i in range(...  29.8 us
    all_to_all x4, waiting for transfers between devices, exchange(): return lax.all_to_all(array, axis, split_axis=0, concat_axis=0, tiled=True)  7.88 us
    pallas_call x1, Pallas kernels, newton(): pl.pallas_call(newton_kernel, out_shape=like((home_count, tile, width)),...  6.18 us
    unnamed x16, local copies, waits for them, and re-layouts  5.83 us
    pallas_call x6, Pallas kernels, call(): pl.pallas_call(kernel, out_shape=outs, in_specs=in_specs or [SCALARS] + [...  5.51 us
  transfers between devices with their start and end apart: 18, of which 9 were waited for; matrix products, arithmetic and copies ran while one was open for 1% of the time, Pallas kernels for 5%

profile of v3, /device:TPU:1, one launch (start us, length us, event | category | flops | bytes accessed | tf_op | source)
XLA Modules:
  0.0 234.2 jit_solution(5418008589512807516)
XLA Ops:
  7.2 2.3 copy.7
  9.5 17.7 %all-to-all-start = ((bf16[8,2,128,256]{3,2,1,0:T(8,128)(2,1)}), bf16[8,2,128,256]{3,2,1,0:T(8,128)(2,1)S(1)}, u32[]{:S(2)}, u32[]{:S(2)}) async-start(bf16[8,2,128,256]{3,2,1,0:T(8,128)(2,1)} %copy.7), calls=%async_computation | async-start | bytes 2097152 | tf_op jit(solution)/shard_map/all_to_all | solution.py:307
  27.3 0.6 shard_map.61
  27.9 1.9 collective-permute-start.3
  29.9 11.2 %collective-permute-start.4 = (bf16[144,128]{1,0:T(8,128)(2,1)S(1)}, bf16[144,128]{1,0:T(8,128)(2,1)S(1)}, u32[]{:S(2)}, u32[]{:S(2)}) collective-permute-start(bf16[144,128]{1,0:T(8,128)(2,1)S(1)} %get-tuple-element.27), channel_id=1, source_target_pairs={{0,2},{1,3},{2,0},{3,1},{4,6},{5,7},{6,4},{7,5},{8,10},{9,11},{10,... | collective-permute-start | bytes 110600 | tf_op jit(solution)/shard_map/ppermute | solution.py:312
  41.1 3.4 %collective-permute-start.5 = (bf16[144,128]{1,0:T(8,128)(2,1)S(1)}, bf16[144,128]{1,0:T(8,128)(2,1)S(1)}, u32[]{:S(2)}, u32[]{:S(2)}) collective-permute-start(bf16[144,128]{1,0:T(8,128)(2,1)S(1)} %get-tuple-element.28), channel_id=1, source_target_pairs={{0,3},{1,0},{2,1},{3,2},{4,7},{5,4},{6,5},{7,6},{8,11},{9,8},{10,9... | collective-permute-start | bytes 110600 | tf_op jit(solution)/shard_map/ppermute | solution.py:312
  44.4 0.2 select_reduce_fusion
  44.6 0.1 select_reduce_fusion.1
  44.8 0.1 dynamic_slice.10
  44.9 0.1 concatenate.4.table
  45.0 0.4 collective-permute-done.4.refs_2_
  45.4 4.3 %collective-permute-done.5.refs_3_ = bf16[144,128]{1,0:T(8,128)(2,1)S(1)} collective-permute-done((bf16[144,128]{1,0:T(8,128)(2,1)S(1)}, bf16[144,128]{1,0:T(8,128)(2,1)S(1)}, u32[]{:S(2)}, u32[]{:S(2)}) %collective-permute-start.5) | collective-permute-done | bytes 36896 | tf_op jit(solution)/shard_map/ppermute | solution.py:312
  49.7 1.8 shard_map.62
  51.5 0.8 reduce_sum.32
  52.3 11.0 %all-to-all-start.1 = ((bf16[32,144,128]{2,1,0:T(8,128)(2,1)}), bf16[32,144,128]{2,1,0:T(8,128)(2,1)S(1)}, u32[]{:S(2)}, u32[]{:S(2)}) async-start(bf16[32,144,128]{2,1,0:T(8,128)(2,1)} %shard_map.62), calls=%async_computation.1 | async-start | bytes 2359296 | tf_op jit(solution)/shard_map/all_to_all | solution.py:307
  63.4 0.7 all-gather.5.cloned.1.call-update
  64.1 33.6 %all-gather.5.cloned.1.call-done = bf16[16,128,256]{2,1,0:T(8,128)(2,1)} async-done(((bf16[2,128,256]{2,1,0:T(8,128)(2,1)}), bf16[16,128,256]{2,1,0:T(8,128)(2,1)}) %all-gather.5.cloned.1.call-update) | async-done | bytes 1048592 | tf_op jit(solution)/shard_map/all_gather | solution.py:350
  97.6 1.2 copy-done.1
  98.8 0.9 shard_map.59
  99.7 7.7 %collective-permute-start = (bf16[2,144,128]{2,1,0:T(8,128)(2,1)S(1)}, bf16[2,144,128]{2,1,0:T(8,128)(2,1)S(1)}, u32[]{:S(2)}, u32[]{:S(2)}) collective-permute-start(bf16[2,144,128]{2,1,0:T(8,128)(2,1)S(1)} %get-tuple-element.21), channel_id=1, source_target_pairs={{0,1},{1,2},{2,3},{3,0},{4,5},{5,6},{6,7},{7,4},{8,9},{9,10},{10,1... | collective-permute-start | bytes 221192 | tf_op jit(solution)/shard_map/ppermute | solution.py:312
  107.5 8.5 %collective-permute-start.1 = (bf16[2,144,128]{2,1,0:T(8,128)(2,1)S(1)}, bf16[2,144,128]{2,1,0:T(8,128)(2,1)S(1)}, u32[]{:S(2)}, u32[]{:S(2)}) collective-permute-start(bf16[2,144,128]{2,1,0:T(8,128)(2,1)S(1)} %get-tuple-element.22), channel_id=1, source_target_pairs={{0,2},{1,3},{2,0},{3,1},{4,6},{5,7},{6,4},{7,5},{8,10},{9,11},{10,... | collective-permute-start | bytes 221192 | tf_op jit(solution)/shard_map/ppermute | solution.py:312
  116.0 6.3 %collective-permute-start.2 = (bf16[2,144,128]{2,1,0:T(8,128)(2,1)S(1)}, bf16[2,144,128]{2,1,0:T(8,128)(2,1)S(1)}, u32[]{:S(2)}, u32[]{:S(2)}) collective-permute-start(bf16[2,144,128]{2,1,0:T(8,128)(2,1)S(1)} %get-tuple-element.23), channel_id=1, source_target_pairs={{0,3},{1,0},{2,1},{3,2},{4,7},{5,4},{6,5},{7,6},{8,11},{9,8},{10,9... | collective-permute-start | bytes 221192 | tf_op jit(solution)/shard_map/ppermute | solution.py:312
  122.3 9.6 %collective-permute-done.2.refs_3_ = bf16[2,144,128]{2,1,0:T(8,128)(2,1)S(1)} collective-permute-done((bf16[2,144,128]{2,1,0:T(8,128)(2,1)S(1)}, bf16[2,144,128]{2,1,0:T(8,128)(2,1)S(1)}, u32[]{:S(2)}, u32[]{:S(2)}) %collective-permute-start.2) | collective-permute-done | bytes 73760 | tf_op jit(solution)/shard_map/ppermute | solution.py:312
  131.9 0.7 shard_map.60
  132.6 1.0 copy-done.4
  133.6 0.6 shard_map.63.refs_0_
  134.2 6.9 %all-to-all-start.2 = ((bf16[32,144,128]{2,1,0:T(8,128)(2,1)}), bf16[32,144,128]{2,1,0:T(8,128)(2,1)S(1)}, u32[]{:S(2)}, u32[]{:S(2)}) async-start(bf16[32,144,128]{2,1,0:T(8,128)(2,1)} %copy-done.4), calls=%async_computation.2 | async-start | bytes 2359296 | tf_op jit(solution)/shard_map/all_to_all | solution.py:307
  141.1 4.9 %collective-permute-start.8 = (bf16[2,144,128]{2,1,0:T(8,128)(2,1)S(1)}, bf16[2,144,128]{2,1,0:T(8,128)(2,1)S(1)}, u32[]{:S(2)}, u32[]{:S(2)}) collective-permute-start(bf16[2,144,128]{2,1,0:T(8,128)(2,1)S(1)} %shard_map.63.refs_0_), channel_id=1, source_target_pairs={{0,3},{1,0},{2,1},{3,2},{4,7},{5,4},{6,5},{7,6},{8,11},{9,8},{10,9... | collective-permute-start | bytes 221192 | tf_op jit(solution)/shard_map/ppermute | solution.py:312
  146.0 7.4 %collective-permute-start.7 = (bf16[2,144,128]{2,1,0:T(8,128)(2,1)S(1)}, bf16[2,144,128]{2,1,0:T(8,128)(2,1)S(1)}, u32[]{:S(2)}, u32[]{:S(2)}) collective-permute-start(bf16[2,144,128]{2,1,0:T(8,128)(2,1)S(1)} %shard_map.63.refs_0_), channel_id=1, source_target_pairs={{0,2},{1,3},{2,0},{3,1},{4,6},{5,7},{6,4},{7,5},{8,10},{9,11},{10,... | collective-permute-start | bytes 221192 | tf_op jit(solution)/shard_map/ppermute | solution.py:312
  153.5 6.2 %collective-permute-start.6 = (bf16[2,144,128]{2,1,0:T(8,128)(2,1)S(1)}, bf16[2,144,128]{2,1,0:T(8,128)(2,1)S(1)}, u32[]{:S(2)}, u32[]{:S(2)}) collective-permute-start(bf16[2,144,128]{2,1,0:T(8,128)(2,1)S(1)} %shard_map.63.refs_0_), channel_id=1, source_target_pairs={{0,1},{1,2},{2,3},{3,0},{4,5},{5,6},{6,7},{7,4},{8,9},{9,10},{10,1... | collective-permute-start | bytes 221192 | tf_op jit(solution)/shard_map/ppermute | solution.py:312
  159.7 11.8 %collective-permute-done.7.refs_2_ = bf16[2,144,128]{2,1,0:T(8,128)(2,1)S(1)} collective-permute-done((bf16[2,144,128]{2,1,0:T(8,128)(2,1)S(1)}, bf16[2,144,128]{2,1,0:T(8,128)(2,1)S(1)}, u32[]{:S(2)}, u32[]{:S(2)}) %collective-permute-start.7) | collective-permute-done | bytes 73760 | tf_op jit(solution)/shard_map/ppermute | solution.py:312
  171.5 0.6 shard_map.64
  172.1 0.7 copy-done.5
  172.8 7.9 %all-to-all-done.2.came = bf16[32,144,128]{2,1,0:T(8,128)(2,1)S(1)} async-done(((bf16[32,144,128]{2,1,0:T(8,128)(2,1)}), bf16[32,144,128]{2,1,0:T(8,128)(2,1)S(1)}, u32[]{:S(2)}, u32[]{:S(2)}) %all-to-all-start.2) | async-done | bytes 1179680 | tf_op jit(solution)/shard_map/all_to_all | solution.py:307
  180.7 0.6 shard_map.66
  181.3 5.3 %collective-permute-start.9 = (bf16[144,128]{1,0:T(8,128)(2,1)S(1)}, bf16[144,128]{1,0:T(8,128)(2,1)S(1)}, u32[]{:S(2)}, u32[]{:S(2)}) collective-permute-start(bf16[144,128]{1,0:T(8,128)(2,1)S(1)} %get-tuple-element.33), channel_id=1, source_target_pairs={{0,1},{1,2},{2,3},{3,0},{4,5},{5,6},{6,7},{7,4},{8,9},{9,10},{10,1... | collective-permute-start | bytes 110600 | tf_op jit(solution)/shard_map/ppermute | solution.py:312
  186.6 6.2 %collective-permute-start.10 = (bf16[144,128]{1,0:T(8,128)(2,1)S(1)}, bf16[144,128]{1,0:T(8,128)(2,1)S(1)}, u32[]{:S(2)}, u32[]{:S(2)}) collective-permute-start(bf16[144,128]{1,0:T(8,128)(2,1)S(1)} %get-tuple-element.34), channel_id=1, source_target_pairs={{0,2},{1,3},{2,0},{3,1},{4,6},{5,7},{6,4},{7,5},{8,10},{9,11},{10,... | collective-permute-start | bytes 110600 | tf_op jit(solution)/shard_map/ppermute | solution.py:312
  192.9 6.2 %collective-permute-start.11 = (bf16[144,128]{1,0:T(8,128)(2,1)S(1)}, bf16[144,128]{1,0:T(8,128)(2,1)S(1)}, u32[]{:S(2)}, u32[]{:S(2)}) collective-permute-start(bf16[144,128]{1,0:T(8,128)(2,1)S(1)} %get-tuple-element.35), channel_id=1, source_target_pairs={{0,3},{1,0},{2,1},{3,2},{4,7},{5,4},{6,5},{7,6},{8,11},{9,8},{10,9... | collective-permute-start | bytes 110600 | tf_op jit(solution)/shard_map/ppermute | solution.py:312
  199.1 0.9 collective-permute-done.10.refs_2_
  200.1 2.8 %collective-permute-done.11.refs_3_ = bf16[144,128]{1,0:T(8,128)(2,1)S(1)} collective-permute-done((bf16[144,128]{1,0:T(8,128)(2,1)S(1)}, bf16[144,128]{1,0:T(8,128)(2,1)S(1)}, u32[]{:S(2)}, u32[]{:S(2)}) %collective-permute-start.11) | collective-permute-done | bytes 36896 | tf_op jit(solution)/shard_map/ppermute | solution.py:312
  202.8 1.3 shard_map.67
  204.1 6.5 %all-to-all-start.3 = ((bf16[8,128,128]{2,1,0:T(8,128)(2,1)}), bf16[8,128,128]{2,1,0:T(8,128)(2,1)S(1)}, u32[]{:S(2)}, u32[]{:S(2)}) async-start(bf16[8,128,128]{2,1,0:T(8,128)(2,1)} %get-tuple-element.37), calls=%async_computation.3 | async-start | bytes 524288 | tf_op jit(solution)/shard_map/all_to_all | solution.py:307
  210.7 0.6 dynamic_slice.12
  212.0 4.8 %all-gather.7.cloned.1.call-done = bf16[32,2,144,128]{3,2,1,0:T(8,128)(2,1)} async-done(((bf16[4,2,144,128]{3,2,1,0:T(8,128)(2,1)}), bf16[32,2,144,128]{3,2,1,0:T(8,128)(2,1)}) %all-gather.7.cloned.1.call-update) | async-done | bytes 2359312 | tf_op jit(solution)/shard_map/all_gather | solution.py:373
  216.8 1.2 copy-done.2
  218.1 1.7 copy-done.3
  219.7 6.2 %shard_map.65 = bf16[2,128,256]{2,1,0:T(8,128)(2,1)} custom-call(s32[10]{0:T(128)S(1)} %concatenate.4.table, bf16[8,4,2,144,128]{4,3,2,1,0:T(8,128)(2,1)S(1)} %bitcast.14, bf16[8,2,128,256]{3,2,1,0:T(8,128)(2,1)S(1)} %bitcast.13), custom_call_target="tpu_custom_call" | custom-call | tf_op jit(solution)/shard_map/pallas_call | solution.py:289
  225.9 1.4 shard_map.68
  (29 shorter events, 0.4 us)
Async XLA Ops:
  9.5 17.8 %copy-start = (bf16[1,1,1024,1024]{3,2,1,0:T(8,128)(2,1)S(1)}, bf16[1,1,1024,1024]{3,2,1,0:T(8,128)(2,1)}, u32[]{:S(2)}) copy-start(bf16[1,1,1024,1024]{3,2,1,0:T(8,128)(2,1)} %param.7) | copy-start | bytes 6291460
  9.5 42.0 %all-to-all-start = ((bf16[8,2,128,256]{3,2,1,0:T(8,128)(2,1)}), bf16[8,2,128,256]{3,2,1,0:T(8,128)(2,1)S(1)}, u32[]{:S(2)}, u32[]{:S(2)}) async-start(bf16[8,2,128,256]{3,2,1,0:T(8,128)(2,1)} %copy.7), calls=%async_computation | async-start | bytes 2097152 | tf_op jit(solution)/shard_map/all_to_all | solution.py:307
  27.3 17.1 %copy-start.6 = (s32[64]{0:T(128)S(1)}, s32[64]{0:T(128)}, u32[]{:S(2)}) copy-start(s32[64]{0:T(128)} %param.5) | copy-start | bytes 772
  27.3 17.5 %copy-start.7 = (s32[64]{0:T(128)S(1)}, s32[64]{0:T(128)}, u32[]{:S(2)}) copy-start(s32[64]{0:T(128)} %param.6) | copy-start | bytes 772
  27.9 17.1 %collective-permute-start.3 = (bf16[144,128]{1,0:T(8,128)(2,1)S(1)}, bf16[144,128]{1,0:T(8,128)(2,1)S(1)}, u32[]{:S(2)}, u32[]{:S(2)}) collective-permute-start(bf16[144,128]{1,0:T(8,128)(2,1)S(1)} %get-tuple-element.26), channel_id=1, source_target_pairs={{0,1},{1,2},{2,3},{3,0},{4,5},{5,6},{6,7},{7,4},{8,9},{9,10},{10,1... | collective-permute-start | bytes 110600 | tf_op jit(solution)/shard_map/ppermute | solution.py:312
  29.9 15.6 %collective-permute-start.4 = (bf16[144,128]{1,0:T(8,128)(2,1)S(1)}, bf16[144,128]{1,0:T(8,128)(2,1)S(1)}, u32[]{:S(2)}, u32[]{:S(2)}) collective-permute-start(bf16[144,128]{1,0:T(8,128)(2,1)S(1)} %get-tuple-element.27), channel_id=1, source_target_pairs={{0,2},{1,3},{2,0},{3,1},{4,6},{5,7},{6,4},{7,5},{8,10},{9,11},{10,... | collective-permute-start | bytes 110600 | tf_op jit(solution)/shard_map/ppermute | solution.py:312
  41.1 8.6 %collective-permute-start.5 = (bf16[144,128]{1,0:T(8,128)(2,1)S(1)}, bf16[144,128]{1,0:T(8,128)(2,1)S(1)}, u32[]{:S(2)}, u32[]{:S(2)}) collective-permute-start(bf16[144,128]{1,0:T(8,128)(2,1)S(1)} %get-tuple-element.28), channel_id=1, source_target_pairs={{0,3},{1,0},{2,1},{3,2},{4,7},{5,4},{6,5},{7,6},{8,11},{9,8},{10,9... | collective-permute-start | bytes 110600 | tf_op jit(solution)/shard_map/ppermute | solution.py:312
  52.3 81.3 %all-to-all-start.1 = ((bf16[32,144,128]{2,1,0:T(8,128)(2,1)}), bf16[32,144,128]{2,1,0:T(8,128)(2,1)S(1)}, u32[]{:S(2)}, u32[]{:S(2)}) async-start(bf16[32,144,128]{2,1,0:T(8,128)(2,1)} %shard_map.62), calls=%async_computation.1 | async-start | bytes 2359296 | tf_op jit(solution)/shard_map/all_to_all | solution.py:307
  63.3 34.3 %all-gather.5.cloned.1.call-start = ((), (), s32[]{:S(2)}) async-start(), calls=%async_computation.4 | async-start | bytes 1179648 | tf_op jit(solution)/shard_map/all_gather | solution.py:350
  97.6 1.2 copy-start.1
  99.7 22.5 %collective-permute-start = (bf16[2,144,128]{2,1,0:T(8,128)(2,1)S(1)}, bf16[2,144,128]{2,1,0:T(8,128)(2,1)S(1)}, u32[]{:S(2)}, u32[]{:S(2)}) collective-permute-start(bf16[2,144,128]{2,1,0:T(8,128)(2,1)S(1)} %get-tuple-element.21), channel_id=1, source_target_pairs={{0,1},{1,2},{2,3},{3,0},{4,5},{5,6},{6,7},{7,4},{8,9},{9,10},{10,1... | collective-permute-start | bytes 221192 | tf_op jit(solution)/shard_map/ppermute | solution.py:312
  107.5 14.8 %collective-permute-start.1 = (bf16[2,144,128]{2,1,0:T(8,128)(2,1)S(1)}, bf16[2,144,128]{2,1,0:T(8,128)(2,1)S(1)}, u32[]{:S(2)}, u32[]{:S(2)}) collective-permute-start(bf16[2,144,128]{2,1,0:T(8,128)(2,1)S(1)} %get-tuple-element.22), channel_id=1, source_target_pairs={{0,2},{1,3},{2,0},{3,1},{4,6},{5,7},{6,4},{7,5},{8,10},{9,11},{10,... | collective-permute-start | bytes 221192 | tf_op jit(solution)/shard_map/ppermute | solution.py:312
  116.0 15.9 %collective-permute-start.2 = (bf16[2,144,128]{2,1,0:T(8,128)(2,1)S(1)}, bf16[2,144,128]{2,1,0:T(8,128)(2,1)S(1)}, u32[]{:S(2)}, u32[]{:S(2)}) collective-permute-start(bf16[2,144,128]{2,1,0:T(8,128)(2,1)S(1)} %get-tuple-element.23), channel_id=1, source_target_pairs={{0,3},{1,0},{2,1},{3,2},{4,7},{5,4},{6,5},{7,6},{8,11},{9,8},{10,9... | collective-permute-start | bytes 221192 | tf_op jit(solution)/shard_map/ppermute | solution.py:312
  132.6 1.0 copy-start.4
  134.2 46.5 %all-to-all-start.2 = ((bf16[32,144,128]{2,1,0:T(8,128)(2,1)}), bf16[32,144,128]{2,1,0:T(8,128)(2,1)S(1)}, u32[]{:S(2)}, u32[]{:S(2)}) async-start(bf16[32,144,128]{2,1,0:T(8,128)(2,1)} %copy-done.4), calls=%async_computation.2 | async-start | bytes 2359296 | tf_op jit(solution)/shard_map/all_to_all | solution.py:307
  141.1 75.8 %all-gather.7.cloned.1.call-start = ((), (), s32[]{:S(2)}) async-start(), calls=%async_computation.5 | async-start | bytes 2654208 | tf_op jit(solution)/shard_map/all_gather | solution.py:373
  141.1 18.6 %collective-permute-start.8 = (bf16[2,144,128]{2,1,0:T(8,128)(2,1)S(1)}, bf16[2,144,128]{2,1,0:T(8,128)(2,1)S(1)}, u32[]{:S(2)}, u32[]{:S(2)}) collective-permute-start(bf16[2,144,128]{2,1,0:T(8,128)(2,1)S(1)} %shard_map.63.refs_0_), channel_id=1, source_target_pairs={{0,3},{1,0},{2,1},{3,2},{4,7},{5,4},{6,5},{7,6},{8,11},{9,8},{10,9... | collective-permute-start | bytes 221192 | tf_op jit(solution)/shard_map/ppermute | solution.py:312
  146.0 25.5 %collective-permute-start.7 = (bf16[2,144,128]{2,1,0:T(8,128)(2,1)S(1)}, bf16[2,144,128]{2,1,0:T(8,128)(2,1)S(1)}, u32[]{:S(2)}, u32[]{:S(2)}) collective-permute-start(bf16[2,144,128]{2,1,0:T(8,128)(2,1)S(1)} %shard_map.63.refs_0_), channel_id=1, source_target_pairs={{0,2},{1,3},{2,0},{3,1},{4,6},{5,7},{6,4},{7,5},{8,10},{9,11},{10,... | collective-permute-start | bytes 221192 | tf_op jit(solution)/shard_map/ppermute | solution.py:312
  153.5 18.1 %collective-permute-start.6 = (bf16[2,144,128]{2,1,0:T(8,128)(2,1)S(1)}, bf16[2,144,128]{2,1,0:T(8,128)(2,1)S(1)}, u32[]{:S(2)}, u32[]{:S(2)}) collective-permute-start(bf16[2,144,128]{2,1,0:T(8,128)(2,1)S(1)} %shard_map.63.refs_0_), channel_id=1, source_target_pairs={{0,1},{1,2},{2,3},{3,0},{4,5},{5,6},{6,7},{7,4},{8,9},{9,10},{10,1... | collective-permute-start | bytes 221192 | tf_op jit(solution)/shard_map/ppermute | solution.py:312
  172.1 0.7 copy-start.5
  181.3 17.8 %collective-permute-start.9 = (bf16[144,128]{1,0:T(8,128)(2,1)S(1)}, bf16[144,128]{1,0:T(8,128)(2,1)S(1)}, u32[]{:S(2)}, u32[]{:S(2)}) collective-permute-start(bf16[144,128]{1,0:T(8,128)(2,1)S(1)} %get-tuple-element.33), channel_id=1, source_target_pairs={{0,1},{1,2},{2,3},{3,0},{4,5},{5,6},{6,7},{7,4},{8,9},{9,10},{10,1... | collective-permute-start | bytes 110600 | tf_op jit(solution)/shard_map/ppermute | solution.py:312
  186.6 13.4 %collective-permute-start.10 = (bf16[144,128]{1,0:T(8,128)(2,1)S(1)}, bf16[144,128]{1,0:T(8,128)(2,1)S(1)}, u32[]{:S(2)}, u32[]{:S(2)}) collective-permute-start(bf16[144,128]{1,0:T(8,128)(2,1)S(1)} %get-tuple-element.34), channel_id=1, source_target_pairs={{0,2},{1,3},{2,0},{3,1},{4,6},{5,7},{6,4},{7,5},{8,10},{9,11},{10,... | collective-permute-start | bytes 110600 | tf_op jit(solution)/shard_map/ppermute | solution.py:312
  192.9 10.0 %collective-permute-start.11 = (bf16[144,128]{1,0:T(8,128)(2,1)S(1)}, bf16[144,128]{1,0:T(8,128)(2,1)S(1)}, u32[]{:S(2)}, u32[]{:S(2)}) collective-permute-start(bf16[144,128]{1,0:T(8,128)(2,1)S(1)} %get-tuple-element.35), channel_id=1, source_target_pairs={{0,3},{1,0},{2,1},{3,2},{4,7},{5,4},{6,5},{7,6},{8,11},{9,8},{10,9... | collective-permute-start | bytes 110600 | tf_op jit(solution)/shard_map/ppermute | solution.py:312
  204.1 21.8 %all-to-all-start.3 = ((bf16[8,128,128]{2,1,0:T(8,128)(2,1)}), bf16[8,128,128]{2,1,0:T(8,128)(2,1)S(1)}, u32[]{:S(2)}, u32[]{:S(2)}) async-start(bf16[8,128,128]{2,1,0:T(8,128)(2,1)} %get-tuple-element.37), calls=%async_computation.3 | async-start | bytes 524288 | tf_op jit(solution)/shard_map/all_to_all | solution.py:307
  216.8 1.2 copy-start.2
  218.1 1.7 copy-start.3
Sparse Core Ops, SparseCore 0:
  67.5 30.1 all-gather.4
  173.0 43.8 all-gather.6

commit v4 on v3

--- a/solution.py
+++ b/solution.py
@@ -49,25 +49,44 @@
     return jax.ShapeDtypeStruct(shape, dtype)
 
 
-def history_kernel(place, column, half, *refs):
-    outs, held = refs[:-1], refs[-1]
-    shards, depth, tile = held.shape
-    for part, row, step, inner, size in pieces(tile, shards):
-        if step < 4:
-            start = lax.rem(place[0] + step, 8) * tile + inner
-            held[part, row : row + size] = column[ds(start, size, 16), :]
-        else:
-            held[part, row : row + size] = half[inner : inner + size]
-    for step in range(shards):
-        outs[step][...] = held[lax.rem(place[1] + step, shards)]
-
-
-def cut_history(place, history, shards, tile):
-    depth = (4 * tile + tile // 2) // shards
+def split_kernel(grads, out, sems):
+    copies = []
+    for band in range(out.shape[0]):
+        for block in range(out.shape[1]):
+            rows = pl.ds(band * out.shape[2], out.shape[2])
+            copies.append(
+                pltpu.make_async_copy(grads.at[block, rows], out.at[band, block], sems.at[band, block])
+            )
+    for copy in copies:
+        copy.start()
+    for copy in copies:
+        copy.wait()
+
+
+def split_bands(grads, replicas):
+    home_count, order_full, width = grads.shape
+    return pl.pallas_call(
+        split_kernel,
+        out_shape=like((replicas, home_count, order_full // replicas, width)),
+        in_specs=[pl.BlockSpec(memory_space=pl.ANY)],
+        out_specs=pl.BlockSpec(memory_space=pl.ANY),
+        scratch_shapes=[pltpu.SemaphoreType.DMA((replicas, home_count))],
+    )(grads)
+
+
+def history_kernel(place, column, half, out):
+    tile = column.shape[1]
+    for step in range(4):
+        out[step * tile : (step + 1) * tile] = column[ds(lax.rem(place[0] + step, 8) * tile, tile, tile), :]
+    out[4 * tile : 4 * tile + tile // 2] = half[...]
+
+
+def cut_history(place, history, tile):
     order_full = history.shape[0]
+    shape = (order_full, tile)
     return pl.pallas_call(
         history_kernel,
-        out_shape=[like((depth, tile))] * shards,
+        out_shape=like(shape),
         grid_spec=pltpu.PrefetchScalarGridSpec(
             num_scalar_prefetch=1,
             grid=(1,),
@@ -81,23 +100,22 @@
                     ),
                 ),
             ],
-            out_specs=[pl.BlockSpec((depth, tile), lambda i, place: (0, 0))] * shards,
-            scratch_shapes=[pltpu.VMEM((shards, depth, tile), jnp.bfloat16)],
+            out_specs=pl.BlockSpec(shape, lambda i, place: (0, 0)),
         ),
         compiler_params=BIG,
     )(place, history, history)
 
 
-def spread_kernel(table, *refs):
-    arrived, out = refs[:-1], refs[-1]
-    shards = len(arrived)
+def spread_kernel(table, bands, out):
+    depth = out.shape[1]
+    start = table[BLK_AT] * depth
     out[...] = jnp.zeros_like(out)
-    for step in range(shards):
-        holder = table[HOLDER_AT + lax.rem(table[BLK_AT] + shards - step, shards)]
+    for shard in range(bands.shape[0]):
+        holder = table[HOLDER_AT + shard]
 
         @pl.when(holder >= 0)
-        def _(step=step, holder=holder):
-            out[lax.div(holder, 2)] = arrived[step][...]
+        def _(shard=shard, holder=holder):
+            out[lax.div(holder, 2)] = bands[shard, ds(start, depth, 16), :]
 
 
 def gram_kernel(place, cols, *refs):
@@ -145,27 +163,15 @@
         out[block] = (DECAY * history + gram[block] + damping).astype(jnp.bfloat16)
 
 
-def order_kernel(table, *refs):
-    arrived, out = refs[:-1], refs[-1]
-    shards = len(arrived)
-    for step in range(shards):
-        out[lax.rem(table[BLK_AT] + shards - step, shards)] = arrived[step][...]
-
-
-def choose_kernel(table, came, *outs):
-    shards = len(outs)
-    for step in range(shards):
-        holder = table[HOLDER_AT + lax.rem(table[BLK_AT] + step, shards)]
-        outs[step][...] = came[lax.div(jnp.maximum(holder, 0), 2)]
-
-
-def turn_kernel(table, *refs):
-    arrived, band, sent = refs[:-2], refs[-2], refs[-1]
-    shards = len(arrived)
-    depth, tile = arrived[0].shape
-    for step in range(shards):
-        part = lax.rem(table[BLK_AT] + shards - step, shards)
-        band[ds(part * depth, depth, 16), :] = arrived[step][...]
+def choose_kernel(table, came, out):
+    for shard in range(out.shape[0]):
+        out[shard] = came[lax.div(jnp.maximum(table[HOLDER_AT + shard], 0), 2)]
+
+
+def turn_kernel(table, parts, band, sent):
+    shards, depth, tile = parts.shape
+    for part in range(shards):
+        band[part * depth : (part + 1) * depth] = parts[part]
     sent[...] = jnp.zeros_like(sent)
     for step in range(1, 4):
         sent[lax.rem(table[REP_AT] + step, 8)] = band[step * tile : (step + 1) * tile]
@@ -340,17 +346,14 @@
     my_need = lax.dynamic_slice_in_dim(iterations, my_own * home_count, home_count)
     table = jnp.concatenate([place, my_owners, my_need, holder]).astype(jnp.int32)
 
-    outgoing = (
-        partial_grads[0].reshape(home_count, replicas, tile, band_cols).transpose(1, 0, 2, 3)
-    )
-    history_parts = cut_history(place, history, shards, tile)
-    history_arrived = swap(history_parts, shards)
+    outgoing = split_bands(partial_grads[0], replicas)
+    history_bands = lax.all_gather(cut_history(place, history, tile), "blk", axis=0, tiled=False)
     partials = exchange(outgoing, "rep")
     grad_tile = jnp.sum(partials.astype(jnp.float32), axis=0).astype(jnp.bfloat16)
-    grad_cols = lax.all_gather(grad_tile, "rep", axis=0, tiled=False)
-
-    history_sent = call(spread_kernel, [table, *history_arrived], like((owners, depth, tile)))
-    history_came = exchange(after(history_sent, grad_tile), "own")
+    grad_cols = exchange(jnp.broadcast_to(grad_tile[None], (replicas,) + grad_tile.shape), "rep")
+
+    history_sent = call(spread_kernel, [table, history_bands], like((owners, depth, tile)))
+    history_came = exchange(after(history_sent, grad_cols), "own")
 
     gram_parts = pl.pallas_call(
         gram_kernel,
@@ -367,16 +370,14 @@
         [like((home_count, depth, tile), jnp.float32), like((owners, depth, tile))],
     )
     stat = call(stat_kernel, [table, gram, history_came], like((home_count, depth, tile)))
-    stat_band = call(
-        order_kernel, [table, *swap([stat] * shards, shards)], like((shards, home_count, depth, tile))
-    )
+    gram_came = exchange(after(gram_sent, history_came), "own")
+    stat_band = lax.all_gather(stat, "blk", axis=0, tiled=False)
     stat_full = lax.all_gather(stat_band, "rep", axis=0, tiled=False)
 
-    gram_came = exchange(after(gram_sent, stat), "own")
-    slot_parts = call(choose_kernel, [table, gram_came], [like((depth, tile))] * shards)
+    slot_parts = call(choose_kernel, [table, gram_came], like((shards, depth, tile)))
     band, turned = call(
         turn_kernel,
-        [table, *swap(slot_parts, shards)],
+        [table, exchange(slot_parts, "blk")],
         [like((shards * depth, tile)), like((replicas, tile, tile))],
     )
     turned = exchange(turned, "rep")

time: 236 us -> 284 us (1.20)
  starting transfers between devices: 118 us -> 66.2 us
  blocking collectives: 0 us -> 50.6 us
  Pallas kernels: 14.7 us -> 47.5 us
  waiting for transfers between devices: 76.8 us -> 92 us
    ppermute x12 -> x3, starting transfers between devices: 75.3 us -> 13.4 us  [swap(): lax.ppermute(parts[step], 'blk', [(i, (i + step) % count) for i in range(...]
    pallas_call x1 -> x2, Pallas kernels: 0.64 us -> 34.3 us  [the longest x1 33 us: split_bands(): pl.pallas_call(split_kernel, out_shape=like((replicas, home_count, order_...]
    all_gather x0 -> x1, blocking collectives: none -> 31.8 us  [body(): stat_band = lax.all_gather(stat, 'blk', axis=0, tiled=False)]
    all_to_all x0 -> x1, blocking collectives: none -> 18.9 us  [exchange(): return lax.all_to_all(array, axis, split_axis=0, concat_axis=0, tiled=True)]
    ppermute x12 -> x3, waiting for transfers between devices: 29.8 us -> 13.1 us  [swap(): lax.ppermute(parts[step], 'blk', [(i, (i + step) % count) for i in range(...]
    all_to_all x4 -> x5, waiting for transfers between devices: 7.88 us -> 23.5 us  [exchange(): return lax.all_to_all(array, axis, split_axis=0, concat_axis=0, tiled=True)]
    all_to_all x4 -> x5, starting transfers between devices: 42.2 us -> 52.7 us  [exchange(): return lax.all_to_all(array, axis, split_axis=0, concat_axis=0, tiled=True)]
    all_gather x1, waiting for transfers between devices: 4.85 us -> 14.1 us  [body(): stat_full = lax.all_gather(stat_band, 'rep', axis=0, tiled=False)]
  transfers between devices with their start and end apart: 18 -> 10, of which waited for: 9 -> 6; matrix products, arithmetic and copies ran while one was open for 1% -> 2% of each run, Pallas kernels for 5% -> 5%
where the time goes in v4:
time: 284 us; the launch traced here: 283 us
  waiting for transfers between devices  92 us (32%)
  starting transfers between devices  66.2 us (23%)
  blocking collectives  50.6 us (18%)
  Pallas kernels  47.5 us (17%)
  between operations  14.8 us (5%)
  local copies, waits for them, and re-layouts  9.52 us (3%)
    all_to_all x5, starting transfers between devices, exchange(): return lax.all_to_all(array, axis, split_axis=0, concat_axis=0, tiled=True)  52.7 us
    all_gather x1, waiting for transfers between devices, body(): lax.all_gather(cut_history(place, history, tile), 'blk', axis=0, tiled=Fa...  41.3 us
    pallas_call x1, Pallas kernels, split_bands(): pl.pallas_call(split_kernel, out_shape=like((replicas, home_count, order_...  33 us
    all_gather x1, blocking collectives, body(): stat_band = lax.all_gather(stat, 'blk', axis=0, tiled=False)  31.8 us
    all_to_all x5, waiting for transfers between devices, exchange(): return lax.all_to_all(array, axis, split_axis=0, concat_axis=0, tiled=True)  23.5 us
    all_to_all x1, blocking collectives, exchange(): return lax.all_to_all(array, axis, split_axis=0, concat_axis=0, tiled=True)  18.9 us
    all_gather x1, waiting for transfers between devices, body(): stat_full = lax.all_gather(stat_band, 'rep', axis=0, tiled=False)  14.1 us
    ppermute x3, starting transfers between devices, swap(): lax.ppermute(parts[step], 'blk', [(i, (i + step) % count) for i in range(...  13.4 us
  transfers between devices with their start and end apart: 10, of which 6 were waited for; matrix products, arithmetic and copies ran while one was open for 2% of the time, Pallas kernels for 5%

profile of v4, /device:TPU:1, one launch (start us, length us, event | category | flops | bytes accessed | tf_op | source)
XLA Modules:
  0.0 283.2 jit_solution(16878579729139712553)
XLA Ops:
  7.2 33.0 %shard_map.59 = bf16[8,2,128,256]{3,2,1,0:T(8,128)(2,1)} custom-call(bf16[2,1024,256]{2,1,0:T(8,128)(2,1)} %bitcast.14), custom_call_target="tpu_custom_call" | custom-call | tf_op jit(solution)/shard_map/pallas_call | solution.py:68
  40.2 0.0 copy-start
  40.2 18.4 %all-to-all-start = ((bf16[8,2,128,256]{3,2,1,0:T(8,128)(2,1)}), bf16[8,2,128,256]{3,2,1,0:T(8,128)(2,1)}, u32[]{:S(2)}, u32[]{:S(2)}) async-start(bf16[8,2,128,256]{3,2,1,0:T(8,128)(2,1)} %shard_map.59), calls=%async_computation | async-start | bytes 2097152 | tf_op jit(solution)/shard_map/all_to_all | solution.py:313
  58.6 0.1 pad_add_fusion.place
  58.7 1.3 shard_map.62
  60.0 0.0 all-gather.6.cloned.1.call-update
  60.0 13.8 %all-to-all-done = bf16[8,2,128,256]{3,2,1,0:T(8,128)(2,1)} async-done(((bf16[8,2,128,256]{3,2,1,0:T(8,128)(2,1)}), bf16[8,2,128,256]{3,2,1,0:T(8,128)(2,1)}, u32[]{:S(2)}, u32[]{:S(2)}) %all-to-all-start) | async-done | bytes 1048608 | tf_op jit(solution)/shard_map/all_to_all | solution.py:313
  73.8 1.4 reduce_sum.32
  75.2 1.1 broadcast_in_dim.41
  76.3 4.5 %all-to-all-start.1 = ((bf16[8,2,128,256]{3,2,1,0:T(8,128)(2,1)}), bf16[8,2,128,256]{3,2,1,0:T(8,128)(2,1)S(1)}, u32[]{:S(2)}, u32[]{:S(2)}) async-start(bf16[8,2,128,256]{3,2,1,0:T(8,128)(2,1)} %broadcast_in_dim.41), calls=%async_computation.1 | async-start | bytes 2097152 | tf_op jit(solution)/shard_map/all_to_all | solution.py:313
  80.8 0.1 dynamic_slice.11
  80.8 0.1 dynamic_slice.10
  80.9 0.2 select_reduce_fusion
  81.1 0.1 select_reduce_fusion.1
  81.2 0.1 concatenate.4.table
  81.3 41.3 %all-gather.6.cloned.1.call-done = bf16[4096,128]{1,0:T(8,128)(2,1)} async-done(((bf16[1024,128]{1,0:T(8,128)(2,1)}), bf16[4096,128]{1,0:T(8,128)(2,1)}) %all-gather.6.cloned.1.call-update) | async-done | bytes 1048592 | tf_op jit(solution)/shard_map/all_gather | solution.py:350
  122.6 1.2 copy-done.4
  123.8 0.7 shard_map.63
  124.6 1.0 copy-done.1
  125.6 9.2 %all-to-all-start.2 = ((bf16[32,144,128]{2,1,0:T(8,128)(2,1)}), bf16[32,144,128]{2,1,0:T(8,128)(2,1)}, u32[]{:S(2)}, u32[]{:S(2)}) async-start(bf16[32,144,128]{2,1,0:T(8,128)(2,1)} %copy-done.1), calls=%async_computation.2 | async-start | bytes 2359296 | tf_op jit(solution)/shard_map/all_to_all | solution.py:313
  134.8 0.9 shard_map.60
  135.7 3.0 %collective-permute-start = (bf16[2,144,128]{2,1,0:T(8,128)(2,1)S(1)}, bf16[2,144,128]{2,1,0:T(8,128)(2,1)S(1)}, u32[]{:S(2)}, u32[]{:S(2)}) collective-permute-start(bf16[2,144,128]{2,1,0:T(8,128)(2,1)S(1)} %get-tuple-element.13), channel_id=1, source_target_pairs={{0,1},{1,2},{2,3},{3,0},{4,5},{5,6},{6,7},{7,4},{8,9},{9,10},{10,1... | collective-permute-start | bytes 221192 | tf_op jit(solution)/shard_map/ppermute | solution.py:318
  138.7 6.3 %collective-permute-start.1 = (bf16[2,144,128]{2,1,0:T(8,128)(2,1)S(1)}, bf16[2,144,128]{2,1,0:T(8,128)(2,1)S(1)}, u32[]{:S(2)}, u32[]{:S(2)}) collective-permute-start(bf16[2,144,128]{2,1,0:T(8,128)(2,1)S(1)} %get-tuple-element.14), channel_id=1, source_target_pairs={{0,2},{1,3},{2,0},{3,1},{4,6},{5,7},{6,4},{7,5},{8,10},{9,11},{10,... | collective-permute-start | bytes 221192 | tf_op jit(solution)/shard_map/ppermute | solution.py:318
  145.0 4.1 %collective-permute-start.2 = (bf16[2,144,128]{2,1,0:T(8,128)(2,1)S(1)}, bf16[2,144,128]{2,1,0:T(8,128)(2,1)S(1)}, u32[]{:S(2)}, u32[]{:S(2)}) collective-permute-start(bf16[2,144,128]{2,1,0:T(8,128)(2,1)S(1)} %get-tuple-element.15), channel_id=1, source_target_pairs={{0,3},{1,0},{2,1},{3,2},{4,7},{5,4},{6,5},{7,6},{8,11},{9,8},{10,9... | collective-permute-start | bytes 221192 | tf_op jit(solution)/shard_map/ppermute | solution.py:318
  149.1 9.9 %collective-permute-done.refs_1_ = bf16[2,144,128]{2,1,0:T(8,128)(2,1)S(1)} collective-permute-done((bf16[2,144,128]{2,1,0:T(8,128)(2,1)S(1)}, bf16[2,144,128]{2,1,0:T(8,128)(2,1)S(1)}, u32[]{:S(2)}, u32[]{:S(2)}) %collective-permute-start) | collective-permute-done | bytes 73760 | tf_op jit(solution)/shard_map/ppermute | solution.py:318
  159.1 3.2 %collective-permute-done.1.refs_2_ = bf16[2,144,128]{2,1,0:T(8,128)(2,1)S(1)} collective-permute-done((bf16[2,144,128]{2,1,0:T(8,128)(2,1)S(1)}, bf16[2,144,128]{2,1,0:T(8,128)(2,1)S(1)}, u32[]{:S(2)}, u32[]{:S(2)}) %collective-permute-start.1) | collective-permute-done | bytes 73760 | tf_op jit(solution)/shard_map/ppermute | solution.py:318
  162.3 0.7 shard_map.61
  163.0 1.0 copy-done.3
  164.0 9.7 %all-to-all-done.2.came = bf16[32,144,128]{2,1,0:T(8,128)(2,1)} async-done(((bf16[32,144,128]{2,1,0:T(8,128)(2,1)}), bf16[32,144,128]{2,1,0:T(8,128)(2,1)}, u32[]{:S(2)}, u32[]{:S(2)}) %all-to-all-start.2) | async-done | bytes 1179680 | tf_op jit(solution)/shard_map/all_to_all | solution.py:313
  173.7 10.5 %all-to-all-start.3 = ((bf16[32,144,128]{2,1,0:T(8,128)(2,1)}), bf16[32,144,128]{2,1,0:T(8,128)(2,1)}, u32[]{:S(2)}, u32[]{:S(2)}) async-start(bf16[32,144,128]{2,1,0:T(8,128)(2,1)} %copy-done.3), calls=%async_computation.3 | async-start | bytes 2359296 | tf_op jit(solution)/shard_map/all_to_all | solution.py:313
  184.2 0.0 all-gather.8.cloned.1.call-start
  184.2 1.3 shard_map.64
  185.6 31.8 %all-gather.1 = bf16[8,144,128]{2,1,0:T(8,128)(2,1)} all-gather(bf16[2,144,128]{2,1,0:T(8,128)(2,1)S(1)} %shard_map.64), channel_id=3, replica_groups=mesh['rep'=8,'own'=32,'blk'=4] {'blk'}, dimensions={0}, use_global_device_ids=true | all-gather | bytes 368640 | tf_op jit(solution)/shard_map/all_gather | solution.py:374
  217.3 0.0 all-gather.8.cloned.1.call-update
  217.4 1.3 shard_map.66
  218.7 18.9 %all_to_all.30.parts = bf16[4,144,128]{2,1,0:T(8,128)(2,1)S(1)} all-to-all(bf16[4,144,128]{2,1,0:T(8,128)(2,1)S(1)} %shard_map.66), channel_id=1, replica_groups=mesh['rep'=8,'own'=32,'blk'=4] {'blk'}, dimensions={0} | all-to-all | bytes 294912 | tf_op jit(solution)/shard_map/all_to_all | solution.py:313
  237.6 0.6 shard_map.67
  238.2 0.0 copy-start.5
  238.2 0.7 copy-done.5
  238.9 10.2 %all-to-all-start.5 = ((bf16[8,128,128]{2,1,0:T(8,128)(2,1)}), bf16[8,128,128]{2,1,0:T(8,128)(2,1)S(1)}, u32[]{:S(2)}, u32[]{:S(2)}) async-start(bf16[8,128,128]{2,1,0:T(8,128)(2,1)} %copy-done.5), calls=%async_computation.5 | async-start | bytes 524288 | tf_op jit(solution)/shard_map/all_to_all | solution.py:313
  249.1 1.2 dynamic_slice.12
  250.9 0.7 pad_add_fusion.1.place
  251.6 14.1 %all-gather.8.cloned.1.call-done = bf16[32,2,144,128]{3,2,1,0:T(8,128)(2,1)} async-done(((bf16[4,2,144,128]{3,2,1,0:T(8,128)(2,1)}), bf16[32,2,144,128]{3,2,1,0:T(8,128)(2,1)}) %all-gather.8.cloned.1.call-update) | async-done | bytes 2359312 | tf_op jit(solution)/shard_map/all_gather | solution.py:375
  265.7 1.7 copy-done.2
  267.4 0.7 copy-done.7
  268.0 6.2 %shard_map.65 = bf16[2,128,256]{2,1,0:T(8,128)(2,1)} custom-call(s32[10]{0:T(128)S(1)} %copy-done.7, bf16[8,4,2,144,128]{4,3,2,1,0:T(8,128)(2,1)S(1)} %bitcast.11, bf16[8,2,128,256]{3,2,1,0:T(8,128)(2,1)S(1)} %all-to-all-done.1.cols), custom_call_target="tpu_custom_call" | custom-call | tf_op jit(solution)/shard_map/pallas_call | solution.py:295
  274.2 0.7 copy-done.8
  274.9 1.4 shard_map.68
  (23 shorter events, 0.1 us)
Async XLA Ops:
  40.2 18.5 %copy-start = (bf16[1,1,1024,1024]{3,2,1,0:T(8,128)(2,1)S(1)}, bf16[1,1,1024,1024]{3,2,1,0:T(8,128)(2,1)}, u32[]{:S(2)}) copy-start(bf16[1,1,1024,1024]{3,2,1,0:T(8,128)(2,1)} %param.7) | copy-start | bytes 6291460
  40.2 33.6 %all-to-all-start = ((bf16[8,2,128,256]{3,2,1,0:T(8,128)(2,1)}), bf16[8,2,128,256]{3,2,1,0:T(8,128)(2,1)}, u32[]{:S(2)}, u32[]{:S(2)}) async-start(bf16[8,2,128,256]{3,2,1,0:T(8,128)(2,1)} %shard_map.59), calls=%async_computation | async-start | bytes 2097152 | tf_op jit(solution)/shard_map/all_to_all | solution.py:313
  58.6 64.0 %all-gather.6.cloned.1.call-start = ((), (), s32[]{:S(2)}) async-start(), calls=%async_computation.6 | async-start | bytes 1310720 | tf_op jit(solution)/shard_map/all_gather | solution.py:350
  76.3 4.5 %copy-start.10 = (s32[64]{0:T(128)S(1)}, s32[64]{0:T(128)}, u32[]{:S(2)}) copy-start(s32[64]{0:T(128)} %param.6) | copy-start | bytes 772
  76.3 4.5 %copy-start.11 = (s32[64]{0:T(128)S(1)}, s32[64]{0:T(128)}, u32[]{:S(2)}) copy-start(s32[64]{0:T(128)} %param.5) | copy-start | bytes 772
  76.3 49.3 %all-to-all-start.1 = ((bf16[8,2,128,256]{3,2,1,0:T(8,128)(2,1)}), bf16[8,2,128,256]{3,2,1,0:T(8,128)(2,1)S(1)}, u32[]{:S(2)}, u32[]{:S(2)}) async-start(bf16[8,2,128,256]{3,2,1,0:T(8,128)(2,1)} %broadcast_in_dim.41), calls=%async_computation.1 | async-start | bytes 2097152 | tf_op jit(solution)/shard_map/all_to_all | solution.py:313
  81.2 44.4 %copy-start.9 = (s32[4]{0:T(128)}, s32[4]{0:T(128)S(1)}, u32[]{:S(2)}) copy-start(s32[4]{0:T(128)S(1)} %broadcast_add_fusion) | copy-start | bytes 52
  81.3 156.2 %copy-start.6 = (s32[10]{0:T(128)}, s32[10]{0:T(128)S(1)}, u32[]{:S(2)}) copy-start(s32[10]{0:T(128)S(1)} %concatenate.4.table) | copy-start | bytes 124
  122.6 1.2 copy-start.4
  124.6 1.0 copy-start.1
  125.6 48.1 %all-to-all-start.2 = ((bf16[32,144,128]{2,1,0:T(8,128)(2,1)}), bf16[32,144,128]{2,1,0:T(8,128)(2,1)}, u32[]{:S(2)}, u32[]{:S(2)}) async-start(bf16[32,144,128]{2,1,0:T(8,128)(2,1)} %copy-done.1), calls=%async_computation.2 | async-start | bytes 2359296 | tf_op jit(solution)/shard_map/all_to_all | solution.py:313
  135.7 23.4 %collective-permute-start = (bf16[2,144,128]{2,1,0:T(8,128)(2,1)S(1)}, bf16[2,144,128]{2,1,0:T(8,128)(2,1)S(1)}, u32[]{:S(2)}, u32[]{:S(2)}) collective-permute-start(bf16[2,144,128]{2,1,0:T(8,128)(2,1)S(1)} %get-tuple-element.13), channel_id=1, source_target_pairs={{0,1},{1,2},{2,3},{3,0},{4,5},{5,6},{6,7},{7,4},{8,9},{9,10},{10,1... | collective-permute-start | bytes 221192 | tf_op jit(solution)/shard_map/ppermute | solution.py:318
  138.7 23.6 %collective-permute-start.1 = (bf16[2,144,128]{2,1,0:T(8,128)(2,1)S(1)}, bf16[2,144,128]{2,1,0:T(8,128)(2,1)S(1)}, u32[]{:S(2)}, u32[]{:S(2)}) collective-permute-start(bf16[2,144,128]{2,1,0:T(8,128)(2,1)S(1)} %get-tuple-element.14), channel_id=1, source_target_pairs={{0,2},{1,3},{2,0},{3,1},{4,6},{5,7},{6,4},{7,5},{8,10},{9,11},{10,... | collective-permute-start | bytes 221192 | tf_op jit(solution)/shard_map/ppermute | solution.py:318
  145.0 17.3 %collective-permute-start.2 = (bf16[2,144,128]{2,1,0:T(8,128)(2,1)S(1)}, bf16[2,144,128]{2,1,0:T(8,128)(2,1)S(1)}, u32[]{:S(2)}, u32[]{:S(2)}) collective-permute-start(bf16[2,144,128]{2,1,0:T(8,128)(2,1)S(1)} %get-tuple-element.15), channel_id=1, source_target_pairs={{0,3},{1,0},{2,1},{3,2},{4,7},{5,4},{6,5},{7,6},{8,11},{9,8},{10,9... | collective-permute-start | bytes 221192 | tf_op jit(solution)/shard_map/ppermute | solution.py:318
  163.0 1.0 copy-start.3
  173.7 43.6 %all-to-all-start.3 = ((bf16[32,144,128]{2,1,0:T(8,128)(2,1)}), bf16[32,144,128]{2,1,0:T(8,128)(2,1)}, u32[]{:S(2)}, u32[]{:S(2)}) async-start(bf16[32,144,128]{2,1,0:T(8,128)(2,1)} %copy-done.3), calls=%async_computation.3 | async-start | bytes 2359296 | tf_op jit(solution)/shard_map/all_to_all | solution.py:313
  184.2 81.5 %all-gather.8.cloned.1.call-start = ((), (), s32[]{:S(2)}) async-start(), calls=%async_computation.7 | async-start | bytes 2654208 | tf_op jit(solution)/shard_map/all_gather | solution.py:375
  238.2 0.7 copy-start.5
  238.9 35.3 %all-to-all-start.5 = ((bf16[8,128,128]{2,1,0:T(8,128)(2,1)}), bf16[8,128,128]{2,1,0:T(8,128)(2,1)S(1)}, u32[]{:S(2)}, u32[]{:S(2)}) async-start(bf16[8,128,128]{2,1,0:T(8,128)(2,1)} %copy-done.5), calls=%async_computation.5 | async-start | bytes 524288 | tf_op jit(solution)/shard_map/all_to_all | solution.py:313
  265.7 1.7 copy-start.2
  267.4 0.7 copy-start.7
  274.2 0.7 copy-start.8
Sparse Core Ops, SparseCore 0:
  62.7 59.8 all-gather.5
  217.5 48.1 all-gather.7

commit v5 on v3

--- a/solution.py
+++ b/solution.py
@@ -100,35 +100,33 @@
             out[lax.div(holder, 2)] = arrived[step][...]
 
 
-def gram_kernel(place, cols, *refs):
-    outs, held = refs[:-1], refs[-1]
-    shards, home_count, depth, tile = held.shape
-    order_full = cols.shape[0] * tile
+def gram_kernel(place, *refs):
+    out = refs[-1]
+    shards, home_count, depth, tile = out.shape
+    order_full = refs[0].shape[0] * tile
     rep = place[0]
     quarter = lax.rem(rep, 4)
     for block in range(home_count):
-        mine = cols[rep, block]
+        cols = refs[block]
+        mine = cols[rep]
         tiles = []
         for step in range(5):
             if step < 4:
-                left, right = cols[lax.rem(rep + step, 8), block], mine
+                left, right = cols[lax.rem(rep + step, 8)], mine
             else:
                 start = lax.div(rep, 4) * (tile // 2)
-                left = cols[quarter + 4, block, ds(start, tile // 2, 16), :]
-                right = cols[quarter, block]
+                left = cols[quarter + 4, ds(start, tile // 2, 16), :]
+                right = cols[quarter]
             product = lax.dot_general(
                 left, right, (((1,), (1,)), ((), ())), preferred_element_type=jnp.float32
             )
             tiles.append((product * ((1.0 - DECAY) / order_full)).astype(jnp.bfloat16))
         for part, row, step, inner, size in pieces(tile, shards):
-            held[part, block, row : row + size] = tiles[step][inner : inner + size]
-    for step in range(shards):
-        outs[step][...] = held[lax.rem(place[1] + step, shards)]
-
-
-def add_kernel(table, *refs):
-    arrived, total_out, sent = refs[:-2], refs[-2], refs[-1]
-    total = sum(ref[...].astype(jnp.float32) for ref in arrived)
+            out[part, block, row : row + size] = tiles[step][inner : inner + size]
+
+
+def add_kernel(table, arrived, total_out, sent):
+    total = jnp.sum(arrived[...].astype(jnp.float32), axis=0)
     total_out[...] = total
     sent[...] = jnp.zeros_like(sent)
     for block in range(total.shape[0]):
@@ -145,27 +143,15 @@
         out[block] = (DECAY * history + gram[block] + damping).astype(jnp.bfloat16)
 
 
-def order_kernel(table, *refs):
-    arrived, out = refs[:-1], refs[-1]
-    shards = len(arrived)
-    for step in range(shards):
-        out[lax.rem(table[BLK_AT] + shards - step, shards)] = arrived[step][...]
-
-
-def choose_kernel(table, came, *outs):
-    shards = len(outs)
-    for step in range(shards):
-        holder = table[HOLDER_AT + lax.rem(table[BLK_AT] + step, shards)]
-        outs[step][...] = came[lax.div(jnp.maximum(holder, 0), 2)]
-
-
-def turn_kernel(table, *refs):
-    arrived, band, sent = refs[:-2], refs[-2], refs[-1]
-    shards = len(arrived)
-    depth, tile = arrived[0].shape
-    for step in range(shards):
-        part = lax.rem(table[BLK_AT] + shards - step, shards)
-        band[ds(part * depth, depth, 16), :] = arrived[step][...]
+def choose_kernel(table, came, out):
+    for shard in range(out.shape[0]):
+        out[shard] = came[lax.div(jnp.maximum(table[HOLDER_AT + shard], 0), 2)]
+
+
+def turn_kernel(table, parts, band, sent):
+    shards, depth, tile = parts.shape
+    for part in range(shards):
+        band[part * depth : (part + 1) * depth] = parts[part]
     sent[...] = jnp.zeros_like(sent)
     for step in range(1, 4):
         sent[lax.rem(table[REP_AT] + step, 8)] = band[step * tile : (step + 1) * tile]
@@ -220,7 +206,8 @@
     )(place, history, band, came)
 
 
-def newton_kernel(table, stat, cols, out, full):
+def newton_kernel(table, stat, *refs):
+    *cols, out, full = refs
     bands, shards, _, depth, tile = stat.shape
     order_full = bands * tile
     block = pl.program_id(0)
@@ -277,15 +264,21 @@
     update = (identity - 0.5 * product).astype(jnp.bfloat16)
     second = times_factor(update).astype(jnp.bfloat16)
     root = jnp.where(table[NEED_AT + block] >= ITERS, second, mine)
-    total = jnp.zeros(out.shape[1:], jnp.float32)
-    for band in range(bands):
-        total = total + jnp.dot(root[:, at(band)], cols[band, 0], preferred_element_type=jnp.float32)
-    out[0] = total.astype(jnp.bfloat16)
+    for index, ref in enumerate(cols):
+
+        @pl.when(block == index)
+        def _(ref=ref):
+            total = jnp.zeros(out.shape[1:], jnp.float32)
+            for band in range(bands):
+                total = total + jnp.dot(
+                    root[:, at(band)], ref[band], preferred_element_type=jnp.float32
+                )
+            out[0] = total.astype(jnp.bfloat16)
 
 
 def newton(table, stat, cols):
     bands, shards, home_count, depth, tile = stat.shape
-    width = cols.shape[3]
+    width = cols[0].shape[2]
     return pl.pallas_call(
         newton_kernel,
         out_shape=like((home_count, tile, width)),
@@ -294,13 +287,13 @@
             grid=(home_count,),
             in_specs=[
                 pl.BlockSpec((bands, shards, 1, depth, tile), lambda i, table: (0, 0, i, 0, 0)),
-                pl.BlockSpec((bands, 1, tile, width), lambda i, table: (0, i, 0, 0)),
-            ],
+            ]
+            + [pl.BlockSpec((bands, tile, width), lambda i, table: (0, 0, 0))] * len(cols),
             out_specs=pl.BlockSpec((1, tile, width), lambda i, table: (i, 0, 0)),
             scratch_shapes=[pltpu.VMEM((bands * tile, bands * tile), jnp.bfloat16)],
         ),
         compiler_params=BIG,
-    )(table, stat, cols)
+    )(table, stat, *cols)
 
 
 def exchange(array, axis):
@@ -343,40 +336,33 @@
     outgoing = (
         partial_grads[0].reshape(home_count, replicas, tile, band_cols).transpose(1, 0, 2, 3)
     )
-    history_parts = cut_history(place, history, shards, tile)
-    history_arrived = swap(history_parts, shards)
+    history_arrived = swap(cut_history(place, history, shards, tile), shards)
     partials = exchange(outgoing, "rep")
     grad_tile = jnp.sum(partials.astype(jnp.float32), axis=0).astype(jnp.bfloat16)
-    grad_cols = lax.all_gather(grad_tile, "rep", axis=0, tiled=False)
-
+    grad_cols = [lax.all_gather(grad_tile[0], "rep", axis=0, tiled=False)]
+    for block in range(1, home_count):
+        mine = after(grad_tile[block], grad_cols[-1])
+        grad_cols.append(lax.all_gather(mine, "rep", axis=0, tiled=False))
+
+    history_arrived = lax.optimization_barrier((tuple(history_arrived), grad_tile))[0]
     history_sent = call(spread_kernel, [table, *history_arrived], like((owners, depth, tile)))
-    history_came = exchange(after(history_sent, grad_tile), "own")
-
-    gram_parts = pl.pallas_call(
-        gram_kernel,
-        out_shape=[like((home_count, depth, tile))] * shards,
-        in_specs=[SCALARS, WHOLE],
-        out_specs=[WHOLE] * shards,
-        scratch_shapes=[pltpu.VMEM((shards, home_count, depth, tile), jnp.bfloat16)],
-        compiler_params=BIG,
-    )(place, grad_cols)
-    gram_arrived = swap(gram_parts, shards)
+    history_came = exchange(history_sent, "own")
+
+    gram_parts = call(gram_kernel, [place, *grad_cols], like((shards, home_count, depth, tile)))
     gram, gram_sent = call(
         add_kernel,
-        [table, *gram_arrived],
+        [table, exchange(after(gram_parts, history_came), "blk")],
         [like((home_count, depth, tile), jnp.float32), like((owners, depth, tile))],
     )
     stat = call(stat_kernel, [table, gram, history_came], like((home_count, depth, tile)))
-    stat_band = call(
-        order_kernel, [table, *swap([stat] * shards, shards)], like((shards, home_count, depth, tile))
-    )
+    gram_came = exchange(after(gram_sent, history_came), "own")
+    stat_band = lax.all_gather(stat, "blk", axis=0, tiled=False)
     stat_full = lax.all_gather(stat_band, "rep", axis=0, tiled=False)
 
-    gram_came = exchange(after(gram_sent, stat), "own")
-    slot_parts = call(choose_kernel, [table, gram_came], [like((depth, tile))] * shards)
+    slot_parts = call(choose_kernel, [table, gram_came], like((shards, depth, tile)))
     band, turned = call(
         turn_kernel,
-        [table, *swap(slot_parts, shards)],
+        [table, exchange(slot_parts, "blk")],
         [like((shards * depth, tile)), like((replicas, tile, tile))],
     )
     turned = exchange(turned, "rep")

time: 236 us -> 229 us (0.970)
  blocking collectives: 0 us -> 95.6 us
  waiting for transfers between devices: 76.8 us -> 19 us
  starting transfers between devices: 118 us -> 71.4 us
  local copies, waits for them, and re-layouts: 8.94 us -> 11.7 us
    ppermute x12 -> x3, starting transfers between devices: 75.3 us -> 15.8 us  [swap(): lax.ppermute(parts[step], 'blk', [(i, (i + step) % count) for i in range(...]
    all_gather x0 -> x3, blocking collectives: none -> 57.3 us  [the longest x1 29.5 us: body(): stat_band = lax.all_gather(stat, 'blk', axis=0, tiled=False)]
    all_to_all x0 -> x2, blocking collectives: none -> 38.3 us  [exchange(): return lax.all_to_all(array, axis, split_axis=0, concat_axis=0, tiled=True)]
    all_gather x1 -> x0, waiting for transfers between devices: 33.6 us -> none  [body(): grad_cols = lax.all_gather(grad_tile, 'rep', axis=0, tiled=False)]
    ppermute x12 -> x3, waiting for transfers between devices: 29.8 us -> 2.61 us  [swap(): lax.ppermute(parts[step], 'blk', [(i, (i + step) % count) for i in range(...]
    all_to_all x4, starting transfers between devices: 42.2 us -> 55.5 us  [exchange(): return lax.all_to_all(array, axis, split_axis=0, concat_axis=0, tiled=True)]
    all_gather x1, waiting for transfers between devices: 4.85 us -> 14.8 us  [body(): stat_full = lax.all_gather(stat_band, 'rep', axis=0, tiled=False)]
    all_to_all x4, waiting for transfers between devices: 7.88 us -> 1.63 us  [exchange(): return lax.all_to_all(array, axis, split_axis=0, concat_axis=0, tiled=True)]
  transfers between devices with their start and end apart: 18 -> 8, of which waited for: 9 -> 3; matrix products, arithmetic and copies ran while one was open for 1% -> 2% of each run, Pallas kernels for 5% -> 4%
where the time goes in v5:
time: 229 us
  blocking collectives  95.6 us (42%)
  starting transfers between devices  71.4 us (31%)
  waiting for transfers between devices  19 us (8%)
  between operations  14.9 us (7%)
  Pallas kernels  12.9 us (6%)
  local copies, waits for them, and re-layouts  11.7 us (5%)
  other arithmetic  3.07 us (1%)
    all_to_all x4, starting transfers between devices, exchange(): return lax.all_to_all(array, axis, split_axis=0, concat_axis=0, tiled=True)  55.5 us
    all_to_all x2, blocking collectives, exchange(): return lax.all_to_all(array, axis, split_axis=0, concat_axis=0, tiled=True)  38.3 us
    all_gather x1, blocking collectives, body(): stat_band = lax.all_gather(stat, 'blk', axis=0, tiled=False)  29.5 us
    ppermute x3, starting transfers between devices, swap(): lax.ppermute(parts[step], 'blk', [(i, (i + step) % count) for i in range(...  15.8 us
    all_gather x1, waiting for transfers between devices, body(): stat_full = lax.all_gather(stat_band, 'rep', axis=0, tiled=False)  14.8 us
    all_gather x1, blocking collectives, body(): grad_cols = [lax.all_gather(grad_tile[0], 'rep', axis=0, tiled=False)]  14.7 us
    all_gather x1, blocking collectives, body(): grad_cols.append(lax.all_gather(mine, 'rep', axis=0, tiled=False))  13.1 us
    unnamed x36, local copies, waits for them, and re-layouts  7.95 us
  transfers between devices with their start and end apart: 8, of which 3 were waited for; matrix products, arithmetic and copies ran while one was open for 2% of the time, Pallas kernels for 4%

profile of v5, /device:TPU:1, one launch (start us, length us, event | category | flops | bytes accessed | tf_op | source)
XLA Modules:
  0.0 228.5 jit_solution(16314247899890492243)
XLA Ops:
  7.2 2.3 copy.7
  9.4 18.4 %all-to-all-start = ((bf16[8,2,128,256]{3,2,1,0:T(8,128)(2,1)}), bf16[8,2,128,256]{3,2,1,0:T(8,128)(2,1)}, u32[]{:S(2)}, u32[]{:S(2)}) async-start(bf16[8,2,128,256]{3,2,1,0:T(8,128)(2,1)} %copy.7), calls=%async_computation | async-start | bytes 2097152 | tf_op jit(solution)/shard_map/all_to_all | solution.py:300
  27.8 0.1 pad_add_fusion.place
  27.9 0.6 shard_map.60
  28.6 1.9 collective-permute-start
  30.5 10.5 %collective-permute-start.1 = (bf16[144,128]{1,0:T(8,128)(2,1)S(1)}, bf16[144,128]{1,0:T(8,128)(2,1)S(1)}, u32[]{:S(2)}, u32[]{:S(2)}) collective-permute-start(bf16[144,128]{1,0:T(8,128)(2,1)S(1)} %get-tuple-element.20), channel_id=1, source_target_pairs={{0,2},{1,3},{2,0},{3,1},{4,6},{5,7},{6,4},{7,5},{8,10},{9,11},{10,... | collective-permute-start | bytes 110600 | tf_op jit(solution)/shard_map/ppermute | solution.py:305
  41.0 3.4 %collective-permute-start.2 = (bf16[144,128]{1,0:T(8,128)(2,1)S(1)}, bf16[144,128]{1,0:T(8,128)(2,1)S(1)}, u32[]{:S(2)}, u32[]{:S(2)}) collective-permute-start(bf16[144,128]{1,0:T(8,128)(2,1)S(1)} %get-tuple-element.21), channel_id=1, source_target_pairs={{0,3},{1,0},{2,1},{3,2},{4,7},{5,4},{6,5},{7,6},{8,11},{9,8},{10,9... | collective-permute-start | bytes 110600 | tf_op jit(solution)/shard_map/ppermute | solution.py:305
  44.4 0.2 select_reduce_fusion
  44.6 0.1 select_reduce_fusion.1
  44.7 0.1 dynamic_slice.10
  44.8 0.1 dynamic_slice.11
  44.9 0.1 concatenate.4.table
  45.0 0.0 all-to-all-done
  45.0 2.1 reduce_sum.32
  47.0 0.0 collective-permute-done.refs_1_
  47.0 2.6 %collective-permute-done.2.refs_3_ = bf16[144,128]{1,0:T(8,128)(2,1)S(1)} collective-permute-done((bf16[144,128]{1,0:T(8,128)(2,1)S(1)}, bf16[144,128]{1,0:T(8,128)(2,1)S(1)}, u32[]{:S(2)}, u32[]{:S(2)}) %collective-permute-start.2) | collective-permute-done | bytes 36896 | tf_op jit(solution)/shard_map/ppermute | solution.py:305
  49.7 0.8 shard_map.61
  50.4 1.0 copy-done.1
  51.5 11.2 %all-to-all-start.1 = ((bf16[32,144,128]{2,1,0:T(8,128)(2,1)}), bf16[32,144,128]{2,1,0:T(8,128)(2,1)S(1)}, u32[]{:S(2)}, u32[]{:S(2)}) async-start(bf16[32,144,128]{2,1,0:T(8,128)(2,1)} %copy-done.1), calls=%async_computation.1 | async-start | bytes 2359296 | tf_op jit(solution)/shard_map/all_to_all | solution.py:300
  62.7 14.7 %all_gather.21.refs_0_ = bf16[8,128,256]{2,1,0:T(8,128)(2,1)S(1)} all-gather(bf16[1,128,256]{2,1,0:T(8,128)(2,1)S(1)} %get-tuple-element.33), channel_id=1, replica_groups=mesh['rep'=8,'own'=32,'blk'=4] {'rep'}, dimensions={0}, use_global_device_ids=true | all-gather | bytes 589824 | tf_op jit(solution)/shard_map/all_gather | solution.py:342
  77.3 13.1 %all-gather = bf16[1024,256]{1,0:T(8,128)(2,1)S(1)} all-gather(bf16[128,256]{1,0:T(8,128)(2,1)S(1)} %get-tuple-element.17), channel_id=2, replica_groups=mesh['rep'=8,'own'=32,'blk'=4] {'rep'}, dimensions={0}, use_global_device_ids=true | all-gather | bytes 589824 | tf_op jit(solution)/shard_map/all_gather | solution.py:345
  90.4 0.9 shard_map.59
  91.3 0.8 copy-done.4
  92.1 0.7 copy-done.7
  92.8 21.9 %all_to_all.30.arrived = bf16[4,2,144,128]{3,2,1,0:T(8,128)(2,1)S(1)} all-to-all(bf16[4,2,144,128]{3,2,1,0:T(8,128)(2,1)} %copy-done.7), channel_id=1, replica_groups=mesh['rep'=8,'own'=32,'blk'=4] {'blk'}, dimensions={0} | all-to-all | bytes 589824 | tf_op jit(solution)/shard_map/all_to_all | solution.py:300
  114.7 0.7 shard_map.62
  115.5 1.0 copy-done.8
  116.5 15.8 %all-to-all-start.3 = ((bf16[32,144,128]{2,1,0:T(8,128)(2,1)}), bf16[32,144,128]{2,1,0:T(8,128)(2,1)}, u32[]{:S(2)}, u32[]{:S(2)}) async-start(bf16[32,144,128]{2,1,0:T(8,128)(2,1)} %copy-done.8), calls=%async_computation.3 | async-start | bytes 2359296 | tf_op jit(solution)/shard_map/all_to_all | solution.py:300
  132.3 0.0 all-gather.5.cloned.1.call-start
  132.4 0.6 shard_map.63
  133.0 29.5 %all-gather.1 = bf16[8,144,128]{2,1,0:T(8,128)(2,1)} all-gather(bf16[2,144,128]{2,1,0:T(8,128)(2,1)S(1)} %shard_map.63), channel_id=3, replica_groups=mesh['rep'=8,'own'=32,'blk'=4] {'blk'}, dimensions={0}, use_global_device_ids=true | all-gather | bytes 368640 | tf_op jit(solution)/shard_map/all_gather | solution.py:359
  162.5 0.0 all-gather.5.cloned.1.call-update
  162.5 1.6 all-to-all-done.3.came
  164.1 1.3 shard_map.65
  165.4 16.4 %all_to_all.31.parts = bf16[4,144,128]{2,1,0:T(8,128)(2,1)S(1)} all-to-all(bf16[4,144,128]{2,1,0:T(8,128)(2,1)S(1)} %shard_map.65), channel_id=1, replica_groups=mesh['rep'=8,'own'=32,'blk'=4] {'blk'}, dimensions={0} | all-to-all | bytes 294912 | tf_op jit(solution)/shard_map/all_to_all | solution.py:300
  181.8 0.7 copy-done.11
  182.5 0.6 shard_map.66
  183.1 0.0 copy-start.9
  183.1 0.7 copy-done.9
  183.8 10.1 %all-to-all-start.5 = ((bf16[8,128,128]{2,1,0:T(8,128)(2,1)}), bf16[8,128,128]{2,1,0:T(8,128)(2,1)S(1)}, u32[]{:S(2)}, u32[]{:S(2)}) async-start(bf16[8,128,128]{2,1,0:T(8,128)(2,1)} %copy-done.9), calls=%async_computation.5 | async-start | bytes 524288 | tf_op jit(solution)/shard_map/all_to_all | solution.py:300
  193.9 1.2 dynamic_slice.12
  195.8 0.6 pad_add_fusion.1.place
  196.5 14.8 %all-gather.5.cloned.1.call-done = bf16[32,2,144,128]{3,2,1,0:T(8,128)(2,1)} async-done(((bf16[4,2,144,128]{3,2,1,0:T(8,128)(2,1)}), bf16[32,2,144,128]{3,2,1,0:T(8,128)(2,1)}) %all-gather.5.cloned.1.call-update) | async-done | bytes 2359312 | tf_op jit(solution)/shard_map/all_gather | solution.py:360
  211.3 1.7 copy-done.6
  212.9 0.7 copy-done.12
  213.6 6.0 %shard_map.64 = bf16[2,128,256]{2,1,0:T(8,128)(2,1)} custom-call(s32[10]{0:T(128)S(1)} %copy-done.12, bf16[8,4,2,144,128]{4,3,2,1,0:T(8,128)(2,1)S(1)} %bitcast.17, bf16[8,128,256]{2,1,0:T(8,128)(2,1)S(1)} %copy-done.3, bf16[8,128,256]{2,1,0:T(8,128)(2,1)S(1)} %bitcast.16), custom_call_target="tpu_custom_call" | custom-call | tf_op jit(solution)/shard_map/pallas_call | solution.py:282
  219.6 0.6 copy-done.13
  220.3 1.4 shard_map.67
  (33 shorter events, 0.1 us)
Async XLA Ops:
  9.4 18.5 %copy-start = (bf16[1,1,1024,1024]{3,2,1,0:T(8,128)(2,1)S(1)}, bf16[1,1,1024,1024]{3,2,1,0:T(8,128)(2,1)}, u32[]{:S(2)}) copy-start(bf16[1,1,1024,1024]{3,2,1,0:T(8,128)(2,1)} %param.7) | copy-start | bytes 6291460
  9.4 35.5 %all-to-all-start = ((bf16[8,2,128,256]{3,2,1,0:T(8,128)(2,1)}), bf16[8,2,128,256]{3,2,1,0:T(8,128)(2,1)}, u32[]{:S(2)}, u32[]{:S(2)}) async-start(bf16[8,2,128,256]{3,2,1,0:T(8,128)(2,1)} %copy.7), calls=%async_computation | async-start | bytes 2097152 | tf_op jit(solution)/shard_map/all_to_all | solution.py:300
  27.9 16.5 %copy-start.16 = (s32[64]{0:T(128)S(1)}, s32[64]{0:T(128)}, u32[]{:S(2)}) copy-start(s32[64]{0:T(128)} %param.5) | copy-start | bytes 772
  27.9 16.9 %copy-start.17 = (s32[64]{0:T(128)S(1)}, s32[64]{0:T(128)}, u32[]{:S(2)}) copy-start(s32[64]{0:T(128)} %param.6) | copy-start | bytes 772
  28.6 18.5 %collective-permute-start = (bf16[144,128]{1,0:T(8,128)(2,1)S(1)}, bf16[144,128]{1,0:T(8,128)(2,1)S(1)}, u32[]{:S(2)}, u32[]{:S(2)}) collective-permute-start(bf16[144,128]{1,0:T(8,128)(2,1)S(1)} %get-tuple-element.19), channel_id=1, source_target_pairs={{0,1},{1,2},{2,3},{3,0},{4,5},{5,6},{6,7},{7,4},{8,9},{9,10},{10,1... | collective-permute-start | bytes 110600 | tf_op jit(solution)/shard_map/ppermute | solution.py:305
  30.5 16.6 %collective-permute-start.1 = (bf16[144,128]{1,0:T(8,128)(2,1)S(1)}, bf16[144,128]{1,0:T(8,128)(2,1)S(1)}, u32[]{:S(2)}, u32[]{:S(2)}) collective-permute-start(bf16[144,128]{1,0:T(8,128)(2,1)S(1)} %get-tuple-element.20), channel_id=1, source_target_pairs={{0,2},{1,3},{2,0},{3,1},{4,6},{5,7},{6,4},{7,5},{8,10},{9,11},{10,... | collective-permute-start | bytes 110600 | tf_op jit(solution)/shard_map/ppermute | solution.py:305
  41.0 8.6 %collective-permute-start.2 = (bf16[144,128]{1,0:T(8,128)(2,1)S(1)}, bf16[144,128]{1,0:T(8,128)(2,1)S(1)}, u32[]{:S(2)}, u32[]{:S(2)}) collective-permute-start(bf16[144,128]{1,0:T(8,128)(2,1)S(1)} %get-tuple-element.21), channel_id=1, source_target_pairs={{0,3},{1,0},{2,1},{3,2},{4,7},{5,4},{6,5},{7,6},{8,11},{9,8},{10,9... | collective-permute-start | bytes 110600 | tf_op jit(solution)/shard_map/ppermute | solution.py:305
  44.7 4.9 %copy-start.15 = (s32[4]{0:T(128)}, s32[4]{0:T(128)S(1)}, u32[]{:S(2)}) copy-start(s32[4]{0:T(128)S(1)} %broadcast_add_fusion) | copy-start | bytes 52
  45.0 119.2 %copy-start.10 = (s32[10]{0:T(128)}, s32[10]{0:T(128)S(1)}, u32[]{:S(2)}) copy-start(s32[10]{0:T(128)S(1)} %concatenate.4.table) | copy-start | bytes 124
  50.4 1.0 copy-start.1
  51.5 11.2 %copy-start.14 = (bf16[2,128,256]{2,1,0:T(8,128)(2,1)S(1)}, bf16[2,128,256]{2,1,0:T(8,128)(2,1)}, u32[]{:S(2)}) copy-start(bf16[2,128,256]{2,1,0:T(8,128)(2,1)} %reduce_sum.32) | copy-start | bytes 393220
  51.5 41.4 %all-to-all-start.1 = ((bf16[32,144,128]{2,1,0:T(8,128)(2,1)}), bf16[32,144,128]{2,1,0:T(8,128)(2,1)S(1)}, u32[]{:S(2)}, u32[]{:S(2)}) async-start(bf16[32,144,128]{2,1,0:T(8,128)(2,1)} %copy-done.1), calls=%async_computation.1 | async-start | bytes 2359296 | tf_op jit(solution)/shard_map/all_to_all | solution.py:300
  77.3 13.1 %copy-start.2 = (bf16[8,128,256]{2,1,0:T(8,128)(2,1)}, bf16[8,128,256]{2,1,0:T(8,128)(2,1)S(1)}, u32[]{:S(2)}) copy-start(bf16[8,128,256]{2,1,0:T(8,128)(2,1)S(1)} %all_gather.21.refs_0_) | copy-start | bytes 1572868
  91.3 0.8 copy-start.4
  92.1 0.7 copy-start.7
  115.5 1.0 copy-start.8
  116.5 47.6 %all-to-all-start.3 = ((bf16[32,144,128]{2,1,0:T(8,128)(2,1)}), bf16[32,144,128]{2,1,0:T(8,128)(2,1)}, u32[]{:S(2)}, u32[]{:S(2)}) async-start(bf16[32,144,128]{2,1,0:T(8,128)(2,1)} %copy-done.8), calls=%async_computation.3 | async-start | bytes 2359296 | tf_op jit(solution)/shard_map/all_to_all | solution.py:300
  132.3 78.9 %all-gather.5.cloned.1.call-start = ((), (), s32[]{:S(2)}) async-start(), calls=%async_computation.6 | async-start | bytes 2654208 | tf_op jit(solution)/shard_map/all_gather | solution.py:360
  162.5 48.8 %copy-start.3 = (bf16[8,128,256]{2,1,0:T(8,128)(2,1)S(1)}, bf16[8,128,256]{2,1,0:T(8,128)(2,1)}, u32[]{:S(2)}) copy-start(bf16[8,128,256]{2,1,0:T(8,128)(2,1)} %copy-done.2) | copy-start | bytes 1572868
  162.5 48.7 %copy-start.5 = (bf16[1024,256]{1,0:T(8,128)(2,1)S(1)}, bf16[1024,256]{1,0:T(8,128)(2,1)}, u32[]{:S(2)}) copy-start(bf16[1024,256]{1,0:T(8,128)(2,1)} %copy-done.4) | copy-start | bytes 1572868
  181.8 0.7 copy-start.11
  183.1 0.7 copy-start.9
  183.8 35.8 %all-to-all-start.5 = ((bf16[8,128,128]{2,1,0:T(8,128)(2,1)}), bf16[8,128,128]{2,1,0:T(8,128)(2,1)S(1)}, u32[]{:S(2)}, u32[]{:S(2)}) async-start(bf16[8,128,128]{2,1,0:T(8,128)(2,1)} %copy-done.9), calls=%async_computation.5 | async-start | bytes 524288 | tf_op jit(solution)/shard_map/all_to_all | solution.py:300
  211.3 1.7 copy-start.6
  212.9 0.7 copy-start.12
  219.6 0.6 copy-start.13
Sparse Core Ops, SparseCore 0:
  162.6 48.5 all-gather.4

commit v6 on v4

v6 whole, which is shorter than its diff:
```python
import math

import jax
import jax.numpy as jnp
from jax import lax
from jax.experimental import pallas as pl
from jax.experimental.pallas import tpu as pltpu
from jax.sharding import Mesh, PartitionSpec as P

ITERS = 2


DECAY = 0.5
DAMPING = 0.05

REP = ("x", "core")
OWN = ("zl", "y")
BLK = "zh"
RING = ("zl", "zh")

BIG = pltpu.CompilerParams(vmem_limit_bytes=40 * 1024 * 1024)
SCALARS = pl.BlockSpec(memory_space=pltpu.SMEM)
WHOLE = pl.BlockSpec(memory_space=pltpu.VMEM)

BANDS, STEPS = 8, 5
REP_AT, BLK_AT, TURN_AT, NEED_AT, LEVEL_AT, HAS_AT, HISTORY_AT, GRAM_AT = 0, 1, 2, 4, 6, 7, 8, 24


def ds(start, size, unit):
    return pl.ds(pl.multiple_of(start, unit), size)


def like(shape, dtype=jnp.bfloat16):
    return jax.ShapeDtypeStruct(shape, dtype)


def call(kernel, ins, outs, in_specs=None, scratch=()):
    many = isinstance(outs, (list, tuple))
    return pl.pallas_call(
        kernel,
        out_shape=outs,
        in_specs=in_specs or [SCALARS] + [WHOLE] * (len(ins) - 1),
        out_specs=[WHOLE] * len(outs) if many else WHOLE,
        scratch_shapes=list(scratch),
        compiler_params=BIG,
    )(*ins)


def fan_kernel(table, grads, *outs):
    rows = outs[0].shape[1]
    for step, out in enumerate(outs):
        start = lax.rem(table[REP_AT] + step, BANDS) * rows
        for block in range(out.shape[0]):
            out[block] = grads[block, ds(start, rows, rows), :]


def sum_kernel(table, *refs):
    *ins, out = refs
    total = ins[0][...].astype(jnp.float32)
    for ref in ins[1:]:
        total = total + ref[...].astype(jnp.float32)
    out[...] = total.astype(jnp.bfloat16)


def history_kernel(table, column, out):
    tile = column.shape[1]
    shards = 4
    size = tile // shards
    for step in range(STEPS):
        start = lax.rem(table[REP_AT] + step, BANDS) * tile
        for shard in range(shards):
            piece = column[ds(start + shard * size, size, size), :]
            for level in range(out.shape[0] // shards):
                out[level * shards + shard, step * size : (step + 1) * size] = piece


def cut_history(table, history, places, tile, shards):
    order_full = history.shape[0]
    shape = (places, STEPS * tile // shards, tile)
    return pl.pallas_call(
        history_kernel,
        out_shape=like(shape),
        grid_spec=pltpu.PrefetchScalarGridSpec(
            num_scalar_prefetch=1,
            grid=(1,),
            in_specs=[pl.BlockSpec((order_full, tile), lambda i, table: (0, table[REP_AT]))],
            out_specs=pl.BlockSpec(shape, lambda i, table: (0, 0, 0)),
        ),
        compiler_params=BIG,
    )(table, history)


def take(table, tiles, first):
    def kernel(table, tiles, out):
        for place in range(out.shape[0]):
            out[place] = tiles[table[first + place]]

    return call(kernel, [table, tiles], like(tiles.shape))


def gram_kernel(table, band, *refs):
    *slices, out, sent = refs
    shards, home_count, tile, _ = band.shape
    size = tile // shards
    order_full = BANDS * tile
    start = table[BLK_AT] * size
    for block in range(home_count):
        total = jnp.zeros((STEPS * size, tile), jnp.float32)
        for shard in range(shards):
            left = [band[shard, block, ds(start, size, size), :]]
            left += [ref[shard, block] for ref in slices]
            total = total + lax.dot_general(
                jnp.concatenate(left, axis=0),
                band[shard, block],
                (((1,), (1,)), ((), ())),
                preferred_element_type=jnp.float32,
            )
        total = total * ((1.0 - DECAY) / order_full)
        out[block] = total
        for turn in range(sent.shape[0]):
            sent[turn, block] = total.astype(jnp.bfloat16)


def stat_kernel(table, gram, came, out):
    home_count, depth, tile = out.shape
    size = depth // STEPS
    row_ids = lax.broadcasted_iota(jnp.int32, (depth, tile), 0)
    col_ids = lax.broadcasted_iota(jnp.int32, (depth, tile), 1)
    on = (row_ids < size) & (row_ids + table[BLK_AT] * size == col_ids)
    damping = jnp.where(on, DAMPING, 0.0)
    for block in range(home_count):
        history = came[table[TURN_AT + block], block].astype(jnp.float32)
        out[block] = (DECAY * history + gram[block] + damping).astype(jnp.bfloat16)


def turn_kernel(table, came, band, sent):
    tile = sent.shape[1]
    size = came.shape[1] // STEPS
    shards = tile // size
    for shard in range(shards):
        part = came[table[LEVEL_AT] * shards + shard]
        for step in range(STEPS):
            start = step * tile + shard * size
            band[start : start + size] = part[step * size : (step + 1) * size]
    sent[...] = jnp.zeros_like(sent)
    for step in range(1, STEPS):
        sent[lax.rem(table[REP_AT] + step, BANDS)] = band[step * tile : (step + 1) * tile]


def finish_kernel(table, rows, band, came, out):
    tile = rows.shape[0]
    rep = table[REP_AT]

    def put(column, gram, damping=None):
        columns = ds(column * tile, tile, tile)
        history = rows[:, columns].astype(jnp.float32)
        fresh = DECAY * history + gram
        if damping is not None:
            fresh = fresh + damping
        out[:, columns] = jnp.where(table[HAS_AT] > 0, fresh, history).astype(jnp.bfloat16)

    row_ids = lax.broadcasted_iota(jnp.int32, (tile, tile), 0)
    col_ids = lax.broadcasted_iota(jnp.int32, (tile, tile), 1)
    put(rep, band[:tile].astype(jnp.float32), jnp.where(row_ids == col_ids, DAMPING, 0.0))
    for step in range(1, STEPS):
        other = lax.rem(rep + BANDS - step, BANDS)
        put(other, came[other].astype(jnp.float32))
        if step < STEPS - 1:
            mine = band[step * tile : (step + 1) * tile].astype(jnp.float32)
            put(lax.rem(rep + step, BANDS), mine.T)


def finish(table, history, band, came):
    tile, order_full = band.shape[1], history.shape[1]
    return pl.pallas_call(
        finish_kernel,
        out_shape=like((tile, order_full)),
        grid_spec=pltpu.PrefetchScalarGridSpec(
            num_scalar_prefetch=1,
            grid=(1,),
            in_specs=[
                pl.BlockSpec((tile, order_full), lambda i, table: (table[REP_AT], 0)),
                pl.BlockSpec(band.shape, lambda i, table: (0, 0)),
                pl.BlockSpec(came.shape, lambda i, table: (0, 0, 0)),
            ],
            out_specs=pl.BlockSpec((tile, order_full), lambda i, table: (0, 0)),
        ),
        compiler_params=BIG,
    )(table, history, band, came)


def newton_kernel(table, stat, cols, out, full):
    bands, shards, _, depth, tile = stat.shape
    size = depth // STEPS
    order_full = bands * tile
    block = pl.program_id(0)
    squares = jnp.zeros((8, tile), jnp.float32)
    for band in range(bands):
        for shard in range(shards):
            part = stat[band, shard, 0].astype(jnp.float32)
            part = (part * part).reshape(-1, 8, tile)
            ends, middle = size // 8, (STEPS - 1) * size // 8
            squares = squares + jnp.sum(part, axis=0) + jnp.sum(part[ends:middle], axis=0)
    frobenius = jnp.sqrt(jnp.sum(squares, keepdims=True)[:1, :1])
    norm_scale = math.sqrt(order_full) / (2.0 * frobenius)

    def at(index):
        return slice(index * tile, (index + 1) * tile)

    for band in range(bands):
        for shard in range(shards):
            part = (stat[band, shard, 0].astype(jnp.float32) * norm_scale).astype(jnp.bfloat16)
            for step in range(STEPS):
                start = (band + step) % bands * tile + shard * size
                full[start : start + size, at(band)] = part[step * size : (step + 1) * size]
    for band in range(bands):
        for step in range(1, STEPS - 1):
            other = (band + step) % bands
            full[at(band), at(other)] = full[at(other), at(band)].T

    row_ids = lax.broadcasted_iota(jnp.int32, (tile, tile), 0)
    col_ids = lax.broadcasted_iota(jnp.int32, (tile, tile), 1)
    diagonals = []
    for band in range(bands):
        corner = full[at(band), at(band)].astype(jnp.float32)
        values = jnp.sum(jnp.where(row_ids == col_ids, corner, 0.0), axis=0, keepdims=True)
        rounded = (1.5 - 0.5 * values).astype(jnp.bfloat16).astype(jnp.float32)
        diagonals.append(rounded + 0.5 * values)
    diagonal = jnp.concatenate(diagonals, axis=1)

    def times_scaled(left):
        return jnp.dot(left, full[...], preferred_element_type=jnp.float32)

    def times_factor(left):
        return left.astype(jnp.float32) * diagonal - 0.5 * times_scaled(left)

    first = table[REP_AT] * tile
    wide_rows = lax.broadcasted_iota(jnp.int32, (tile, order_full), 0) + first
    wide_cols = lax.broadcasted_iota(jnp.int32, (tile, order_full), 1)
    identity = jnp.where(wide_rows == wide_cols, 1.5, 0.0)
    mine = full[ds(first, tile, tile), :].astype(jnp.float32)
    mine = (identity - 0.5 * mine).astype(jnp.bfloat16)
    product = times_factor(times_scaled(mine).astype(jnp.bfloat16))
    update = (identity - 0.5 * product).astype(jnp.bfloat16)
    second = times_factor(update).astype(jnp.bfloat16)
    root = jnp.where(table[NEED_AT + block] >= ITERS, second, mine)
    total = jnp.zeros(out.shape[1:], jnp.float32)
    for band in range(bands):
        total = total + jnp.dot(root[:, at(band)], cols[band, 0], preferred_element_type=jnp.float32)
    out[0] = total.astype(jnp.bfloat16)


def newton(table, stat, cols):
    bands, shards, home_count, depth, tile = stat.shape
    width = cols.shape[3]
    return pl.pallas_call(
        newton_kernel,
        out_shape=like((home_count, tile, width)),
        grid_spec=pltpu.PrefetchScalarGridSpec(
            num_scalar_prefetch=1,
            grid=(home_count,),
            in_specs=[
                pl.BlockSpec((bands, shards, 1, depth, tile), lambda i, table: (0, 0, i, 0, 0)),
                pl.BlockSpec((bands, 1, tile, width), lambda i, table: (0, i, 0, 0)),
            ],
            out_specs=pl.BlockSpec((1, tile, width), lambda i, table: (i, 0, 0)),
            scratch_shapes=[pltpu.VMEM((bands * tile, bands * tile), jnp.bfloat16)],
        ),
        compiler_params=BIG,
    )(table, stat, cols)


def exchange(array, axis):
    return lax.all_to_all(array, axis, split_axis=0, concat_axis=0, tiled=True)


def shift(array, step):
    return lax.ppermute(array, REP, [(i, (i + step) % BANDS) for i in range(BANDS)])


def after(array, other):
    return lax.optimization_barrier((array, other))[0]


def tables(owner_map, iterations, home_count):
    levels, turns, shards = lax.axis_size("zl"), lax.axis_size("y"), lax.axis_size(BLK)
    my_level, my_turn, my_blk = lax.axis_index("zl"), lax.axis_index("y"), lax.axis_index(BLK)
    my_own = lax.axis_index(OWN)
    total_blocks = owner_map.shape[0]
    column = turns * home_count
    position = jnp.arange(total_blocks, dtype=jnp.int32)
    same = owner_map[:, None] == owner_map[None, :]
    slot = jnp.sum(jnp.where(same & (position[None, :] < position[:, None]), 1, 0), axis=1)
    place_ids = jnp.arange(levels * turns * shards, dtype=jnp.int32)
    lands = (owner_map * shards + slot)[None, :] == place_ids[:, None]
    holder = jnp.sum(jnp.where(lands, position[None, :] + 1, 0), axis=1) - 1
    holder = holder.reshape(levels, turns, shards)
    mine = holder[my_level, my_turn, my_blk]
    from_ring = (owner_map // turns) * shards + slot
    cut = lax.dynamic_slice_in_dim
    return jnp.concatenate(
        [
            jnp.stack([lax.axis_index(REP), my_blk]),
            cut(owner_map, my_own * home_count, home_count) % turns,
            cut(iterations, my_own * home_count, home_count),
            jnp.stack([jnp.maximum(mine, 0) // column, jnp.where(mine >= 0, 1, 0)]),
            cut(from_ring, my_level * column, column),
            (jnp.maximum(holder, 0) % column)[:, my_turn].reshape(-1),
        ]
    ).astype(jnp.int32)


def body(partial_grads, owner_map, iterations, slot_history):
    turns, shards = lax.axis_size("y"), lax.axis_size(BLK)
    ring = lax.axis_size("zl") * shards
    my_blk = lax.axis_index(BLK)
    _, home_count, order_full, width = partial_grads.shape
    tile = order_full // BANDS
    size = tile // shards
    depth = STEPS * size
    history = slot_history[0, 0]
    table = tables(owner_map, iterations, home_count)
    place = jnp.stack([lax.axis_index(REP), my_blk]).astype(jnp.int32)

    history_ring = exchange(cut_history(place, history, ring, tile, shards), RING)

    partials = call(
        fan_kernel, [place, partial_grads[0]], [like((home_count, tile, width))] * BANDS
    )
    partials = [partials[0]] + [shift(partials[step], step) for step in range(1, BANDS)]
    grad_tile = call(sum_kernel, [place, *partials], like((home_count, tile, width)))
    grad_cols = lax.all_gather(grad_tile, REP, axis=0, tiled=False)

    history_sent = take(table, history_ring, HISTORY_AT)
    history_sent = history_sent.reshape(turns, home_count, depth, tile)
    history_came = exchange(history_sent, "y")

    grad_band = lax.all_gather(grad_tile, BLK, axis=0, tiled=False)
    mine = lax.dynamic_slice_in_dim(grad_band, my_blk * size, size, 2)
    slices = [shift(mine, -step) for step in range(1, STEPS)]
    gram, gram_sent = call(
        gram_kernel,
        [place, grad_band, *slices],
        [like((home_count, depth, tile), jnp.float32), like((turns, home_count, depth, tile))],
    )
    gram_came = exchange(after(gram_sent, history_came), "y")
    stat = call(stat_kernel, [table, gram, history_came], like((home_count, depth, tile)))
    stat_band = lax.all_gather(stat, BLK, axis=0, tiled=False)
    stat_full = lax.all_gather(stat_band, REP, axis=0, tiled=False)

    gram_sent = take(table, gram_came.reshape(ring, depth, tile), GRAM_AT)
    gram_slot = exchange(gram_sent, RING)
    band, turned = call(
        turn_kernel, [table, gram_slot], [like((STEPS * tile, tile)), like((BANDS, tile, tile))]
    )
    new_rows = finish(table, history, band, exchange(turned, REP))

    directions = newton(table, stat_full, grad_cols)
    return (directions, new_rows[None, None])


def solution(mesh):
    fine = Mesh(mesh.devices.reshape(4, 2, 4, 8, 4), ("x", "core", "zl", "y", "zh"))
    return jax.shard_map(
        body,
        mesh=fine,
        in_specs=(P(REP, OWN, None, BLK), P(), P(), P(OWN, BLK, None, None)),
        out_specs=(P(OWN, REP, BLK), P(OWN, BLK, REP, None)),
        check_vma=False,
    )
```

time: 284 us -> 240 us (0.85)
  blocking collectives: 50.6 us -> 136 us
  waiting for transfers between devices: 92 us -> 9.31 us
  Pallas kernels: 47.5 us -> 15.4 us
  starting transfers between devices: 66.2 us -> 57.1 us
  local copies, waits for them, and re-layouts: 9.52 us -> 5.58 us
    all_to_all x1 -> x3, blocking collectives: 18.9 us -> 80.1 us  [exchange(): return lax.all_to_all(array, axis, split_axis=0, concat_axis=0, tiled=True)]
    all_gather x2, waiting for transfers between devices: 55.4 us -> 0.01 us  [the longest x1 0.01 us: body(): grad_cols = lax.all_gather(grad_tile, REP, axis=0, tiled=False)]
    pallas_call x2 -> x0, Pallas kernels: 33.9 us -> none  [the longest x1 33 us: split_bands(): pl.pallas_call(split_kernel, out_shape=like((replicas, home_count, order_...]
    all_to_all x5 -> x2, starting transfers between devices: 52.7 us -> 26.2 us  [exchange(): return lax.all_to_all(array, axis, split_axis=0, concat_axis=0, tiled=True)]
    all_gather x1 -> x2, blocking collectives: 31.8 us -> 55.9 us  [the longest x1 32.4 us: body(): grad_band = lax.all_gather(grad_tile, BLK, axis=0, tiled=False)]
    all_to_all x5 -> x2, waiting for transfers between devices: 23.5 us -> 0.01 us  [exchange(): return lax.all_to_all(array, axis, split_axis=0, concat_axis=0, tiled=True)]
    ppermute x3 -> x11, starting transfers between devices: 13.4 us -> 30.8 us  [shift(): lax.ppermute(array, REP, [(i, (i + step) % BANDS) for i in range(BANDS)])]
    ppermute x3 -> x11, waiting for transfers between devices: 13.1 us -> 9.27 us  [shift(): lax.ppermute(array, REP, [(i, (i + step) % BANDS) for i in range(BANDS)])]
  transfers between devices with their start and end apart: 10 -> 15, of which waited for: 6 -> 4; matrix products, arithmetic and copies ran while one was open for 2% -> 1% of each run, Pallas kernels for 5% -> 3%
where the time goes in v6:
time: 240 us; the launch traced here: 239 us
  blocking collectives  136 us (57%)
  starting transfers between devices  57.1 us (24%)
  Pallas kernels  15.4 us (6%)
  between operations  15.4 us (6%)
  waiting for transfers between devices  9.31 us (4%)
  local copies, waits for them, and re-layouts  5.58 us (2%)
    all_to_all x3, blocking collectives, exchange(): return lax.all_to_all(array, axis, split_axis=0, concat_axis=0, tiled=True)  80.1 us
    all_gather x1, blocking collectives, body(): grad_band = lax.all_gather(grad_tile, BLK, axis=0, tiled=False)  32.4 us
    ppermute x11, starting transfers between devices, shift(): lax.ppermute(array, REP, [(i, (i + step) % BANDS) for i in range(BANDS)])  30.8 us
    all_to_all x2, starting transfers between devices, exchange(): return lax.all_to_all(array, axis, split_axis=0, concat_axis=0, tiled=True)  26.2 us
    all_gather x1, blocking collectives, body(): stat_band = lax.all_gather(stat, BLK, axis=0, tiled=False)  23.5 us
    ppermute x11, waiting for transfers between devices, shift(): lax.ppermute(array, REP, [(i, (i + step) % BANDS) for i in range(BANDS)])  9.27 us
    pallas_call x1, Pallas kernels, newton(): pl.pallas_call(newton_kernel, out_shape=like((home_count, tile, width)),...  6.32 us
    pallas_call x7, Pallas kernels, call(): pl.pallas_call(kernel, out_shape=outs, in_specs=in_specs or [SCALARS] + [...  6.05 us
  transfers between devices with their start and end apart: 15, of which 4 were waited for; matrix products, arithmetic and copies ran while one was open for 1% of the time, Pallas kernels for 3%

profile of v6, /device:TPU:1, one launch (start us, length us, event | category | flops | bytes accessed | tf_op | source)
XLA Modules:
  0.0 239.3 jit_solution(1652663466293611707)
XLA Ops:
  7.2 0.1 pad_add_fusion.table
  7.3 1.6 copy-done
  8.9 1.6 shard_map.62
  10.4 19.4 %all-to-all-start = ((bf16[16,160,128]{2,1,0:T(8,128)(2,1)}), bf16[16,160,128]{2,1,0:T(8,128)(2,1)S(1)}, u32[]{:S(2)}, u32[]{:S(2)}) async-start(bf16[16,160,128]{2,1,0:T(8,128)(2,1)} %shard_map.62), calls=%async_computation | async-start | bytes 1310720 | tf_op jit(solution)/shard_map/all_to_all | solution.py:274
  29.8 0.0 all-gather.9.cloned.1.call-start
  29.9 0.6 shard_map.59
  30.5 2.1 collective-permute-start
  32.6 3.1 %collective-permute-start.1 = (bf16[2,128,256]{2,1,0:T(8,128)(2,1)S(1)}, bf16[2,128,256]{2,1,0:T(8,128)(2,1)S(1)}, u32[]{:S(2)}, u32[]{:S(2)}) collective-permute-start(bf16[2,128,256]{2,1,0:T(8,128)(2,1)S(1)} %get-tuple-element.17), channel_id=1, source_target_pairs={{0,256},{128,384},{256,512},{384,640},{512,768},{640,896},{768,0},... | collective-permute-start | bytes 393224 | tf_op jit(solution)/shard_map/ppermute | solution.py:278
  35.7 3.5 %collective-permute-start.2 = (bf16[2,128,256]{2,1,0:T(8,128)(2,1)S(1)}, bf16[2,128,256]{2,1,0:T(8,128)(2,1)S(1)}, u32[]{:S(2)}, u32[]{:S(2)}) collective-permute-start(bf16[2,128,256]{2,1,0:T(8,128)(2,1)S(1)} %get-tuple-element.18), channel_id=1, source_target_pairs={{0,384},{128,512},{256,640},{384,768},{512,896},{640,0},{768,128},... | collective-permute-start | bytes 393224 | tf_op jit(solution)/shard_map/ppermute | solution.py:278
  39.2 2.4 %collective-permute-start.3 = (bf16[2,128,256]{2,1,0:T(8,128)(2,1)S(1)}, bf16[2,128,256]{2,1,0:T(8,128)(2,1)S(1)}, u32[]{:S(2)}, u32[]{:S(2)}) collective-permute-start(bf16[2,128,256]{2,1,0:T(8,128)(2,1)S(1)} %get-tuple-element.19), channel_id=1, source_target_pairs={{0,512},{128,640},{256,768},{384,896},{512,0},{640,128},{768,256},... | collective-permute-start | bytes 393224 | tf_op jit(solution)/shard_map/ppermute | solution.py:278
  41.6 3.9 %collective-permute-start.4 = (bf16[2,128,256]{2,1,0:T(8,128)(2,1)S(1)}, bf16[2,128,256]{2,1,0:T(8,128)(2,1)S(1)}, u32[]{:S(2)}, u32[]{:S(2)}) collective-permute-start(bf16[2,128,256]{2,1,0:T(8,128)(2,1)S(1)} %get-tuple-element.20), channel_id=1, source_target_pairs={{0,640},{128,768},{256,896},{384,0},{512,128},{640,256},{768,384},... | collective-permute-start | bytes 393224 | tf_op jit(solution)/shard_map/ppermute | solution.py:278
  45.5 2.6 %collective-permute-start.5 = (bf16[2,128,256]{2,1,0:T(8,128)(2,1)S(1)}, bf16[2,128,256]{2,1,0:T(8,128)(2,1)S(1)}, u32[]{:S(2)}, u32[]{:S(2)}) collective-permute-start(bf16[2,128,256]{2,1,0:T(8,128)(2,1)S(1)} %get-tuple-element.21), channel_id=1, source_target_pairs={{0,768},{128,896},{256,0},{384,128},{512,256},{640,384},{768,512},... | collective-permute-start | bytes 393224 | tf_op jit(solution)/shard_map/ppermute | solution.py:278
  48.1 1.6 collective-permute-start.6
  49.7 0.2 select_reduce_fusion.1
  50.0 1.7 collective-permute-done.5.refs_6_
  51.6 2.8 %collective-permute-done.6.refs_7_ = bf16[2,128,256]{2,1,0:T(8,128)(2,1)S(1)} collective-permute-done((bf16[2,128,256]{2,1,0:T(8,128)(2,1)S(1)}, bf16[2,128,256]{2,1,0:T(8,128)(2,1)S(1)}, u32[]{:S(2)}, u32[]{:S(2)}) %collective-permute-start.6) | collective-permute-done | bytes 131104 | tf_op jit(solution)/shard_map/ppermute | solution.py:278
  54.4 1.3 shard_map.60
  55.7 0.1 select_reduce_fusion
  55.9 0.1 sub.17
  56.0 0.6 dynamic_slice.20
  57.7 0.1 reshape_squeeze.3
  57.8 0.1 dynamic_slice.19
  57.9 0.1 dynamic_slice.21
  58.0 0.1 and_select_fusion.2
  58.0 0.1 concatenate.3.table
  58.1 1.5 shard_map.63
  59.6 6.8 %all-to-all-start.1 = ((bf16[8,2,160,128]{3,2,1,0:T(8,128)(2,1)}), bf16[8,2,160,128]{3,2,1,0:T(8,128)(2,1)S(1)}, u32[]{:S(2)}, u32[]{:S(2)}) async-start(bf16[8,2,160,128]{3,2,1,0:T(8,128)(2,1)} %bitcast.9), calls=%async_computation.1 | async-start | bytes 1310720 | tf_op jit(solution)/shard_map/all_to_all | solution.py:274
  66.4 0.0 all-gather.7.cloned.1.call-start
  66.5 32.4 %all-gather = bf16[8,128,256]{2,1,0:T(8,128)(2,1)S(1)} all-gather(bf16[2,128,256]{2,1,0:T(8,128)(2,1)} %shard_map.60), channel_id=2, replica_groups=mesh['x'=4,'core'=2,'zl'=4,'y'=8,'zh'=4] {'zh'}, dimensions={0}, use_global_device_ids=true | all-gather | bytes 655360 | tf_op jit(solution)/shard_map/all_gather | solution.py:338
  98.8 2.8 %collective-permute-start.10 = (bf16[4,2,32,256]{3,2,1,0:T(8,128)(2,1)S(1)}, bf16[4,2,32,256]{3,2,1,0:T(8,128)(2,1)S(1)}, u32[]{:S(2)}, u32[]{:S(2)}) collective-permute-start(bf16[4,2,32,256]{3,2,1,0:T(8,128)(2,1)S(1)} %constant_dynamic-slice_fusion), channel_id=1, source_target_pairs={{0,512},{128,640},{256,768},{384,896},{512,0},{640,128},{768,256},... | collective-permute-start | bytes 393224 | tf_op jit(solution)/shard_map/ppermute | solution.py:278
  101.7 2.8 %collective-permute-start.7 = (bf16[4,2,32,256]{3,2,1,0:T(8,128)(2,1)S(1)}, bf16[4,2,32,256]{3,2,1,0:T(8,128)(2,1)S(1)}, u32[]{:S(2)}, u32[]{:S(2)}) collective-permute-start(bf16[4,2,32,256]{3,2,1,0:T(8,128)(2,1)S(1)} %constant_dynamic-slice_fusion), channel_id=1, source_target_pairs={{0,896},{128,0},{256,128},{384,256},{512,384},{640,512},{768,640},... | collective-permute-start | bytes 393224 | tf_op jit(solution)/shard_map/ppermute | solution.py:278
  104.4 3.1 %collective-permute-start.8 = (bf16[4,2,32,256]{3,2,1,0:T(8,128)(2,1)S(1)}, bf16[4,2,32,256]{3,2,1,0:T(8,128)(2,1)S(1)}, u32[]{:S(2)}, u32[]{:S(2)}) collective-permute-start(bf16[4,2,32,256]{3,2,1,0:T(8,128)(2,1)S(1)} %constant_dynamic-slice_fusion), channel_id=1, source_target_pairs={{0,768},{128,896},{256,0},{384,128},{512,256},{640,384},{768,512},... | collective-permute-start | bytes 393224 | tf_op jit(solution)/shard_map/ppermute | solution.py:278
  107.6 2.9 %collective-permute-start.9 = (bf16[4,2,32,256]{3,2,1,0:T(8,128)(2,1)S(1)}, bf16[4,2,32,256]{3,2,1,0:T(8,128)(2,1)S(1)}, u32[]{:S(2)}, u32[]{:S(2)}) collective-permute-start(bf16[4,2,32,256]{3,2,1,0:T(8,128)(2,1)S(1)} %constant_dynamic-slice_fusion), channel_id=1, source_target_pairs={{0,640},{128,768},{256,896},{384,0},{512,128},{640,256},{768,384},... | collective-permute-start | bytes 393224 | tf_op jit(solution)/shard_map/ppermute | solution.py:278
  110.5 0.0 collective-permute-done.7.refs_0_
  110.6 1.3 collective-permute-done.8.refs_1_
  111.9 3.4 %collective-permute-done.9.refs_2_ = bf16[4,2,32,256]{3,2,1,0:T(8,128)(2,1)S(1)} collective-permute-done((bf16[4,2,32,256]{3,2,1,0:T(8,128)(2,1)S(1)}, bf16[4,2,32,256]{3,2,1,0:T(8,128)(2,1)S(1)}, u32[]{:S(2)}, u32[]{:S(2)}) %collective-permute-start.9) | collective-permute-done | bytes 131104 | tf_op jit(solution)/shard_map/ppermute | solution.py:278
  115.4 0.9 shard_map.61
  116.3 0.6 shard_map.64
  116.8 23.5 %all-gather.1 = bf16[8,160,128]{2,1,0:T(8,128)(2,1)} all-gather(bf16[2,160,128]{2,1,0:T(8,128)(2,1)S(1)} %shard_map.64), channel_id=3, replica_groups=mesh['x'=4,'core'=2,'zl'=4,'y'=8,'zh'=4] {'zh'}, dimensions={0}, use_global_device_ids=true | all-gather | bytes 409600 | tf_op jit(solution)/shard_map/all_gather | solution.py:348
  140.4 24.7 %all_to_all.25 = bf16[8,2,160,128]{3,2,1,0:T(8,128)(2,1)S(1)} all-to-all(bf16[8,2,160,128]{3,2,1,0:T(8,128)(2,1)S(1)} %get-tuple-element.25), channel_id=1, replica_groups=mesh['x'=4,'core'=2,'zl'=4,'y'=8,'zh'=4] {'y'}, dimensions={0} | all-to-all | bytes 1310720 | tf_op jit(solution)/shard_map/all_to_all | solution.py:274
  165.1 0.6 shard_map.66
  165.7 39.2 %all_to_all.26.came = bf16[16,160,128]{2,1,0:T(8,128)(2,1)S(1)} all-to-all(bf16[16,160,128]{2,1,0:T(8,128)(2,1)S(1)} %shard_map.66), channel_id=1, replica_groups=mesh['x'=4,'core'=2,'zl'=4,'y'=8,'zh'=4] {'zl','zh'}, dimensions={0} | all-to-all | bytes 1310720 | tf_op jit(solution)/shard_map/all_to_all | solution.py:274
  204.9 0.6 shard_map.67
  205.5 16.2 %all_to_all.27.came = bf16[8,128,128]{2,1,0:T(8,128)(2,1)S(1)} all-to-all(bf16[8,128,128]{2,1,0:T(8,128)(2,1)S(1)} %get-tuple-element.27), channel_id=1, replica_groups=mesh['x'=4,'core'=2,'zl'=4,'y'=8,'zh'=4] {'x','core'}, dimensions={0} | all-to-all | bytes 524288 | tf_op jit(solution)/shard_map/all_to_all | solution.py:274
  221.7 1.4 shard_map.68
  223.1 1.7 copy-done.2
  224.9 1.2 copy-done.4
  226.1 6.3 %shard_map.65 = bf16[2,128,256]{2,1,0:T(8,128)(2,1)} custom-call(s32[40]{0:T(128)S(1)} %concatenate.3.table, bf16[8,4,2,160,128]{4,3,2,1,0:T(8,128)(2,1)S(1)} %bitcast.20, bf16[8,2,128,256]{3,2,1,0:T(8,128)(2,1)S(1)} %bitcast.22), custom_call_target="tpu_custom_call" | custom-call | tf_op jit(solution)/shard_map/pallas_call | solution.py:256
  (27 shorter events, 0.1 us)
Async XLA Ops:
  7.2 42.6 %copy-start.5 = (s32[64]{0:T(128)S(1)}, s32[64]{0:T(128)}, u32[]{:S(2)}) copy-start(s32[64]{0:T(128)} %param.5) | copy-start | bytes 772
  7.3 1.6 copy-start
  8.8 21.0 %copy-start.3 = (bf16[1,2,1024,256]{3,2,1,0:T(8,128)(2,1)S(1)}, bf16[1,2,1024,256]{3,2,1,0:T(8,128)(2,1)}, u32[]{:S(2)}) copy-start(bf16[1,2,1024,256]{3,2,1,0:T(8,128)(2,1)} %param.4) | copy-start | bytes 3145732
  8.9 49.0 %copy-start.6 = (s32[64]{0:T(128)S(1)}, s32[64]{0:T(128)}, u32[]{:S(2)}) copy-start(s32[64]{0:T(128)} %param.6) | copy-start | bytes 772
  10.4 47.7 %all-to-all-start = ((bf16[16,160,128]{2,1,0:T(8,128)(2,1)}), bf16[16,160,128]{2,1,0:T(8,128)(2,1)S(1)}, u32[]{:S(2)}, u32[]{:S(2)}) async-start(bf16[16,160,128]{2,1,0:T(8,128)(2,1)} %shard_map.62), calls=%async_computation | async-start | bytes 1310720 | tf_op jit(solution)/shard_map/all_to_all | solution.py:274
  29.8 193.3 %all-gather.9.cloned.1.call-start = ((), (), s32[]{:S(2)}) async-start(), calls=%async_computation.6 | async-start | bytes 1179648 | tf_op jit(solution)/shard_map/all_gather | solution.py:332
  30.5 15.0 %collective-permute-start = (bf16[2,128,256]{2,1,0:T(8,128)(2,1)S(1)}, bf16[2,128,256]{2,1,0:T(8,128)(2,1)S(1)}, u32[]{:S(2)}, u32[]{:S(2)}) collective-permute-start(bf16[2,128,256]{2,1,0:T(8,128)(2,1)S(1)} %get-tuple-element.16), channel_id=1, source_target_pairs={{0,128},{128,256},{256,384},{384,512},{512,640},{640,768},{768,896... | collective-permute-start | bytes 393224 | tf_op jit(solution)/shard_map/ppermute | solution.py:278
  32.6 15.5 %collective-permute-start.1 = (bf16[2,128,256]{2,1,0:T(8,128)(2,1)S(1)}, bf16[2,128,256]{2,1,0:T(8,128)(2,1)S(1)}, u32[]{:S(2)}, u32[]{:S(2)}) collective-permute-start(bf16[2,128,256]{2,1,0:T(8,128)(2,1)S(1)} %get-tuple-element.17), channel_id=1, source_target_pairs={{0,256},{128,384},{256,512},{384,640},{512,768},{640,896},{768,0},... | collective-permute-start | bytes 393224 | tf_op jit(solution)/shard_map/ppermute | solution.py:278
  35.7 14.2 %collective-permute-start.2 = (bf16[2,128,256]{2,1,0:T(8,128)(2,1)S(1)}, bf16[2,128,256]{2,1,0:T(8,128)(2,1)S(1)}, u32[]{:S(2)}, u32[]{:S(2)}) collective-permute-start(bf16[2,128,256]{2,1,0:T(8,128)(2,1)S(1)} %get-tuple-element.18), channel_id=1, source_target_pairs={{0,384},{128,512},{256,640},{384,768},{512,896},{640,0},{768,128},... | collective-permute-start | bytes 393224 | tf_op jit(solution)/shard_map/ppermute | solution.py:278
  39.2 10.8 %collective-permute-start.3 = (bf16[2,128,256]{2,1,0:T(8,128)(2,1)S(1)}, bf16[2,128,256]{2,1,0:T(8,128)(2,1)S(1)}, u32[]{:S(2)}, u32[]{:S(2)}) collective-permute-start(bf16[2,128,256]{2,1,0:T(8,128)(2,1)S(1)} %get-tuple-element.19), channel_id=1, source_target_pairs={{0,512},{128,640},{256,768},{384,896},{512,0},{640,128},{768,256},... | collective-permute-start | bytes 393224 | tf_op jit(solution)/shard_map/ppermute | solution.py:278
  41.6 8.3 %collective-permute-start.4 = (bf16[2,128,256]{2,1,0:T(8,128)(2,1)S(1)}, bf16[2,128,256]{2,1,0:T(8,128)(2,1)S(1)}, u32[]{:S(2)}, u32[]{:S(2)}) collective-permute-start(bf16[2,128,256]{2,1,0:T(8,128)(2,1)S(1)} %get-tuple-element.20), channel_id=1, source_target_pairs={{0,640},{128,768},{256,896},{384,0},{512,128},{640,256},{768,384},... | collective-permute-start | bytes 393224 | tf_op jit(solution)/shard_map/ppermute | solution.py:278
  45.5 6.1 %collective-permute-start.5 = (bf16[2,128,256]{2,1,0:T(8,128)(2,1)S(1)}, bf16[2,128,256]{2,1,0:T(8,128)(2,1)S(1)}, u32[]{:S(2)}, u32[]{:S(2)}) collective-permute-start(bf16[2,128,256]{2,1,0:T(8,128)(2,1)S(1)} %get-tuple-element.21), channel_id=1, source_target_pairs={{0,768},{128,896},{256,0},{384,128},{512,256},{640,384},{768,512},... | collective-permute-start | bytes 393224 | tf_op jit(solution)/shard_map/ppermute | solution.py:278
  48.1 6.2 %collective-permute-start.6 = (bf16[2,128,256]{2,1,0:T(8,128)(2,1)S(1)}, bf16[2,128,256]{2,1,0:T(8,128)(2,1)S(1)}, u32[]{:S(2)}, u32[]{:S(2)}) collective-permute-start(bf16[2,128,256]{2,1,0:T(8,128)(2,1)S(1)} %get-tuple-element.22), channel_id=1, source_target_pairs={{0,896},{128,0},{256,128},{384,256},{512,384},{640,512},{768,640},... | collective-permute-start | bytes 393224 | tf_op jit(solution)/shard_map/ppermute | solution.py:278
  59.6 56.7 %all-to-all-start.1 = ((bf16[8,2,160,128]{3,2,1,0:T(8,128)(2,1)}), bf16[8,2,160,128]{3,2,1,0:T(8,128)(2,1)S(1)}, u32[]{:S(2)}, u32[]{:S(2)}) async-start(bf16[8,2,160,128]{3,2,1,0:T(8,128)(2,1)} %bitcast.9), calls=%async_computation.1 | async-start | bytes 1310720 | tf_op jit(solution)/shard_map/all_to_all | solution.py:274
  66.4 156.7 %all-gather.7.cloned.1.call-start = ((), (), s32[]{:S(2)}) async-start(), calls=%async_computation.5 | async-start | bytes 2949120 | tf_op jit(solution)/shard_map/all_gather | solution.py:349
  98.8 11.7 %collective-permute-start.10 = (bf16[4,2,32,256]{3,2,1,0:T(8,128)(2,1)S(1)}, bf16[4,2,32,256]{3,2,1,0:T(8,128)(2,1)S(1)}, u32[]{:S(2)}, u32[]{:S(2)}) collective-permute-start(bf16[4,2,32,256]{3,2,1,0:T(8,128)(2,1)S(1)} %constant_dynamic-slice_fusion), channel_id=1, source_target_pairs={{0,512},{128,640},{256,768},{384,896},{512,0},{640,128},{768,256},... | collective-permute-start | bytes 393224 | tf_op jit(solution)/shard_map/ppermute | solution.py:278
  101.7 8.9 %collective-permute-start.7 = (bf16[4,2,32,256]{3,2,1,0:T(8,128)(2,1)S(1)}, bf16[4,2,32,256]{3,2,1,0:T(8,128)(2,1)S(1)}, u32[]{:S(2)}, u32[]{:S(2)}) collective-permute-start(bf16[4,2,32,256]{3,2,1,0:T(8,128)(2,1)S(1)} %constant_dynamic-slice_fusion), channel_id=1, source_target_pairs={{0,896},{128,0},{256,128},{384,256},{512,384},{640,512},{768,640},... | collective-permute-start | bytes 393224 | tf_op jit(solution)/shard_map/ppermute | solution.py:278
  104.4 7.5 %collective-permute-start.8 = (bf16[4,2,32,256]{3,2,1,0:T(8,128)(2,1)S(1)}, bf16[4,2,32,256]{3,2,1,0:T(8,128)(2,1)S(1)}, u32[]{:S(2)}, u32[]{:S(2)}) collective-permute-start(bf16[4,2,32,256]{3,2,1,0:T(8,128)(2,1)S(1)} %constant_dynamic-slice_fusion), channel_id=1, source_target_pairs={{0,768},{128,896},{256,0},{384,128},{512,256},{640,384},{768,512},... | collective-permute-start | bytes 393224 | tf_op jit(solution)/shard_map/ppermute | solution.py:278
  107.6 7.8 %collective-permute-start.9 = (bf16[4,2,32,256]{3,2,1,0:T(8,128)(2,1)S(1)}, bf16[4,2,32,256]{3,2,1,0:T(8,128)(2,1)S(1)}, u32[]{:S(2)}, u32[]{:S(2)}) collective-permute-start(bf16[4,2,32,256]{3,2,1,0:T(8,128)(2,1)S(1)} %constant_dynamic-slice_fusion), channel_id=1, source_target_pairs={{0,640},{128,768},{256,896},{384,0},{512,128},{640,256},{768,384},... | collective-permute-start | bytes 393224 | tf_op jit(solution)/shard_map/ppermute | solution.py:278
  140.4 81.3 %copy-start.1 = (bf16[1,1,1024,1024]{3,2,1,0:T(8,128)(2,1)S(1)}, bf16[1,1,1024,1024]{3,2,1,0:T(8,128)(2,1)}, u32[]{:S(2)}) copy-start(bf16[1,1,1024,1024]{3,2,1,0:T(8,128)(2,1)} %param.7) | copy-start | bytes 6291460
  223.1 1.7 copy-start.2
  224.9 1.2 copy-start.4
Sparse Core Ops, SparseCore 0:
  55.8 34.3 all-gather.8
  140.5 33.8 all-gather.6

commit v7 on v6

--- a/solution.py
+++ b/solution.py
@@ -23,7 +23,7 @@
 WHOLE = pl.BlockSpec(memory_space=pltpu.VMEM)
 
 BANDS, STEPS = 8, 5
-REP_AT, BLK_AT, TURN_AT, NEED_AT, LEVEL_AT, HAS_AT, HISTORY_AT, GRAM_AT = 0, 1, 2, 4, 6, 7, 8, 24
+REP_AT, BLK_AT, TURN_AT, NEED_AT, LEVEL_AT, HAS_AT, HISTORY_AT, GRAM_AT = 0, 1, 2, 4, 6, 10, 11, 27
 
 
 def ds(start, size, unit):
@@ -117,8 +117,7 @@
             )
         total = total * ((1.0 - DECAY) / order_full)
         out[block] = total
-        for turn in range(sent.shape[0]):
-            sent[turn, block] = total.astype(jnp.bfloat16)
+        sent[block] = total.astype(jnp.bfloat16)
 
 
 def stat_kernel(table, gram, came, out):
@@ -133,12 +132,18 @@
         out[block] = (DECAY * history + gram[block] + damping).astype(jnp.bfloat16)
 
 
+def choose_kernel(table, came, out):
+    shards = out.shape[0]
+    for shard in range(shards):
+        out[shard] = came[table[LEVEL_AT + shard] * shards + shard]
+
+
 def turn_kernel(table, came, band, sent):
     tile = sent.shape[1]
     size = came.shape[1] // STEPS
     shards = tile // size
     for shard in range(shards):
-        part = came[table[LEVEL_AT] * shards + shard]
+        part = came[shard]
         for step in range(STEPS):
             start = step * tile + shard * size
             band[start : start + size] = part[step * size : (step + 1) * size]
@@ -303,7 +308,8 @@
             jnp.stack([lax.axis_index(REP), my_blk]),
             cut(owner_map, my_own * home_count, home_count) % turns,
             cut(iterations, my_own * home_count, home_count),
-            jnp.stack([jnp.maximum(mine, 0) // column, jnp.where(mine >= 0, 1, 0)]),
+            jnp.maximum(holder, 0)[my_level, my_turn] // column,
+            jnp.where(mine >= 0, 1, 0)[None],
             cut(from_ring, my_level * column, column),
             (jnp.maximum(holder, 0) % column)[:, my_turn].reshape(-1),
         ]
@@ -331,31 +337,36 @@
     grad_tile = call(sum_kernel, [place, *partials], like((home_count, tile, width)))
     grad_cols = lax.all_gather(grad_tile, REP, axis=0, tiled=False)
 
-    history_sent = take(table, history_ring, HISTORY_AT)
+    grad_band = lax.all_gather(grad_tile, BLK, axis=0, tiled=False)
+
+    history_sent = take(table, after(history_ring, grad_band), HISTORY_AT)
     history_sent = history_sent.reshape(turns, home_count, depth, tile)
     history_came = exchange(history_sent, "y")
 
-    grad_band = lax.all_gather(grad_tile, BLK, axis=0, tiled=False)
     mine = lax.dynamic_slice_in_dim(grad_band, my_blk * size, size, 2)
     slices = [shift(mine, -step) for step in range(1, STEPS)]
     gram, gram_sent = call(
         gram_kernel,
         [place, grad_band, *slices],
-        [like((home_count, depth, tile), jnp.float32), like((turns, home_count, depth, tile))],
+        [like((home_count, depth, tile), jnp.float32), like((home_count, depth, tile))],
     )
-    gram_came = exchange(after(gram_sent, history_came), "y")
     stat = call(stat_kernel, [table, gram, history_came], like((home_count, depth, tile)))
     stat_band = lax.all_gather(stat, BLK, axis=0, tiled=False)
     stat_full = lax.all_gather(stat_band, REP, axis=0, tiled=False)
 
+    gram_came = lax.all_gather(after(gram_sent, stat_band), "y", axis=0, tiled=False)
     gram_sent = take(table, gram_came.reshape(ring, depth, tile), GRAM_AT)
-    gram_slot = exchange(gram_sent, RING)
+    gram_level = exchange(gram_sent, "zl")
+    gram_slot = call(choose_kernel, [table, gram_level], like((shards, depth, tile)))
+    gram_slot = exchange(gram_slot, BLK)
     band, turned = call(
-        turn_kernel, [table, gram_slot], [like((STEPS * tile, tile)), like((BANDS, tile, tile))]
+        turn_kernel,
+        [table, gram_slot],
+        [like((STEPS * tile, tile)), like((BANDS, tile, tile))],
     )
-    new_rows = finish(table, history, band, exchange(turned, REP))
-
     directions = newton(table, stat_full, grad_cols)
+    turned = after(exchange(turned, REP), directions)
+    new_rows = finish(table, history, band, turned)
     return (directions, new_rows[None, None])
 
 

time: 240 us -> 227 us (0.946)
  blocking collectives: 136 us -> 105 us
  starting transfers between devices: 57.1 us -> 73 us
    all_to_all x3 -> x2, blocking collectives: 80.1 us -> 36 us  [exchange(): return lax.all_to_all(array, axis, split_axis=0, concat_axis=0, tiled=True)]
    all_gather x0 -> x1, blocking collectives: none -> 19.5 us  [body(): lax.all_gather(after(gram_sent, stat_band), 'y', axis=0, tiled=False)]
    all_to_all x2 -> x3, starting transfers between devices: 26.2 us -> 40.4 us  [exchange(): return lax.all_to_all(array, axis, split_axis=0, concat_axis=0, tiled=True)]
    all_gather x1, blocking collectives: 23.5 us -> 19.6 us  [body(): stat_band = lax.all_gather(stat, BLK, axis=0, tiled=False)]
    all_gather x1, blocking collectives: 32.4 us -> 29.4 us  [body(): grad_band = lax.all_gather(grad_tile, BLK, axis=0, tiled=False)]
    pallas_call x7 -> x8, Pallas kernels: 6.05 us -> 7.29 us  [call(): pl.pallas_call(kernel, out_shape=outs, in_specs=in_specs or [SCALARS] + [...]
  transfers between devices with their start and end apart: 15 -> 16, of which waited for: 4 -> 5; matrix products, arithmetic and copies ran while one was open for 1% -> 1% of each run, Pallas kernels for 3% -> 6%
where the time goes in v7:
time: 227 us; the launch traced here: 226 us
  blocking collectives  105 us (46%)
  starting transfers between devices  73 us (32%)
  Pallas kernels  16.6 us (7%)
  between operations  14.9 us (7%)
  waiting for transfers between devices  11 us (5%)
  local copies, waits for them, and re-layouts  5.64 us (2%)
    all_to_all x3, starting transfers between devices, exchange(): return lax.all_to_all(array, axis, split_axis=0, concat_axis=0, tiled=True)  40.4 us
    all_to_all x2, blocking collectives, exchange(): return lax.all_to_all(array, axis, split_axis=0, concat_axis=0, tiled=True)  36 us
    ppermute x11, starting transfers between devices, shift(): lax.ppermute(array, REP, [(i, (i + step) % BANDS) for i in range(BANDS)])  32.5 us
    all_gather x1, blocking collectives, body(): grad_band = lax.all_gather(grad_tile, BLK, axis=0, tiled=False)  29.4 us
    all_gather x1, blocking collectives, body(): stat_band = lax.all_gather(stat, BLK, axis=0, tiled=False)  19.6 us
    all_gather x1, blocking collectives, body(): lax.all_gather(after(gram_sent, stat_band), 'y', axis=0, tiled=False)  19.5 us
    ppermute x11, waiting for transfers between devices, shift(): lax.ppermute(array, REP, [(i, (i + step) % BANDS) for i in range(BANDS)])  8.84 us
    pallas_call x8, Pallas kernels, call(): pl.pallas_call(kernel, out_shape=outs, in_specs=in_specs or [SCALARS] + [...  7.29 us
  transfers between devices with their start and end apart: 16, of which 5 were waited for; matrix products, arithmetic and copies ran while one was open for 1% of the time, Pallas kernels for 6%

profile of v7, /device:TPU:1, one launch (start us, length us, event | category | flops | bytes accessed | tf_op | source)
XLA Modules:
  0.0 226.1 jit_solution(16490046487499445110)
XLA Ops:
  7.2 0.1 pad_add_fusion.table
  7.3 1.6 copy-done
  8.9 1.6 shard_map.62
  10.4 19.4 %all-to-all-start = ((bf16[16,160,128]{2,1,0:T(8,128)(2,1)}), bf16[16,160,128]{2,1,0:T(8,128)(2,1)S(1)}, u32[]{:S(2)}, u32[]{:S(2)}) async-start(bf16[16,160,128]{2,1,0:T(8,128)(2,1)} %shard_map.62), calls=%async_computation | async-start | bytes 1310720 | tf_op jit(solution)/shard_map/all_to_all | solution.py:279
  29.9 0.6 shard_map.59
  30.5 2.1 collective-permute-start
  32.6 3.1 %collective-permute-start.1 = (bf16[2,128,256]{2,1,0:T(8,128)(2,1)S(1)}, bf16[2,128,256]{2,1,0:T(8,128)(2,1)S(1)}, u32[]{:S(2)}, u32[]{:S(2)}) collective-permute-start(bf16[2,128,256]{2,1,0:T(8,128)(2,1)S(1)} %get-tuple-element.19), channel_id=1, source_target_pairs={{0,256},{128,384},{256,512},{384,640},{512,768},{640,896},{768,0},... | collective-permute-start | bytes 393224 | tf_op jit(solution)/shard_map/ppermute | solution.py:283
  35.7 3.5 %collective-permute-start.2 = (bf16[2,128,256]{2,1,0:T(8,128)(2,1)S(1)}, bf16[2,128,256]{2,1,0:T(8,128)(2,1)S(1)}, u32[]{:S(2)}, u32[]{:S(2)}) collective-permute-start(bf16[2,128,256]{2,1,0:T(8,128)(2,1)S(1)} %get-tuple-element.20), channel_id=1, source_target_pairs={{0,384},{128,512},{256,640},{384,768},{512,896},{640,0},{768,128},... | collective-permute-start | bytes 393224 | tf_op jit(solution)/shard_map/ppermute | solution.py:283
  39.2 2.4 %collective-permute-start.3 = (bf16[2,128,256]{2,1,0:T(8,128)(2,1)S(1)}, bf16[2,128,256]{2,1,0:T(8,128)(2,1)S(1)}, u32[]{:S(2)}, u32[]{:S(2)}) collective-permute-start(bf16[2,128,256]{2,1,0:T(8,128)(2,1)S(1)} %get-tuple-element.21), channel_id=1, source_target_pairs={{0,512},{128,640},{256,768},{384,896},{512,0},{640,128},{768,256},... | collective-permute-start | bytes 393224 | tf_op jit(solution)/shard_map/ppermute | solution.py:283
  41.6 3.9 %collective-permute-start.4 = (bf16[2,128,256]{2,1,0:T(8,128)(2,1)S(1)}, bf16[2,128,256]{2,1,0:T(8,128)(2,1)S(1)}, u32[]{:S(2)}, u32[]{:S(2)}) collective-permute-start(bf16[2,128,256]{2,1,0:T(8,128)(2,1)S(1)} %get-tuple-element.22), channel_id=1, source_target_pairs={{0,640},{128,768},{256,896},{384,0},{512,128},{640,256},{768,384},... | collective-permute-start | bytes 393224 | tf_op jit(solution)/shard_map/ppermute | solution.py:283
  45.5 0.2 select_reduce_fusion.1
  45.7 0.1 select_reduce_fusion
  45.8 2.6 %collective-permute-start.5 = (bf16[2,128,256]{2,1,0:T(8,128)(2,1)S(1)}, bf16[2,128,256]{2,1,0:T(8,128)(2,1)S(1)}, u32[]{:S(2)}, u32[]{:S(2)}) collective-permute-start(bf16[2,128,256]{2,1,0:T(8,128)(2,1)S(1)} %get-tuple-element.23), channel_id=1, source_target_pairs={{0,768},{128,896},{256,0},{384,128},{512,256},{640,384},{768,512},... | collective-permute-start | bytes 393224 | tf_op jit(solution)/shard_map/ppermute | solution.py:283
  48.4 1.6 collective-permute-start.6
  50.0 0.1 sub.17
  50.2 1.7 collective-permute-done.5.refs_6_
  51.9 2.7 %collective-permute-done.6.refs_7_ = bf16[2,128,256]{2,1,0:T(8,128)(2,1)S(1)} collective-permute-done((bf16[2,128,256]{2,1,0:T(8,128)(2,1)S(1)}, bf16[2,128,256]{2,1,0:T(8,128)(2,1)S(1)}, u32[]{:S(2)}, u32[]{:S(2)}) %collective-permute-start.6) | collective-permute-done | bytes 131104 | tf_op jit(solution)/shard_map/ppermute | solution.py:283
  54.6 1.3 shard_map.60
  56.0 0.1 reshape_squeeze.3
  56.1 0.1 dynamic_slice.22
  56.2 0.1 dynamic_slice.25
  56.3 0.6 dynamic_slice.24
  57.6 0.1 and_select_fusion.3
  57.7 0.1 concatenate.3.table
  57.8 29.4 %all-gather = bf16[8,128,256]{2,1,0:T(8,128)(2,1)S(1)} all-gather(bf16[2,128,256]{2,1,0:T(8,128)(2,1)} %shard_map.60), channel_id=2, replica_groups=mesh['x'=4,'core'=2,'zl'=4,'y'=8,'zh'=4] {'zh'}, dimensions={0}, use_global_device_ids=true | all-gather | bytes 655360 | tf_op jit(solution)/shard_map/all_gather | solution.py:340
  87.2 1.4 shard_map.63
  88.6 6.8 %all-to-all-start.1 = ((bf16[8,2,160,128]{3,2,1,0:T(8,128)(2,1)}), bf16[8,2,160,128]{3,2,1,0:T(8,128)(2,1)S(1)}, u32[]{:S(2)}, u32[]{:S(2)}) async-start(bf16[8,2,160,128]{3,2,1,0:T(8,128)(2,1)} %bitcast.7), calls=%async_computation.1 | async-start | bytes 1310720 | tf_op jit(solution)/shard_map/all_to_all | solution.py:279
  95.5 4.8 %collective-permute-start.10 = (bf16[4,2,32,256]{3,2,1,0:T(8,128)(2,1)S(1)}, bf16[4,2,32,256]{3,2,1,0:T(8,128)(2,1)S(1)}, u32[]{:S(2)}, u32[]{:S(2)}) collective-permute-start(bf16[4,2,32,256]{3,2,1,0:T(8,128)(2,1)S(1)} %constant_dynamic-slice_fusion), channel_id=1, source_target_pairs={{0,512},{128,640},{256,768},{384,896},{512,0},{640,128},{768,256},... | collective-permute-start | bytes 393224 | tf_op jit(solution)/shard_map/ppermute | solution.py:283
  100.3 3.4 %collective-permute-start.9 = (bf16[4,2,32,256]{3,2,1,0:T(8,128)(2,1)S(1)}, bf16[4,2,32,256]{3,2,1,0:T(8,128)(2,1)S(1)}, u32[]{:S(2)}, u32[]{:S(2)}) collective-permute-start(bf16[4,2,32,256]{3,2,1,0:T(8,128)(2,1)S(1)} %constant_dynamic-slice_fusion), channel_id=1, source_target_pairs={{0,640},{128,768},{256,896},{384,0},{512,128},{640,256},{768,384},... | collective-permute-start | bytes 393224 | tf_op jit(solution)/shard_map/ppermute | solution.py:283
  103.8 2.0 collective-permute-start.8
  105.8 3.1 %collective-permute-start.7 = (bf16[4,2,32,256]{3,2,1,0:T(8,128)(2,1)S(1)}, bf16[4,2,32,256]{3,2,1,0:T(8,128)(2,1)S(1)}, u32[]{:S(2)}, u32[]{:S(2)}) collective-permute-start(bf16[4,2,32,256]{3,2,1,0:T(8,128)(2,1)S(1)} %constant_dynamic-slice_fusion), channel_id=1, source_target_pairs={{0,896},{128,0},{256,128},{384,256},{512,384},{640,512},{768,640},... | collective-permute-start | bytes 393224 | tf_op jit(solution)/shard_map/ppermute | solution.py:283
  108.9 2.9 %collective-permute-done.8.refs_1_ = bf16[4,2,32,256]{3,2,1,0:T(8,128)(2,1)S(1)} collective-permute-done((bf16[4,2,32,256]{3,2,1,0:T(8,128)(2,1)S(1)}, bf16[4,2,32,256]{3,2,1,0:T(8,128)(2,1)S(1)}, u32[]{:S(2)}, u32[]{:S(2)}) %collective-permute-start.8) | collective-permute-done | bytes 131104 | tf_op jit(solution)/shard_map/ppermute | solution.py:283
  111.8 1.4 collective-permute-done.7.refs_0_
  113.3 0.9 shard_map.61
  114.1 2.1 all-to-all-done.1.came
  116.2 0.6 shard_map.64
  116.8 19.6 %all-gather.1 = bf16[8,160,128]{2,1,0:T(8,128)(2,1)} all-gather(bf16[2,160,128]{2,1,0:T(8,128)(2,1)S(1)} %shard_map.64), channel_id=3, replica_groups=mesh['x'=4,'core'=2,'zl'=4,'y'=8,'zh'=4] {'zh'}, dimensions={0}, use_global_device_ids=true | all-gather | bytes 409600 | tf_op jit(solution)/shard_map/all_gather | solution.py:354
  136.5 19.5 %all-gather.4.tiles = bf16[16,160,128]{2,1,0:T(8,128)(2,1)S(1)} all-gather(bf16[2,160,128]{2,1,0:T(8,128)(2,1)S(1)} %get-tuple-element.28), channel_id=6, replica_groups=mesh['x'=4,'core'=2,'zl'=4,'y'=8,'zh'=4] {'y'}, dimensions={0}, use_global_device_ids=true | all-gather | bytes 737280 | tf_op jit(solution)/shard_map/all_gather | solution.py:357
  155.9 0.6 shard_map.66
  156.5 18.0 %all_to_all.25.came = bf16[16,160,128]{2,1,0:T(8,128)(2,1)S(1)} all-to-all(bf16[16,160,128]{2,1,0:T(8,128)(2,1)S(1)} %shard_map.66), channel_id=1, replica_groups=mesh['x'=4,'core'=2,'zl'=4,'y'=8,'zh'=4] {'zl'}, dimensions={0} | all-to-all | bytes 1310720 | tf_op jit(solution)/shard_map/all_to_all | solution.py:279
  174.6 0.6 shard_map.67
  175.2 18.0 %all_to_all.26.came = bf16[4,160,128]{2,1,0:T(8,128)(2,1)S(1)} all-to-all(bf16[4,160,128]{2,1,0:T(8,128)(2,1)S(1)} %shard_map.67), channel_id=1, replica_groups=mesh['x'=4,'core'=2,'zl'=4,'y'=8,'zh'=4] {'zh'}, dimensions={0} | all-to-all | bytes 327680 | tf_op jit(solution)/shard_map/all_to_all | solution.py:279
  193.1 1.3 shard_map.68
  194.4 14.2 %all-to-all-start.4 = ((bf16[8,128,128]{2,1,0:T(8,128)(2,1)}), bf16[8,128,128]{2,1,0:T(8,128)(2,1)S(1)}, u32[]{:S(2)}, u32[]{:S(2)}) async-start(bf16[8,128,128]{2,1,0:T(8,128)(2,1)} %get-tuple-element.30), calls=%async_computation.4 | async-start | bytes 524288 | tf_op jit(solution)/shard_map/all_to_all | solution.py:279
  208.6 1.7 copy-done.2
  210.3 1.2 copy-done.4
  211.6 6.3 %shard_map.65 = bf16[2,128,256]{2,1,0:T(8,128)(2,1)} custom-call(s32[43]{0:T(128)S(1)} %concatenate.3.table, bf16[8,4,2,160,128]{4,3,2,1,0:T(8,128)(2,1)S(1)} %bitcast.19, bf16[8,2,128,256]{3,2,1,0:T(8,128)(2,1)S(1)} %bitcast.21), custom_call_target="tpu_custom_call" | custom-call | tf_op jit(solution)/shard_map/pallas_call | solution.py:261
  217.9 1.4 shard_map.69
  (32 shorter events, 0.2 us)
Async XLA Ops:
  7.2 38.3 %copy-start.5 = (s32[64]{0:T(128)S(1)}, s32[64]{0:T(128)}, u32[]{:S(2)}) copy-start(s32[64]{0:T(128)} %param.5) | copy-start | bytes 772
  7.3 1.6 copy-start
  8.8 21.0 %copy-start.3 = (bf16[1,2,1024,256]{3,2,1,0:T(8,128)(2,1)S(1)}, bf16[1,2,1024,256]{3,2,1,0:T(8,128)(2,1)}, u32[]{:S(2)}) copy-start(bf16[1,2,1024,256]{3,2,1,0:T(8,128)(2,1)} %param.4) | copy-start | bytes 3145732
  8.9 47.3 %copy-start.6 = (s32[64]{0:T(128)S(1)}, s32[64]{0:T(128)}, u32[]{:S(2)}) copy-start(s32[64]{0:T(128)} %param.6) | copy-start | bytes 772
  10.4 76.8 %all-to-all-start = ((bf16[16,160,128]{2,1,0:T(8,128)(2,1)}), bf16[16,160,128]{2,1,0:T(8,128)(2,1)S(1)}, u32[]{:S(2)}, u32[]{:S(2)}) async-start(bf16[16,160,128]{2,1,0:T(8,128)(2,1)} %shard_map.62), calls=%async_computation | async-start | bytes 1310720 | tf_op jit(solution)/shard_map/all_to_all | solution.py:279
  29.8 178.7 %all-gather.10.cloned.1.call-start = ((), (), s32[]{:S(2)}) async-start(), calls=%async_computation.6 | async-start | bytes 1179648 | tf_op jit(solution)/shard_map/all_gather | solution.py:338
  30.5 15.3 %collective-permute-start = (bf16[2,128,256]{2,1,0:T(8,128)(2,1)S(1)}, bf16[2,128,256]{2,1,0:T(8,128)(2,1)S(1)}, u32[]{:S(2)}, u32[]{:S(2)}) collective-permute-start(bf16[2,128,256]{2,1,0:T(8,128)(2,1)S(1)} %get-tuple-element.18), channel_id=1, source_target_pairs={{0,128},{128,256},{256,384},{384,512},{512,640},{640,768},{768,896... | collective-permute-start | bytes 393224 | tf_op jit(solution)/shard_map/ppermute | solution.py:283
  32.6 15.8 %collective-permute-start.1 = (bf16[2,128,256]{2,1,0:T(8,128)(2,1)S(1)}, bf16[2,128,256]{2,1,0:T(8,128)(2,1)S(1)}, u32[]{:S(2)}, u32[]{:S(2)}) collective-permute-start(bf16[2,128,256]{2,1,0:T(8,128)(2,1)S(1)} %get-tuple-element.19), channel_id=1, source_target_pairs={{0,256},{128,384},{256,512},{384,640},{512,768},{640,896},{768,0},... | collective-permute-start | bytes 393224 | tf_op jit(solution)/shard_map/ppermute | solution.py:283
  35.7 14.5 %collective-permute-start.2 = (bf16[2,128,256]{2,1,0:T(8,128)(2,1)S(1)}, bf16[2,128,256]{2,1,0:T(8,128)(2,1)S(1)}, u32[]{:S(2)}, u32[]{:S(2)}) collective-permute-start(bf16[2,128,256]{2,1,0:T(8,128)(2,1)S(1)} %get-tuple-element.20), channel_id=1, source_target_pairs={{0,384},{128,512},{256,640},{384,768},{512,896},{640,0},{768,128},... | collective-permute-start | bytes 393224 | tf_op jit(solution)/shard_map/ppermute | solution.py:283
  39.2 11.0 %collective-permute-start.3 = (bf16[2,128,256]{2,1,0:T(8,128)(2,1)S(1)}, bf16[2,128,256]{2,1,0:T(8,128)(2,1)S(1)}, u32[]{:S(2)}, u32[]{:S(2)}) collective-permute-start(bf16[2,128,256]{2,1,0:T(8,128)(2,1)S(1)} %get-tuple-element.21), channel_id=1, source_target_pairs={{0,512},{128,640},{256,768},{384,896},{512,0},{640,128},{768,256},... | collective-permute-start | bytes 393224 | tf_op jit(solution)/shard_map/ppermute | solution.py:283
  41.6 8.6 %collective-permute-start.4 = (bf16[2,128,256]{2,1,0:T(8,128)(2,1)S(1)}, bf16[2,128,256]{2,1,0:T(8,128)(2,1)S(1)}, u32[]{:S(2)}, u32[]{:S(2)}) collective-permute-start(bf16[2,128,256]{2,1,0:T(8,128)(2,1)S(1)} %get-tuple-element.22), channel_id=1, source_target_pairs={{0,640},{128,768},{256,896},{384,0},{512,128},{640,256},{768,384},... | collective-permute-start | bytes 393224 | tf_op jit(solution)/shard_map/ppermute | solution.py:283
  45.8 6.1 %collective-permute-start.5 = (bf16[2,128,256]{2,1,0:T(8,128)(2,1)S(1)}, bf16[2,128,256]{2,1,0:T(8,128)(2,1)S(1)}, u32[]{:S(2)}, u32[]{:S(2)}) collective-permute-start(bf16[2,128,256]{2,1,0:T(8,128)(2,1)S(1)} %get-tuple-element.23), channel_id=1, source_target_pairs={{0,768},{128,896},{256,0},{384,128},{512,256},{640,384},{768,512},... | collective-permute-start | bytes 393224 | tf_op jit(solution)/shard_map/ppermute | solution.py:283
  48.4 6.2 %collective-permute-start.6 = (bf16[2,128,256]{2,1,0:T(8,128)(2,1)S(1)}, bf16[2,128,256]{2,1,0:T(8,128)(2,1)S(1)}, u32[]{:S(2)}, u32[]{:S(2)}) collective-permute-start(bf16[2,128,256]{2,1,0:T(8,128)(2,1)S(1)} %get-tuple-element.24), channel_id=1, source_target_pairs={{0,896},{128,0},{256,128},{384,256},{512,384},{640,512},{768,640},... | collective-permute-start | bytes 393224 | tf_op jit(solution)/shard_map/ppermute | solution.py:283
  88.6 27.6 %all-to-all-start.1 = ((bf16[8,2,160,128]{3,2,1,0:T(8,128)(2,1)}), bf16[8,2,160,128]{3,2,1,0:T(8,128)(2,1)S(1)}, u32[]{:S(2)}, u32[]{:S(2)}) async-start(bf16[8,2,160,128]{3,2,1,0:T(8,128)(2,1)} %bitcast.7), calls=%async_computation.1 | async-start | bytes 1310720 | tf_op jit(solution)/shard_map/all_to_all | solution.py:279
  95.5 113.1 %all-gather.8.cloned.1.call-start = ((), (), s32[]{:S(2)}) async-start(), calls=%async_computation.5 | async-start | bytes 2949120 | tf_op jit(solution)/shard_map/all_gather | solution.py:355
  95.5 13.4 %collective-permute-start.10 = (bf16[4,2,32,256]{3,2,1,0:T(8,128)(2,1)S(1)}, bf16[4,2,32,256]{3,2,1,0:T(8,128)(2,1)S(1)}, u32[]{:S(2)}, u32[]{:S(2)}) collective-permute-start(bf16[4,2,32,256]{3,2,1,0:T(8,128)(2,1)S(1)} %constant_dynamic-slice_fusion), channel_id=1, source_target_pairs={{0,512},{128,640},{256,768},{384,896},{512,0},{640,128},{768,256},... | collective-permute-start | bytes 393224 | tf_op jit(solution)/shard_map/ppermute | solution.py:283
  100.3 8.6 %collective-permute-start.9 = (bf16[4,2,32,256]{3,2,1,0:T(8,128)(2,1)S(1)}, bf16[4,2,32,256]{3,2,1,0:T(8,128)(2,1)S(1)}, u32[]{:S(2)}, u32[]{:S(2)}) collective-permute-start(bf16[4,2,32,256]{3,2,1,0:T(8,128)(2,1)S(1)} %constant_dynamic-slice_fusion), channel_id=1, source_target_pairs={{0,640},{128,768},{256,896},{384,0},{512,128},{640,256},{768,384},... | collective-permute-start | bytes 393224 | tf_op jit(solution)/shard_map/ppermute | solution.py:283
  103.8 8.0 %collective-permute-start.8 = (bf16[4,2,32,256]{3,2,1,0:T(8,128)(2,1)S(1)}, bf16[4,2,32,256]{3,2,1,0:T(8,128)(2,1)S(1)}, u32[]{:S(2)}, u32[]{:S(2)}) collective-permute-start(bf16[4,2,32,256]{3,2,1,0:T(8,128)(2,1)S(1)} %constant_dynamic-slice_fusion), channel_id=1, source_target_pairs={{0,768},{128,896},{256,0},{384,128},{512,256},{640,384},{768,512},... | collective-permute-start | bytes 393224 | tf_op jit(solution)/shard_map/ppermute | solution.py:283
  105.8 7.5 %collective-permute-start.7 = (bf16[4,2,32,256]{3,2,1,0:T(8,128)(2,1)S(1)}, bf16[4,2,32,256]{3,2,1,0:T(8,128)(2,1)S(1)}, u32[]{:S(2)}, u32[]{:S(2)}) collective-permute-start(bf16[4,2,32,256]{3,2,1,0:T(8,128)(2,1)S(1)} %constant_dynamic-slice_fusion), channel_id=1, source_target_pairs={{0,896},{128,0},{256,128},{384,256},{512,384},{640,512},{768,640},... | collective-permute-start | bytes 393224 | tf_op jit(solution)/shard_map/ppermute | solution.py:283
  174.6 43.3 %copy-start.1 = (bf16[1,1,1024,1024]{3,2,1,0:T(8,128)(2,1)S(1)}, bf16[1,1,1024,1024]{3,2,1,0:T(8,128)(2,1)}, u32[]{:S(2)}) copy-start(bf16[1,1,1024,1024]{3,2,1,0:T(8,128)(2,1)} %param.7) | copy-start | bytes 6291460
  194.4 23.4 %all-to-all-start.4 = ((bf16[8,128,128]{2,1,0:T(8,128)(2,1)}), bf16[8,128,128]{2,1,0:T(8,128)(2,1)S(1)}, u32[]{:S(2)}, u32[]{:S(2)}) async-start(bf16[8,128,128]{2,1,0:T(8,128)(2,1)} %get-tuple-element.30), calls=%async_computation.4 | async-start | bytes 524288 | tf_op jit(solution)/shard_map/all_to_all | solution.py:279
  208.6 1.7 copy-start.2
  210.3 1.2 copy-start.4
Sparse Core Ops, SparseCore 0:
  56.1 34.3 all-gather.9
  136.6 32.5 all-gather.7

commit v8 on v7

--- a/solution.py
+++ b/solution.py
@@ -117,7 +117,8 @@
             )
         total = total * ((1.0 - DECAY) / order_full)
         out[block] = total
-        sent[block] = total.astype(jnp.bfloat16)
+        for turn in range(sent.shape[0]):
+            sent[turn, block] = total.astype(jnp.bfloat16)
 
 
 def stat_kernel(table, gram, came, out):
@@ -324,7 +325,7 @@
     tile = order_full // BANDS
     size = tile // shards
     depth = STEPS * size
-    history = slot_history[0, 0]
+    history = pltpu.with_memory_space_constraint(slot_history[0, 0], pltpu.HBM)
     table = tables(owner_map, iterations, home_count)
     place = jnp.stack([lax.axis_index(REP), my_blk]).astype(jnp.int32)
 
@@ -348,13 +349,13 @@
     gram, gram_sent = call(
         gram_kernel,
         [place, grad_band, *slices],
-        [like((home_count, depth, tile), jnp.float32), like((home_count, depth, tile))],
+        [like((home_count, depth, tile), jnp.float32), like((turns, home_count, depth, tile))],
     )
     stat = call(stat_kernel, [table, gram, history_came], like((home_count, depth, tile)))
     stat_band = lax.all_gather(stat, BLK, axis=0, tiled=False)
-    stat_full = lax.all_gather(stat_band, REP, axis=0, tiled=False)
-
-    gram_came = lax.all_gather(after(gram_sent, stat_band), "y", axis=0, tiled=False)
+    gram_came = exchange(gram_sent, "y")
+    stat_full = lax.all_gather(after(stat_band, gram_came), REP, axis=0, tiled=False)
+
     gram_sent = take(table, gram_came.reshape(ring, depth, tile), GRAM_AT)
     gram_level = exchange(gram_sent, "zl")
     gram_slot = call(choose_kernel, [table, gram_level], like((shards, depth, tile)))
@@ -364,7 +365,11 @@
         [table, gram_slot],
         [like((STEPS * tile, tile)), like((BANDS, tile, tile))],
     )
-    directions = newton(table, stat_full, grad_cols)
+    directions = newton(
+        table,
+        pltpu.with_memory_space_constraint(stat_full, pltpu.HBM),
+        pltpu.with_memory_space_constraint(grad_cols, pltpu.HBM),
+    )
     turned = after(exchange(turned, REP), directions)
     new_rows = finish(table, history, band, turned)
     return (directions, new_rows[None, None])

time: 227 us -> 210 us (0.925)
  blocking collectives: 105 us -> 91.8 us
  local copies, waits for them, and re-layouts: 5.64 us -> 1.11 us
  Pallas kernels: 16.6 us -> 20.5 us
  waiting for transfers between devices: 11 us -> 8.44 us
    all_gather x1 -> x0, blocking collectives: 19.5 us -> none  [body(): lax.all_gather(after(gram_sent, stat_band), 'y', axis=0, tiled=False)]
    unnamed x14 -> x6, local copies, waits for them, and re-layouts: 4.57 us -> 0.01 us
    all_gather x1, blocking collectives: 19.6 us -> 22.9 us  [body(): stat_band = lax.all_gather(stat, BLK, axis=0, tiled=False)]
    all_to_all x2, blocking collectives: 36 us -> 38.5 us  [exchange(): return lax.all_to_all(array, axis, split_axis=0, concat_axis=0, tiled=True)]
    all_to_all x3 -> x4, starting transfers between devices: 40.4 us -> 40 us  [exchange(): return lax.all_to_all(array, axis, split_axis=0, concat_axis=0, tiled=True)]
  transfers between devices with their start and end apart: 16 -> 17, of which waited for: 5 -> 4; matrix products, arithmetic and copies ran while one was open for 1% -> 1% of each run, Pallas kernels for 6% -> 7%
where the time goes in v8:
time: 210 us; the launch traced here: 209 us
  blocking collectives  91.8 us (44%)
  starting transfers between devices  71.7 us (34%)
  Pallas kernels  20.5 us (10%)
  between operations  15 us (7%)
  waiting for transfers between devices  8.44 us (4%)
    all_to_all x4, starting transfers between devices, exchange(): return lax.all_to_all(array, axis, split_axis=0, concat_axis=0, tiled=True)  40 us
    all_to_all x2, blocking collectives, exchange(): return lax.all_to_all(array, axis, split_axis=0, concat_axis=0, tiled=True)  38.5 us
    ppermute x11, starting transfers between devices, shift(): lax.ppermute(array, REP, [(i, (i + step) % BANDS) for i in range(BANDS)])  31.6 us
    all_gather x1, blocking collectives, body(): grad_band = lax.all_gather(grad_tile, BLK, axis=0, tiled=False)  30.4 us
    all_gather x1, blocking collectives, body(): stat_band = lax.all_gather(stat, BLK, axis=0, tiled=False)  22.9 us
    pallas_call x8, Pallas kernels, call(): pl.pallas_call(kernel, out_shape=outs, in_specs=in_specs or [SCALARS] + [...  8.17 us
    ppermute x11, waiting for transfers between devices, shift(): lax.ppermute(array, REP, [(i, (i + step) % BANDS) for i in range(BANDS)])  7.73 us
    pallas_call x1, Pallas kernels, newton(): pl.pallas_call(newton_kernel, out_shape=like((home_count, tile, width)),...  7.51 us
  transfers between devices with their start and end apart: 17, of which 4 were waited for; matrix products, arithmetic and copies ran while one was open for 1% of the time, Pallas kernels for 7%

profile of v8, /device:TPU:1, one launch (start us, length us, event | category | flops | bytes accessed | tf_op | source)
XLA Modules:
  0.0 209.1 jit_solution(5159033782701293205)
XLA Ops:
  7.2 0.1 pad_add_fusion.table
  7.3 2.4 %shard_map.62 = bf16[16,160,128]{2,1,0:T(8,128)(2,1)} custom-call(s32[2]{0:T(128)S(1)} %pad_add_fusion.table, bf16[1024,1024]{1,0:T(8,128)(2,1)} %bitcast.20), custom_call_target="tpu_custom_call" | custom-call | tf_op jit(solution)/shard_map/pallas_call | solution.py:80
  9.7 19.4 %all-to-all-start = ((bf16[16,160,128]{2,1,0:T(8,128)(2,1)}), bf16[16,160,128]{2,1,0:T(8,128)(2,1)S(1)}, u32[]{:S(2)}, u32[]{:S(2)}) async-start(bf16[16,160,128]{2,1,0:T(8,128)(2,1)} %shard_map.62), calls=%async_computation | async-start | bytes 1310720 | tf_op jit(solution)/shard_map/all_to_all | solution.py:280
  29.1 0.6 shard_map.59
  29.8 2.1 collective-permute-start
  31.8 3.1 %collective-permute-start.1 = (bf16[2,128,256]{2,1,0:T(8,128)(2,1)S(1)}, bf16[2,128,256]{2,1,0:T(8,128)(2,1)S(1)}, u32[]{:S(2)}, u32[]{:S(2)}) collective-permute-start(bf16[2,128,256]{2,1,0:T(8,128)(2,1)S(1)} %get-tuple-element.19), channel_id=1, source_target_pairs={{0,256},{128,384},{256,512},{384,640},{512,768},{640,896},{768,0},... | collective-permute-start | bytes 393224 | tf_op jit(solution)/shard_map/ppermute | solution.py:284
  35.0 3.5 %collective-permute-start.2 = (bf16[2,128,256]{2,1,0:T(8,128)(2,1)S(1)}, bf16[2,128,256]{2,1,0:T(8,128)(2,1)S(1)}, u32[]{:S(2)}, u32[]{:S(2)}) collective-permute-start(bf16[2,128,256]{2,1,0:T(8,128)(2,1)S(1)} %get-tuple-element.20), channel_id=1, source_target_pairs={{0,384},{128,512},{256,640},{384,768},{512,896},{640,0},{768,128},... | collective-permute-start | bytes 393224 | tf_op jit(solution)/shard_map/ppermute | solution.py:284
  38.4 2.4 %collective-permute-start.3 = (bf16[2,128,256]{2,1,0:T(8,128)(2,1)S(1)}, bf16[2,128,256]{2,1,0:T(8,128)(2,1)S(1)}, u32[]{:S(2)}, u32[]{:S(2)}) collective-permute-start(bf16[2,128,256]{2,1,0:T(8,128)(2,1)S(1)} %get-tuple-element.21), channel_id=1, source_target_pairs={{0,512},{128,640},{256,768},{384,896},{512,0},{640,128},{768,256},... | collective-permute-start | bytes 393224 | tf_op jit(solution)/shard_map/ppermute | solution.py:284
  40.8 3.9 %collective-permute-start.4 = (bf16[2,128,256]{2,1,0:T(8,128)(2,1)S(1)}, bf16[2,128,256]{2,1,0:T(8,128)(2,1)S(1)}, u32[]{:S(2)}, u32[]{:S(2)}) collective-permute-start(bf16[2,128,256]{2,1,0:T(8,128)(2,1)S(1)} %get-tuple-element.22), channel_id=1, source_target_pairs={{0,640},{128,768},{256,896},{384,0},{512,128},{640,256},{768,384},... | collective-permute-start | bytes 393224 | tf_op jit(solution)/shard_map/ppermute | solution.py:284
  44.8 0.2 select_reduce_fusion.1
  45.0 0.1 select_reduce_fusion
  45.1 0.1 sub.17
  45.2 2.6 %collective-permute-start.5 = (bf16[2,128,256]{2,1,0:T(8,128)(2,1)S(1)}, bf16[2,128,256]{2,1,0:T(8,128)(2,1)S(1)}, u32[]{:S(2)}, u32[]{:S(2)}) collective-permute-start(bf16[2,128,256]{2,1,0:T(8,128)(2,1)S(1)} %get-tuple-element.23), channel_id=1, source_target_pairs={{0,768},{128,896},{256,0},{384,128},{512,256},{640,384},{768,512},... | collective-permute-start | bytes 393224 | tf_op jit(solution)/shard_map/ppermute | solution.py:284
  47.8 1.6 collective-permute-start.6
  49.5 0.7 dynamic_slice.24
  50.1 0.1 reshape_squeeze.3
  50.9 0.1 dynamic_slice.22
  51.0 0.1 dynamic_slice.25
  51.1 0.1 and_select_fusion.3
  51.2 0.1 concatenate.3.table
  51.3 2.7 %collective-permute-done.6.refs_7_ = bf16[2,128,256]{2,1,0:T(8,128)(2,1)S(1)} collective-permute-done((bf16[2,128,256]{2,1,0:T(8,128)(2,1)S(1)}, bf16[2,128,256]{2,1,0:T(8,128)(2,1)S(1)}, u32[]{:S(2)}, u32[]{:S(2)}) %collective-permute-start.6) | collective-permute-done | bytes 131104 | tf_op jit(solution)/shard_map/ppermute | solution.py:284
  54.0 1.3 shard_map.60
  55.4 30.4 %all-gather = bf16[8,128,256]{2,1,0:T(8,128)(2,1)S(1)} all-gather(bf16[2,128,256]{2,1,0:T(8,128)(2,1)} %shard_map.60), channel_id=2, replica_groups=mesh['x'=4,'core'=2,'zl'=4,'y'=8,'zh'=4] {'zh'}, dimensions={0}, use_global_device_ids=true | all-gather | bytes 655360 | tf_op jit(solution)/shard_map/all_gather | solution.py:341
  85.8 1.4 shard_map.63
  87.2 6.8 %all-to-all-start.1 = ((bf16[8,2,160,128]{3,2,1,0:T(8,128)(2,1)}), bf16[8,2,160,128]{3,2,1,0:T(8,128)(2,1)S(1)}, u32[]{:S(2)}, u32[]{:S(2)}) async-start(bf16[8,2,160,128]{3,2,1,0:T(8,128)(2,1)} %bitcast.7), calls=%async_computation.1 | async-start | bytes 1310720 | tf_op jit(solution)/shard_map/all_to_all | solution.py:280
  94.0 0.0 all-gather.9.cloned.1.call-start
  94.1 0.7 all-gather.9.cloned.1.call-update
  94.8 4.2 %collective-permute-start.10 = (bf16[4,2,32,256]{3,2,1,0:T(8,128)(2,1)S(1)}, bf16[4,2,32,256]{3,2,1,0:T(8,128)(2,1)S(1)}, u32[]{:S(2)}, u32[]{:S(2)}) collective-permute-start(bf16[4,2,32,256]{3,2,1,0:T(8,128)(2,1)S(1)} %constant_dynamic-slice_fusion), channel_id=1, source_target_pairs={{0,512},{128,640},{256,768},{384,896},{512,0},{640,128},{768,256},... | collective-permute-start | bytes 393224 | tf_op jit(solution)/shard_map/ppermute | solution.py:284
  99.0 1.1 collective-permute-start.7
  100.0 4.4 %collective-permute-start.8 = (bf16[4,2,32,256]{3,2,1,0:T(8,128)(2,1)S(1)}, bf16[4,2,32,256]{3,2,1,0:T(8,128)(2,1)S(1)}, u32[]{:S(2)}, u32[]{:S(2)}) collective-permute-start(bf16[4,2,32,256]{3,2,1,0:T(8,128)(2,1)S(1)} %constant_dynamic-slice_fusion), channel_id=1, source_target_pairs={{0,768},{128,896},{256,0},{384,128},{512,256},{640,384},{768,512},... | collective-permute-start | bytes 393224 | tf_op jit(solution)/shard_map/ppermute | solution.py:284
  104.5 2.8 %collective-permute-start.9 = (bf16[4,2,32,256]{3,2,1,0:T(8,128)(2,1)S(1)}, bf16[4,2,32,256]{3,2,1,0:T(8,128)(2,1)S(1)}, u32[]{:S(2)}, u32[]{:S(2)}) collective-permute-start(bf16[4,2,32,256]{3,2,1,0:T(8,128)(2,1)S(1)} %constant_dynamic-slice_fusion), channel_id=1, source_target_pairs={{0,640},{128,768},{256,896},{384,0},{512,128},{640,256},{768,384},... | collective-permute-start | bytes 393224 | tf_op jit(solution)/shard_map/ppermute | solution.py:284
  107.3 0.2 collective-permute-done.7.refs_0_
  107.5 0.8 collective-permute-done.8.refs_1_
  108.3 4.0 %collective-permute-done.9.refs_2_ = bf16[4,2,32,256]{3,2,1,0:T(8,128)(2,1)S(1)} collective-permute-done((bf16[4,2,32,256]{3,2,1,0:T(8,128)(2,1)S(1)}, bf16[4,2,32,256]{3,2,1,0:T(8,128)(2,1)S(1)}, u32[]{:S(2)}, u32[]{:S(2)}) %collective-permute-start.9) | collective-permute-done | bytes 131104 | tf_op jit(solution)/shard_map/ppermute | solution.py:284
  112.3 1.8 shard_map.61
  114.1 6.9 %all-to-all-start.2 = ((bf16[8,2,160,128]{3,2,1,0:T(8,128)(2,1)}), bf16[8,2,160,128]{3,2,1,0:T(8,128)(2,1)S(1)}, u32[]{:S(2)}, u32[]{:S(2)}) async-start(bf16[8,2,160,128]{3,2,1,0:T(8,128)(2,1)} %get-tuple-element.27), calls=%async_computation.2 | async-start | bytes 1310720 | tf_op jit(solution)/shard_map/all_to_all | solution.py:280
  121.0 0.0 all-gather.7.cloned.1.call-start
  121.0 0.6 shard_map.64
  121.6 22.9 %all-gather.1 = bf16[8,160,128]{2,1,0:T(8,128)(2,1)} all-gather(bf16[2,160,128]{2,1,0:T(8,128)(2,1)S(1)} %shard_map.64), channel_id=3, replica_groups=mesh['x'=4,'core'=2,'zl'=4,'y'=8,'zh'=4] {'zh'}, dimensions={0}, use_global_device_ids=true | all-gather | bytes 409600 | tf_op jit(solution)/shard_map/all_gather | solution.py:355
  144.5 0.0 all-gather.7.cloned.1.call-update
  144.6 0.6 shard_map.66
  145.2 19.4 %all_to_all.30.came = bf16[16,160,128]{2,1,0:T(8,128)(2,1)S(1)} all-to-all(bf16[16,160,128]{2,1,0:T(8,128)(2,1)S(1)} %shard_map.66), channel_id=1, replica_groups=mesh['x'=4,'core'=2,'zl'=4,'y'=8,'zh'=4] {'zl'}, dimensions={0} | all-to-all | bytes 1310720 | tf_op jit(solution)/shard_map/all_to_all | solution.py:280
  164.5 0.6 shard_map.67
  165.1 19.1 %all_to_all.31.came = bf16[4,160,128]{2,1,0:T(8,128)(2,1)S(1)} all-to-all(bf16[4,160,128]{2,1,0:T(8,128)(2,1)S(1)} %shard_map.67), channel_id=1, replica_groups=mesh['x'=4,'core'=2,'zl'=4,'y'=8,'zh'=4] {'zh'}, dimensions={0} | all-to-all | bytes 327680 | tf_op jit(solution)/shard_map/all_to_all | solution.py:280
  184.2 1.3 shard_map.68
  185.5 6.8 %all-to-all-start.5 = ((bf16[8,128,128]{2,1,0:T(8,128)(2,1)}), bf16[8,128,128]{2,1,0:T(8,128)(2,1)S(1)}, u32[]{:S(2)}, u32[]{:S(2)}) async-start(bf16[8,128,128]{2,1,0:T(8,128)(2,1)} %get-tuple-element.30), calls=%async_computation.5 | async-start | bytes 524288 | tf_op jit(solution)/shard_map/all_to_all | solution.py:280
  192.4 7.5 %shard_map.65 = bf16[2,128,256]{2,1,0:T(8,128)(2,1)} custom-call(s32[43]{0:T(128)S(1)} %concatenate.3.table, bf16[8,4,2,160,128]{4,3,2,1,0:T(8,128)(2,1)} %bitcast.22, bf16[8,2,128,256]{3,2,1,0:T(8,128)(2,1)} %bitcast.24), custom_call_target="tpu_custom_call" | custom-call | tf_op jit(solution)/shard_map/pallas_call | solution.py:262
  199.9 2.4 %shard_map.69 = bf16[128,1024]{1,0:T(8,128)(2,1)} custom-call(s32[43]{0:T(128)S(1)} %concatenate.3.table, bf16[1024,1024]{1,0:T(8,128)(2,1)} %bitcast.21, bf16[640,128]{1,0:T(8,128)(2,1)S(1)} %get-tuple-element.29.band, bf16[8,128,128]{2,1,0:T(8,128)(2,1)S(1)} %all-to-all-done.5.came), custom_call_target="tpu_custom_call" | custom-call | tf_op jit(solution)/shard_map/pallas_call | solution.py:181
  (25 shorter events, 0.1 us)
Async XLA Ops:
  7.2 22.0 %copy-start = (bf16[1,2,1024,256]{3,2,1,0:T(8,128)(2,1)S(1)}, bf16[1,2,1024,256]{3,2,1,0:T(8,128)(2,1)}, u32[]{:S(2)}) copy-start(bf16[1,2,1024,256]{3,2,1,0:T(8,128)(2,1)} %param.4) | copy-start | bytes 3145732
  7.2 37.6 %copy-start.1 = (s32[64]{0:T(128)S(1)}, s32[64]{0:T(128)}, u32[]{:S(2)}) copy-start(s32[64]{0:T(128)} %param.5) | copy-start | bytes 772
  7.3 43.7 %copy-start.2 = (s32[64]{0:T(128)S(1)}, s32[64]{0:T(128)}, u32[]{:S(2)}) copy-start(s32[64]{0:T(128)} %param.6) | copy-start | bytes 772
  9.7 76.0 %all-to-all-start = ((bf16[16,160,128]{2,1,0:T(8,128)(2,1)}), bf16[16,160,128]{2,1,0:T(8,128)(2,1)S(1)}, u32[]{:S(2)}, u32[]{:S(2)}) async-start(bf16[16,160,128]{2,1,0:T(8,128)(2,1)} %shard_map.62), calls=%async_computation | async-start | bytes 1310720 | tf_op jit(solution)/shard_map/all_to_all | solution.py:280
  29.8 15.4 %collective-permute-start = (bf16[2,128,256]{2,1,0:T(8,128)(2,1)S(1)}, bf16[2,128,256]{2,1,0:T(8,128)(2,1)S(1)}, u32[]{:S(2)}, u32[]{:S(2)}) collective-permute-start(bf16[2,128,256]{2,1,0:T(8,128)(2,1)S(1)} %get-tuple-element.18), channel_id=1, source_target_pairs={{0,128},{128,256},{256,384},{384,512},{512,640},{640,768},{768,896... | collective-permute-start | bytes 393224 | tf_op jit(solution)/shard_map/ppermute | solution.py:284
  31.8 16.0 %collective-permute-start.1 = (bf16[2,128,256]{2,1,0:T(8,128)(2,1)S(1)}, bf16[2,128,256]{2,1,0:T(8,128)(2,1)S(1)}, u32[]{:S(2)}, u32[]{:S(2)}) collective-permute-start(bf16[2,128,256]{2,1,0:T(8,128)(2,1)S(1)} %get-tuple-element.19), channel_id=1, source_target_pairs={{0,256},{128,384},{256,512},{384,640},{512,768},{640,896},{768,0},... | collective-permute-start | bytes 393224 | tf_op jit(solution)/shard_map/ppermute | solution.py:284
  35.0 16.3 %collective-permute-start.2 = (bf16[2,128,256]{2,1,0:T(8,128)(2,1)S(1)}, bf16[2,128,256]{2,1,0:T(8,128)(2,1)S(1)}, u32[]{:S(2)}, u32[]{:S(2)}) collective-permute-start(bf16[2,128,256]{2,1,0:T(8,128)(2,1)S(1)} %get-tuple-element.20), channel_id=1, source_target_pairs={{0,384},{128,512},{256,640},{384,768},{512,896},{640,0},{768,128},... | collective-permute-start | bytes 393224 | tf_op jit(solution)/shard_map/ppermute | solution.py:284
  38.4 12.9 %collective-permute-start.3 = (bf16[2,128,256]{2,1,0:T(8,128)(2,1)S(1)}, bf16[2,128,256]{2,1,0:T(8,128)(2,1)S(1)}, u32[]{:S(2)}, u32[]{:S(2)}) collective-permute-start(bf16[2,128,256]{2,1,0:T(8,128)(2,1)S(1)} %get-tuple-element.21), channel_id=1, source_target_pairs={{0,512},{128,640},{256,768},{384,896},{512,0},{640,128},{768,256},... | collective-permute-start | bytes 393224 | tf_op jit(solution)/shard_map/ppermute | solution.py:284
  40.8 10.4 %collective-permute-start.4 = (bf16[2,128,256]{2,1,0:T(8,128)(2,1)S(1)}, bf16[2,128,256]{2,1,0:T(8,128)(2,1)S(1)}, u32[]{:S(2)}, u32[]{:S(2)}) collective-permute-start(bf16[2,128,256]{2,1,0:T(8,128)(2,1)S(1)} %get-tuple-element.22), channel_id=1, source_target_pairs={{0,640},{128,768},{256,896},{384,0},{512,128},{640,256},{768,384},... | collective-permute-start | bytes 393224 | tf_op jit(solution)/shard_map/ppermute | solution.py:284
  45.2 6.1 %collective-permute-start.5 = (bf16[2,128,256]{2,1,0:T(8,128)(2,1)S(1)}, bf16[2,128,256]{2,1,0:T(8,128)(2,1)S(1)}, u32[]{:S(2)}, u32[]{:S(2)}) collective-permute-start(bf16[2,128,256]{2,1,0:T(8,128)(2,1)S(1)} %get-tuple-element.23), channel_id=1, source_target_pairs={{0,768},{128,896},{256,0},{384,128},{512,256},{640,384},{768,512},... | collective-permute-start | bytes 393224 | tf_op jit(solution)/shard_map/ppermute | solution.py:284
  47.8 6.2 %collective-permute-start.6 = (bf16[2,128,256]{2,1,0:T(8,128)(2,1)S(1)}, bf16[2,128,256]{2,1,0:T(8,128)(2,1)S(1)}, u32[]{:S(2)}, u32[]{:S(2)}) collective-permute-start(bf16[2,128,256]{2,1,0:T(8,128)(2,1)S(1)} %get-tuple-element.24), channel_id=1, source_target_pairs={{0,896},{128,0},{256,128},{384,256},{512,384},{640,512},{768,640},... | collective-permute-start | bytes 393224 | tf_op jit(solution)/shard_map/ppermute | solution.py:284
  87.2 26.8 %all-to-all-start.1 = ((bf16[8,2,160,128]{3,2,1,0:T(8,128)(2,1)}), bf16[8,2,160,128]{3,2,1,0:T(8,128)(2,1)S(1)}, u32[]{:S(2)}, u32[]{:S(2)}) async-start(bf16[8,2,160,128]{3,2,1,0:T(8,128)(2,1)} %bitcast.7), calls=%async_computation.1 | async-start | bytes 1310720 | tf_op jit(solution)/shard_map/all_to_all | solution.py:280
  94.0 98.3 %all-gather.9.cloned.1.call-start = ((), (), s32[]{:S(2)}) async-start(), calls=%async_computation.7 | async-start | bytes 1179648 | tf_op jit(solution)/shard_map/all_gather | solution.py:339
  94.8 12.5 %collective-permute-start.10 = (bf16[4,2,32,256]{3,2,1,0:T(8,128)(2,1)S(1)}, bf16[4,2,32,256]{3,2,1,0:T(8,128)(2,1)S(1)}, u32[]{:S(2)}, u32[]{:S(2)}) collective-permute-start(bf16[4,2,32,256]{3,2,1,0:T(8,128)(2,1)S(1)} %constant_dynamic-slice_fusion), channel_id=1, source_target_pairs={{0,512},{128,640},{256,768},{384,896},{512,0},{640,128},{768,256},... | collective-permute-start | bytes 393224 | tf_op jit(solution)/shard_map/ppermute | solution.py:284
  99.0 8.5 %collective-permute-start.7 = (bf16[4,2,32,256]{3,2,1,0:T(8,128)(2,1)S(1)}, bf16[4,2,32,256]{3,2,1,0:T(8,128)(2,1)S(1)}, u32[]{:S(2)}, u32[]{:S(2)}) collective-permute-start(bf16[4,2,32,256]{3,2,1,0:T(8,128)(2,1)S(1)} %constant_dynamic-slice_fusion), channel_id=1, source_target_pairs={{0,896},{128,0},{256,128},{384,256},{512,384},{640,512},{768,640},... | collective-permute-start | bytes 393224 | tf_op jit(solution)/shard_map/ppermute | solution.py:284
  100.0 8.3 %collective-permute-start.8 = (bf16[4,2,32,256]{3,2,1,0:T(8,128)(2,1)S(1)}, bf16[4,2,32,256]{3,2,1,0:T(8,128)(2,1)S(1)}, u32[]{:S(2)}, u32[]{:S(2)}) collective-permute-start(bf16[4,2,32,256]{3,2,1,0:T(8,128)(2,1)S(1)} %constant_dynamic-slice_fusion), channel_id=1, source_target_pairs={{0,768},{128,896},{256,0},{384,128},{512,256},{640,384},{768,512},... | collective-permute-start | bytes 393224 | tf_op jit(solution)/shard_map/ppermute | solution.py:284
  104.5 7.8 %collective-permute-start.9 = (bf16[4,2,32,256]{3,2,1,0:T(8,128)(2,1)S(1)}, bf16[4,2,32,256]{3,2,1,0:T(8,128)(2,1)S(1)}, u32[]{:S(2)}, u32[]{:S(2)}) collective-permute-start(bf16[4,2,32,256]{3,2,1,0:T(8,128)(2,1)S(1)} %constant_dynamic-slice_fusion), channel_id=1, source_target_pairs={{0,640},{128,768},{256,896},{384,0},{512,128},{640,256},{768,384},... | collective-permute-start | bytes 393224 | tf_op jit(solution)/shard_map/ppermute | solution.py:284
  114.1 30.5 %all-to-all-start.2 = ((bf16[8,2,160,128]{3,2,1,0:T(8,128)(2,1)}), bf16[8,2,160,128]{3,2,1,0:T(8,128)(2,1)S(1)}, u32[]{:S(2)}, u32[]{:S(2)}) async-start(bf16[8,2,160,128]{3,2,1,0:T(8,128)(2,1)} %get-tuple-element.27), calls=%async_computation.2 | async-start | bytes 1310720 | tf_op jit(solution)/shard_map/all_to_all | solution.py:280
  121.0 71.4 %all-gather.7.cloned.1.call-start = ((), (), s32[]{:S(2)}) async-start(), calls=%async_computation.6 | async-start | bytes 2949120 | tf_op jit(solution)/shard_map/all_gather | solution.py:357
  185.5 14.4 %all-to-all-start.5 = ((bf16[8,128,128]{2,1,0:T(8,128)(2,1)}), bf16[8,128,128]{2,1,0:T(8,128)(2,1)S(1)}, u32[]{:S(2)}, u32[]{:S(2)}) async-start(bf16[8,128,128]{2,1,0:T(8,128)(2,1)} %get-tuple-element.30), calls=%async_computation.5 | async-start | bytes 524288 | tf_op jit(solution)/shard_map/all_to_all | solution.py:280
Sparse Core Ops, SparseCore 0:
  98.2 32.4 all-gather.8
  144.7 31.1 all-gather.6

commit v9 on v8

--- a/solution.py
+++ b/solution.py
@@ -16,7 +16,6 @@
 REP = ("x", "core")
 OWN = ("zl", "y")
 BLK = "zh"
-RING = ("zl", "zh")
 
 BIG = pltpu.CompilerParams(vmem_limit_bytes=40 * 1024 * 1024)
 SCALARS = pl.BlockSpec(memory_space=pltpu.SMEM)
@@ -46,48 +45,53 @@
     )(*ins)
 
 
-def fan_kernel(table, grads, *outs):
-    rows = outs[0].shape[1]
-    for step, out in enumerate(outs):
-        start = lax.rem(table[REP_AT] + step, BANDS) * rows
-        for block in range(out.shape[0]):
-            out[block] = grads[block, ds(start, rows, rows), :]
-
-
-def sum_kernel(table, *refs):
-    *ins, out = refs
-    total = ins[0][...].astype(jnp.float32)
-    for ref in ins[1:]:
-        total = total + ref[...].astype(jnp.float32)
+def split_kernel(table, grads, out):
+    rows = out.shape[2]
+    for band in range(out.shape[0]):
+        out[band] = grads[:, band * rows : (band + 1) * rows]
+
+
+def sum_kernel(table, parts, out):
+    total = parts[0].astype(jnp.float32)
+    for band in range(1, parts.shape[0]):
+        total = total + parts[band].astype(jnp.float32)
     out[...] = total.astype(jnp.bfloat16)
 
 
-def history_kernel(table, column, out):
+def history_kernel(table, column, *outs):
     tile = column.shape[1]
-    shards = 4
+    shards = len(outs)
     size = tile // shards
-    for step in range(STEPS):
-        start = lax.rem(table[REP_AT] + step, BANDS) * tile
-        for shard in range(shards):
-            piece = column[ds(start + shard * size, size, size), :]
-            for level in range(out.shape[0] // shards):
-                out[level * shards + shard, step * size : (step + 1) * size] = piece
-
-
-def cut_history(table, history, places, tile, shards):
+    for turn, out in enumerate(outs):
+        part = lax.rem(table[BLK_AT] + turn, shards)
+        for step in range(STEPS):
+            start = lax.rem(table[REP_AT] + step, BANDS) * tile + part * size
+            out[step * size : (step + 1) * size] = column[ds(start, size, size), :]
+
+
+def cut_history(table, history, tile, shards):
     order_full = history.shape[0]
-    shape = (places, STEPS * tile // shards, tile)
+    shape = (STEPS * tile // shards, tile)
     return pl.pallas_call(
         history_kernel,
-        out_shape=like(shape),
+        out_shape=[like(shape)] * shards,
         grid_spec=pltpu.PrefetchScalarGridSpec(
             num_scalar_prefetch=1,
             grid=(1,),
             in_specs=[pl.BlockSpec((order_full, tile), lambda i, table: (0, table[REP_AT]))],
-            out_specs=pl.BlockSpec(shape, lambda i, table: (0, 0, 0)),
+            out_specs=[pl.BlockSpec(shape, lambda i, table: (0, 0))] * shards,
         ),
         compiler_params=BIG,
     )(table, history)
+
+
+def spread_kernel(table, *refs):
+    *arrived, out = refs
+    shards = len(arrived)
+    for turn, ref in enumerate(arrived):
+        slot = lax.rem(table[BLK_AT] + shards - turn, shards)
+        for level in range(out.shape[0] // shards):
+            out[level * shards + slot] = ref[...]
 
 
 def take(table, tiles, first):
@@ -282,6 +286,13 @@
 
 def shift(array, step):
     return lax.ppermute(array, REP, [(i, (i + step) % BANDS) for i in range(BANDS)])
+
+
+def swap(parts, count):
+    return [parts[0]] + [
+        lax.ppermute(parts[turn], BLK, [(i, (i + turn) % count) for i in range(count)])
+        for turn in range(1, count)
+    ]
 
 
 def after(array, other):
@@ -329,18 +340,18 @@
     table = tables(owner_map, iterations, home_count)
     place = jnp.stack([lax.axis_index(REP), my_blk]).astype(jnp.int32)
 
-    history_ring = exchange(cut_history(place, history, ring, tile, shards), RING)
-
-    partials = call(
-        fan_kernel, [place, partial_grads[0]], [like((home_count, tile, width))] * BANDS
-    )
-    partials = [partials[0]] + [shift(partials[step], step) for step in range(1, BANDS)]
-    grad_tile = call(sum_kernel, [place, *partials], like((home_count, tile, width)))
+    outgoing = call(split_kernel, [place, partial_grads[0]], like((BANDS, home_count, tile, width)))
+    history_parts = swap(cut_history(place, history, tile, shards), shards)
+    partials = exchange(outgoing, REP)
+    grad_tile = call(sum_kernel, [place, partials], like((home_count, tile, width)))
+
+    history_sent = call(spread_kernel, [place, *history_parts], like((ring, depth, tile)))
+    history_level = exchange(after(history_sent, grad_tile), "zl")
     grad_cols = lax.all_gather(grad_tile, REP, axis=0, tiled=False)
 
     grad_band = lax.all_gather(grad_tile, BLK, axis=0, tiled=False)
 
-    history_sent = take(table, after(history_ring, grad_band), HISTORY_AT)
+    history_sent = take(table, after(history_level, grad_band), HISTORY_AT)
     history_sent = history_sent.reshape(turns, home_count, depth, tile)
     history_came = exchange(history_sent, "y")
 

time: 210 us -> 222 us (1.057)
  waiting for transfers between devices: 8.44 us -> 12.4 us
  blocking collectives: 91.8 us -> 94.9 us
    ppermute x11 -> x4, starting transfers between devices: 31.6 us -> 13 us  [shift(): lax.ppermute(array, REP, [(i, (i + step) % BANDS) for i in range(BANDS)])]
    ppermute x0 -> x3, starting transfers between devices: none -> 16.5 us  [swap(): lax.ppermute(parts[turn], BLK, [(i, (i + turn) % count) for i in range(co...]
    all_to_all x2, blocking collectives: 38.5 us -> 49.1 us  [exchange(): return lax.all_to_all(array, axis, split_axis=0, concat_axis=0, tiled=True)]
    ppermute x0 -> x3, waiting for transfers between devices: none -> 5.31 us  [swap(): lax.ppermute(parts[turn], BLK, [(i, (i + turn) % count) for i in range(co...]
    all_gather x1, blocking collectives: 30.4 us -> 25.2 us  [body(): grad_band = lax.all_gather(grad_tile, BLK, axis=0, tiled=False)]
    all_to_all x4 -> x5, starting transfers between devices: 40 us -> 44.3 us  [exchange(): return lax.all_to_all(array, axis, split_axis=0, concat_axis=0, tiled=True)]
    pallas_call x8 -> x9, Pallas kernels: 8.17 us -> 10.6 us  [call(): pl.pallas_call(kernel, out_shape=outs, in_specs=in_specs or [SCALARS] + [...]
    all_gather x1, blocking collectives: 22.9 us -> 20.7 us  [body(): stat_band = lax.all_gather(stat, BLK, axis=0, tiled=False)]
  transfers between devices with their start and end apart: 17 -> 14, of which waited for: 4 -> 4; matrix products, arithmetic and copies ran while one was open for 1% -> 1% of each run, Pallas kernels for 7% -> 7%
where the time goes in v9:
time: 222 us; the launch traced here: 221 us
  blocking collectives  94.9 us (43%)
  starting transfers between devices  73.9 us (33%)
  Pallas kernels  22 us (10%)
  between operations  14.8 us (7%)
  waiting for transfers between devices  12.4 us (6%)
  local copies, waits for them, and re-layouts  2.26 us (1%)
    all_to_all x2, blocking collectives, exchange(): return lax.all_to_all(array, axis, split_axis=0, concat_axis=0, tiled=True)  49.1 us
    all_to_all x5, starting transfers between devices, exchange(): return lax.all_to_all(array, axis, split_axis=0, concat_axis=0, tiled=True)  44.3 us
    all_gather x1, blocking collectives, body(): grad_band = lax.all_gather(grad_tile, BLK, axis=0, tiled=False)  25.2 us
    all_gather x1, blocking collectives, body(): stat_band = lax.all_gather(stat, BLK, axis=0, tiled=False)  20.7 us
    ppermute x3, starting transfers between devices, swap(): lax.ppermute(parts[turn], BLK, [(i, (i + turn) % count) for i in range(co...  16.5 us
    ppermute x4, starting transfers between devices, shift(): lax.ppermute(array, REP, [(i, (i + step) % BANDS) for i in range(BANDS)])  13 us
    pallas_call x9, Pallas kernels, call(): pl.pallas_call(kernel, out_shape=outs, in_specs=in_specs or [SCALARS] + [...  10.6 us
    pallas_call x1, Pallas kernels, newton(): pl.pallas_call(newton_kernel, out_shape=like((home_count, tile, width)),...  7.5 us
  transfers between devices with their start and end apart: 14, of which 4 were waited for; matrix products, arithmetic and copies ran while one was open for 1% of the time, Pallas kernels for 7%

profile of v9, /device:TPU:1, one launch (start us, length us, event | category | flops | bytes accessed | tf_op | source)
XLA Modules:
  0.0 220.8 jit_solution(5281606820309105866)
XLA Ops:
  7.2 0.1 pad_add_fusion.table
  7.3 1.2 copy-done
  8.5 1.6 shard_map.59
  10.1 17.6 %all-to-all-start = ((bf16[8,2,128,256]{3,2,1,0:T(8,128)(2,1)}), bf16[8,2,128,256]{3,2,1,0:T(8,128)(2,1)S(1)}, u32[]{:S(2)}, u32[]{:S(2)}) async-start(bf16[8,2,128,256]{3,2,1,0:T(8,128)(2,1)} %shard_map.59), calls=%async_computation | async-start | bytes 2097152 | tf_op jit(solution)/shard_map/all_to_all | solution.py:284
  27.7 1.5 shard_map.62
  29.2 1.9 collective-permute-start.4
  31.1 11.2 %collective-permute-start.5 = (bf16[160,128]{1,0:T(8,128)(2,1)S(1)}, bf16[160,128]{1,0:T(8,128)(2,1)S(1)}, u32[]{:S(2)}, u32[]{:S(2)}) collective-permute-start(bf16[160,128]{1,0:T(8,128)(2,1)S(1)} %get-tuple-element.17), channel_id=1, source_target_pairs={{0,2},{1,3},{2,0},{3,1},{4,6},{5,7},{6,4},{7,5},{8,10},{9,11},{10,... | collective-permute-start | bytes 122888 | tf_op jit(solution)/shard_map/ppermute | solution.py:293
  42.3 3.4 %collective-permute-start.6 = (bf16[160,128]{1,0:T(8,128)(2,1)S(1)}, bf16[160,128]{1,0:T(8,128)(2,1)S(1)}, u32[]{:S(2)}, u32[]{:S(2)}) collective-permute-start(bf16[160,128]{1,0:T(8,128)(2,1)S(1)} %get-tuple-element.18), channel_id=1, source_target_pairs={{0,3},{1,0},{2,1},{3,2},{4,7},{5,4},{6,5},{7,6},{8,11},{9,8},{10,9... | collective-permute-start | bytes 122888 | tf_op jit(solution)/shard_map/ppermute | solution.py:293
  45.7 0.0 collective-permute-done.4.refs_1_
  45.7 1.4 collective-permute-done.5.refs_2_
  47.1 3.9 %collective-permute-done.6.refs_3_ = bf16[160,128]{1,0:T(8,128)(2,1)S(1)} collective-permute-done((bf16[160,128]{1,0:T(8,128)(2,1)S(1)}, bf16[160,128]{1,0:T(8,128)(2,1)S(1)}, u32[]{:S(2)}, u32[]{:S(2)}) %collective-permute-start.6) | collective-permute-done | bytes 40992 | tf_op jit(solution)/shard_map/ppermute | solution.py:293
  51.0 1.5 shard_map.63
  52.5 1.3 shard_map.60
  53.8 5.9 %all-to-all-start.1 = ((bf16[16,160,128]{2,1,0:T(8,128)(2,1)}), bf16[16,160,128]{2,1,0:T(8,128)(2,1)S(1)}, u32[]{:S(2)}, u32[]{:S(2)}) async-start(bf16[16,160,128]{2,1,0:T(8,128)(2,1)} %shard_map.63), calls=%async_computation.1 | async-start | bytes 1310720 | tf_op jit(solution)/shard_map/all_to_all | solution.py:284
  59.8 0.2 select_reduce_fusion.1
  60.0 0.1 select_reduce_fusion
  60.1 0.1 sub.17
  60.2 0.1 reshape_squeeze.3
  60.3 0.6 dynamic_slice.24
  61.6 0.1 dynamic_slice.22
  61.6 0.1 dynamic_slice.25
  61.7 0.1 and_select_fusion.3
  61.8 0.1 concatenate.3.table
  61.9 25.2 %all-gather = bf16[8,128,256]{2,1,0:T(8,128)(2,1)S(1)} all-gather(bf16[2,128,256]{2,1,0:T(8,128)(2,1)} %shard_map.60), channel_id=2, replica_groups=mesh['x'=4,'core'=2,'zl'=4,'y'=8,'zh'=4] {'zh'}, dimensions={0}, use_global_device_ids=true | all-gather | bytes 655360 | tf_op jit(solution)/shard_map/all_gather | solution.py:352
  87.1 1.4 shard_map.64
  88.5 8.1 %all-to-all-start.2 = ((bf16[8,2,160,128]{3,2,1,0:T(8,128)(2,1)}), bf16[8,2,160,128]{3,2,1,0:T(8,128)(2,1)S(1)}, u32[]{:S(2)}, u32[]{:S(2)}) async-start(bf16[8,2,160,128]{3,2,1,0:T(8,128)(2,1)} %bitcast.7), calls=%async_computation.2 | async-start | bytes 1310720 | tf_op jit(solution)/shard_map/all_to_all | solution.py:284
  96.6 0.0 all-gather.9.cloned.1.call-start
  96.7 0.7 all-gather.9.cloned.1.call-update
  97.4 3.6 %collective-permute-start = (bf16[4,2,32,256]{3,2,1,0:T(8,128)(2,1)S(1)}, bf16[4,2,32,256]{3,2,1,0:T(8,128)(2,1)S(1)}, u32[]{:S(2)}, u32[]{:S(2)}) collective-permute-start(bf16[4,2,32,256]{3,2,1,0:T(8,128)(2,1)S(1)} %constant_dynamic-slice_fusion), channel_id=1, source_target_pairs={{0,896},{128,0},{256,128},{384,256},{512,384},{640,512},{768,640},... | collective-permute-start | bytes 393224 | tf_op jit(solution)/shard_map/ppermute | solution.py:288
  101.0 4.8 %collective-permute-start.1 = (bf16[4,2,32,256]{3,2,1,0:T(8,128)(2,1)S(1)}, bf16[4,2,32,256]{3,2,1,0:T(8,128)(2,1)S(1)}, u32[]{:S(2)}, u32[]{:S(2)}) collective-permute-start(bf16[4,2,32,256]{3,2,1,0:T(8,128)(2,1)S(1)} %constant_dynamic-slice_fusion), channel_id=1, source_target_pairs={{0,768},{128,896},{256,0},{384,128},{512,256},{640,384},{768,512},... | collective-permute-start | bytes 393224 | tf_op jit(solution)/shard_map/ppermute | solution.py:288
  105.8 2.7 %collective-permute-start.2 = (bf16[4,2,32,256]{3,2,1,0:T(8,128)(2,1)S(1)}, bf16[4,2,32,256]{3,2,1,0:T(8,128)(2,1)S(1)}, u32[]{:S(2)}, u32[]{:S(2)}) collective-permute-start(bf16[4,2,32,256]{3,2,1,0:T(8,128)(2,1)S(1)} %constant_dynamic-slice_fusion), channel_id=1, source_target_pairs={{0,640},{128,768},{256,896},{384,0},{512,128},{640,256},{768,384},... | collective-permute-start | bytes 393224 | tf_op jit(solution)/shard_map/ppermute | solution.py:288
  108.5 1.9 collective-permute-start.3
  110.4 3.2 %collective-permute-done.2.refs_2_ = bf16[4,2,32,256]{3,2,1,0:T(8,128)(2,1)S(1)} collective-permute-done((bf16[4,2,32,256]{3,2,1,0:T(8,128)(2,1)S(1)}, bf16[4,2,32,256]{3,2,1,0:T(8,128)(2,1)S(1)}, u32[]{:S(2)}, u32[]{:S(2)}) %collective-permute-start.2) | collective-permute-done | bytes 131104 | tf_op jit(solution)/shard_map/ppermute | solution.py:288
  113.6 3.2 %collective-permute-done.3.refs_3_ = bf16[4,2,32,256]{3,2,1,0:T(8,128)(2,1)S(1)} collective-permute-done((bf16[4,2,32,256]{3,2,1,0:T(8,128)(2,1)S(1)}, bf16[4,2,32,256]{3,2,1,0:T(8,128)(2,1)S(1)}, u32[]{:S(2)}, u32[]{:S(2)}) %collective-permute-start.3) | collective-permute-done | bytes 131104 | tf_op jit(solution)/shard_map/ppermute | solution.py:288
  116.8 1.7 shard_map.61
  118.5 6.9 %all-to-all-start.3 = ((bf16[8,2,160,128]{3,2,1,0:T(8,128)(2,1)}), bf16[8,2,160,128]{3,2,1,0:T(8,128)(2,1)S(1)}, u32[]{:S(2)}, u32[]{:S(2)}) async-start(bf16[8,2,160,128]{3,2,1,0:T(8,128)(2,1)} %get-tuple-element.21), calls=%async_computation.3 | async-start | bytes 1310720 | tf_op jit(solution)/shard_map/all_to_all | solution.py:284
  125.5 0.0 all-gather.7.cloned.1.call-start
  125.5 0.6 shard_map.65
  126.1 20.7 %all-gather.1 = bf16[8,160,128]{2,1,0:T(8,128)(2,1)} all-gather(bf16[2,160,128]{2,1,0:T(8,128)(2,1)S(1)} %shard_map.65), channel_id=3, replica_groups=mesh['x'=4,'core'=2,'zl'=4,'y'=8,'zh'=4] {'zh'}, dimensions={0}, use_global_device_ids=true | all-gather | bytes 409600 | tf_op jit(solution)/shard_map/all_gather | solution.py:366
  146.7 0.0 all-gather.7.cloned.1.call-update
  146.8 0.6 shard_map.67
  147.4 28.8 %all_to_all.35.came = bf16[16,160,128]{2,1,0:T(8,128)(2,1)S(1)} all-to-all(bf16[16,160,128]{2,1,0:T(8,128)(2,1)S(1)} %shard_map.67), channel_id=1, replica_groups=mesh['x'=4,'core'=2,'zl'=4,'y'=8,'zh'=4] {'zl'}, dimensions={0} | all-to-all | bytes 1310720 | tf_op jit(solution)/shard_map/all_to_all | solution.py:284
  176.1 0.6 shard_map.68
  176.7 20.3 %all_to_all.36.came = bf16[4,160,128]{2,1,0:T(8,128)(2,1)S(1)} all-to-all(bf16[4,160,128]{2,1,0:T(8,128)(2,1)S(1)} %shard_map.68), channel_id=1, replica_groups=mesh['x'=4,'core'=2,'zl'=4,'y'=8,'zh'=4] {'zh'}, dimensions={0} | all-to-all | bytes 327680 | tf_op jit(solution)/shard_map/all_to_all | solution.py:284
  197.0 1.3 shard_map.69
  198.3 5.8 %all-to-all-start.6 = ((bf16[8,128,128]{2,1,0:T(8,128)(2,1)}), bf16[8,128,128]{2,1,0:T(8,128)(2,1)S(1)}, u32[]{:S(2)}, u32[]{:S(2)}) async-start(bf16[8,128,128]{2,1,0:T(8,128)(2,1)} %get-tuple-element.24), calls=%async_computation.6 | async-start | bytes 524288 | tf_op jit(solution)/shard_map/all_to_all | solution.py:284
  204.1 7.5 %shard_map.66 = bf16[2,128,256]{2,1,0:T(8,128)(2,1)} custom-call(s32[43]{0:T(128)S(1)} %concatenate.3.table, bf16[8,4,2,160,128]{4,3,2,1,0:T(8,128)(2,1)} %bitcast.22, bf16[8,2,128,256]{3,2,1,0:T(8,128)(2,1)} %bitcast.24), custom_call_target="tpu_custom_call" | custom-call | tf_op jit(solution)/shard_map/pallas_call | solution.py:266
  211.6 2.4 %shard_map.70 = bf16[128,1024]{1,0:T(8,128)(2,1)} custom-call(s32[43]{0:T(128)S(1)} %concatenate.3.table, bf16[1024,1024]{1,0:T(8,128)(2,1)} %bitcast.21, bf16[640,128]{1,0:T(8,128)(2,1)S(1)} %get-tuple-element.23.band, bf16[8,128,128]{2,1,0:T(8,128)(2,1)S(1)} %all-to-all-done.6.came), custom_call_target="tpu_custom_call" | custom-call | tf_op jit(solution)/shard_map/pallas_call | solution.py:185
  (20 shorter events, 0.1 us)
Async XLA Ops:
  7.2 1.2 copy-start
  10.1 42.4 %all-to-all-start = ((bf16[8,2,128,256]{3,2,1,0:T(8,128)(2,1)}), bf16[8,2,128,256]{3,2,1,0:T(8,128)(2,1)S(1)}, u32[]{:S(2)}, u32[]{:S(2)}) async-start(bf16[8,2,128,256]{3,2,1,0:T(8,128)(2,1)} %shard_map.59), calls=%async_computation | async-start | bytes 2097152 | tf_op jit(solution)/shard_map/all_to_all | solution.py:284
  27.7 32.1 %copy-start.1 = (s32[64]{0:T(128)S(1)}, s32[64]{0:T(128)}, u32[]{:S(2)}) copy-start(s32[64]{0:T(128)} %param.5) | copy-start | bytes 772
  27.7 33.9 %copy-start.2 = (s32[64]{0:T(128)S(1)}, s32[64]{0:T(128)}, u32[]{:S(2)}) copy-start(s32[64]{0:T(128)} %param.6) | copy-start | bytes 772
  29.2 16.5 %collective-permute-start.4 = (bf16[160,128]{1,0:T(8,128)(2,1)S(1)}, bf16[160,128]{1,0:T(8,128)(2,1)S(1)}, u32[]{:S(2)}, u32[]{:S(2)}) collective-permute-start(bf16[160,128]{1,0:T(8,128)(2,1)S(1)} %get-tuple-element.16), channel_id=1, source_target_pairs={{0,1},{1,2},{2,3},{3,0},{4,5},{5,6},{6,7},{7,4},{8,9},{9,10},{10,1... | collective-permute-start | bytes 122888 | tf_op jit(solution)/shard_map/ppermute | solution.py:293
  31.1 16.0 %collective-permute-start.5 = (bf16[160,128]{1,0:T(8,128)(2,1)S(1)}, bf16[160,128]{1,0:T(8,128)(2,1)S(1)}, u32[]{:S(2)}, u32[]{:S(2)}) collective-permute-start(bf16[160,128]{1,0:T(8,128)(2,1)S(1)} %get-tuple-element.17), channel_id=1, source_target_pairs={{0,2},{1,3},{2,0},{3,1},{4,6},{5,7},{6,4},{7,5},{8,10},{9,11},{10,... | collective-permute-start | bytes 122888 | tf_op jit(solution)/shard_map/ppermute | solution.py:293
  42.3 8.7 %collective-permute-start.6 = (bf16[160,128]{1,0:T(8,128)(2,1)S(1)}, bf16[160,128]{1,0:T(8,128)(2,1)S(1)}, u32[]{:S(2)}, u32[]{:S(2)}) collective-permute-start(bf16[160,128]{1,0:T(8,128)(2,1)S(1)} %get-tuple-element.18), channel_id=1, source_target_pairs={{0,3},{1,0},{2,1},{3,2},{4,7},{5,4},{6,5},{7,6},{8,11},{9,8},{10,9... | collective-permute-start | bytes 122888 | tf_op jit(solution)/shard_map/ppermute | solution.py:293
  53.8 33.2 %all-to-all-start.1 = ((bf16[16,160,128]{2,1,0:T(8,128)(2,1)}), bf16[16,160,128]{2,1,0:T(8,128)(2,1)S(1)}, u32[]{:S(2)}, u32[]{:S(2)}) async-start(bf16[16,160,128]{2,1,0:T(8,128)(2,1)} %shard_map.63), calls=%async_computation.1 | async-start | bytes 1310720 | tf_op jit(solution)/shard_map/all_to_all | solution.py:284
  88.5 30.0 %all-to-all-start.2 = ((bf16[8,2,160,128]{3,2,1,0:T(8,128)(2,1)}), bf16[8,2,160,128]{3,2,1,0:T(8,128)(2,1)S(1)}, u32[]{:S(2)}, u32[]{:S(2)}) async-start(bf16[8,2,160,128]{3,2,1,0:T(8,128)(2,1)} %bitcast.7), calls=%async_computation.2 | async-start | bytes 1310720 | tf_op jit(solution)/shard_map/all_to_all | solution.py:284
  96.6 107.5 %all-gather.9.cloned.1.call-start = ((), (), s32[]{:S(2)}) async-start(), calls=%async_computation.8 | async-start | bytes 1179648 | tf_op jit(solution)/shard_map/all_gather | solution.py:350
  97.4 13.0 %collective-permute-start = (bf16[4,2,32,256]{3,2,1,0:T(8,128)(2,1)S(1)}, bf16[4,2,32,256]{3,2,1,0:T(8,128)(2,1)S(1)}, u32[]{:S(2)}, u32[]{:S(2)}) collective-permute-start(bf16[4,2,32,256]{3,2,1,0:T(8,128)(2,1)S(1)} %constant_dynamic-slice_fusion), channel_id=1, source_target_pairs={{0,896},{128,0},{256,128},{384,256},{512,384},{640,512},{768,640},... | collective-permute-start | bytes 393224 | tf_op jit(solution)/shard_map/ppermute | solution.py:288
  101.0 9.5 %collective-permute-start.1 = (bf16[4,2,32,256]{3,2,1,0:T(8,128)(2,1)S(1)}, bf16[4,2,32,256]{3,2,1,0:T(8,128)(2,1)S(1)}, u32[]{:S(2)}, u32[]{:S(2)}) collective-permute-start(bf16[4,2,32,256]{3,2,1,0:T(8,128)(2,1)S(1)} %constant_dynamic-slice_fusion), channel_id=1, source_target_pairs={{0,768},{128,896},{256,0},{384,128},{512,256},{640,384},{768,512},... | collective-permute-start | bytes 393224 | tf_op jit(solution)/shard_map/ppermute | solution.py:288
  105.8 7.8 %collective-permute-start.2 = (bf16[4,2,32,256]{3,2,1,0:T(8,128)(2,1)S(1)}, bf16[4,2,32,256]{3,2,1,0:T(8,128)(2,1)S(1)}, u32[]{:S(2)}, u32[]{:S(2)}) collective-permute-start(bf16[4,2,32,256]{3,2,1,0:T(8,128)(2,1)S(1)} %constant_dynamic-slice_fusion), channel_id=1, source_target_pairs={{0,640},{128,768},{256,896},{384,0},{512,128},{640,256},{768,384},... | collective-permute-start | bytes 393224 | tf_op jit(solution)/shard_map/ppermute | solution.py:288
  108.5 8.3 %collective-permute-start.3 = (bf16[4,2,32,256]{3,2,1,0:T(8,128)(2,1)S(1)}, bf16[4,2,32,256]{3,2,1,0:T(8,128)(2,1)S(1)}, u32[]{:S(2)}, u32[]{:S(2)}) collective-permute-start(bf16[4,2,32,256]{3,2,1,0:T(8,128)(2,1)S(1)} %constant_dynamic-slice_fusion), channel_id=1, source_target_pairs={{0,512},{128,640},{256,768},{384,896},{512,0},{640,128},{768,256},... | collective-permute-start | bytes 393224 | tf_op jit(solution)/shard_map/ppermute | solution.py:288
  118.5 28.2 %all-to-all-start.3 = ((bf16[8,2,160,128]{3,2,1,0:T(8,128)(2,1)}), bf16[8,2,160,128]{3,2,1,0:T(8,128)(2,1)S(1)}, u32[]{:S(2)}, u32[]{:S(2)}) async-start(bf16[8,2,160,128]{3,2,1,0:T(8,128)(2,1)} %get-tuple-element.21), calls=%async_computation.3 | async-start | bytes 1310720 | tf_op jit(solution)/shard_map/all_to_all | solution.py:284
  125.5 78.6 %all-gather.7.cloned.1.call-start = ((), (), s32[]{:S(2)}) async-start(), calls=%async_computation.7 | async-start | bytes 2949120 | tf_op jit(solution)/shard_map/all_gather | solution.py:368
  198.3 13.3 %all-to-all-start.6 = ((bf16[8,128,128]{2,1,0:T(8,128)(2,1)}), bf16[8,128,128]{2,1,0:T(8,128)(2,1)S(1)}, u32[]{:S(2)}, u32[]{:S(2)}) async-start(bf16[8,128,128]{2,1,0:T(8,128)(2,1)} %get-tuple-element.24), calls=%async_computation.6 | async-start | bytes 524288 | tf_op jit(solution)/shard_map/all_to_all | solution.py:284
Sparse Core Ops, SparseCore 0:
  100.8 43.5 all-gather.8
  147.1 42.6 all-gather.6

commit v10 on v8

--- a/solution.py
+++ b/solution.py
@@ -46,12 +46,19 @@
     )(*ins)
 
 
-def fan_kernel(table, grads, *outs):
-    rows = outs[0].shape[1]
+def fan_kernel(table, grads, kept, sent):
+    pairs, _, rows, _ = kept.shape
+    pair, core = lax.div(table[REP_AT], 2), lax.rem(table[REP_AT], 2)
+    for step in range(pairs):
+        first = lax.rem(pair + step, pairs) * 2
+        kept[step] = grads[:, ds((first + core) * rows, rows, rows), :]
+        sent[step] = grads[:, ds((first + 1 - core) * rows, rows, rows), :]
+
+
+def pair_kernel(table, kept, came, *outs):
     for step, out in enumerate(outs):
-        start = lax.rem(table[REP_AT] + step, BANDS) * rows
-        for block in range(out.shape[0]):
-            out[block] = grads[block, ds(start, rows, rows), :]
+        total = kept[step].astype(jnp.float32) + came[step].astype(jnp.float32)
+        out[...] = total.astype(jnp.bfloat16)
 
 
 def sum_kernel(table, *refs):
@@ -329,12 +336,18 @@
     table = tables(owner_map, iterations, home_count)
     place = jnp.stack([lax.axis_index(REP), my_blk]).astype(jnp.int32)
 
-    history_ring = exchange(cut_history(place, history, ring, tile, shards), RING)
-
-    partials = call(
-        fan_kernel, [place, partial_grads[0]], [like((home_count, tile, width))] * BANDS
-    )
-    partials = [partials[0]] + [shift(partials[step], step) for step in range(1, BANDS)]
+    pairs = lax.axis_size("x")
+    half = like((pairs, home_count, tile, width))
+    kept, sent = call(fan_kernel, [place, partial_grads[0]], [half, half])
+    came = lax.ppermute(sent, "core", [(0, 1), (1, 0)])
+
+    history_ring = exchange(cut_history(after(place, sent), history, ring, tile, shards), RING)
+
+    chip = call(pair_kernel, [place, kept, came], [like((home_count, tile, width))] * pairs)
+    partials = [chip[0]] + [
+        lax.ppermute(chip[step], "x", [(i, (i + step) % pairs) for i in range(pairs)])
+        for step in range(1, pairs)
+    ]
     grad_tile = call(sum_kernel, [place, *partials], like((home_count, tile, width)))
     grad_cols = lax.all_gather(grad_tile, REP, axis=0, tiled=False)
 

time: 210 us -> 211 us (level)
  starting transfers between devices: 71.7 us -> 67 us
  blocking collectives: 91.8 us -> 94.9 us
    ppermute x11 -> x4, starting transfers between devices: 31.6 us -> 13.6 us  [shift(): lax.ppermute(array, REP, [(i, (i + step) % BANDS) for i in range(BANDS)])]
    ppermute x0 -> x4, starting transfers between devices: none -> 13.4 us  [the longest x3 10.5 us: body(): lax.ppermute(chip[step], 'x', [(i, (i + step) % pairs) for i in range(pai...]
    all_gather x1, blocking collectives: 30.4 us -> 33.2 us  [body(): grad_band = lax.all_gather(grad_tile, BLK, axis=0, tiled=False)]
    all_to_all x2, blocking collectives: 38.5 us -> 41 us  [exchange(): return lax.all_to_all(array, axis, split_axis=0, concat_axis=0, tiled=True)]
    ppermute x0 -> x4, waiting for transfers between devices: none -> 2.38 us  [the longest x3 1.31 us: body(): lax.ppermute(chip[step], 'x', [(i, (i + step) % pairs) for i in range(pai...]
    all_gather x1, blocking collectives: 22.9 us -> 20.7 us  [body(): stat_band = lax.all_gather(stat, BLK, axis=0, tiled=False)]
    ppermute x11 -> x4, waiting for transfers between devices: 7.73 us -> 6.12 us  [shift(): lax.ppermute(array, REP, [(i, (i + step) % BANDS) for i in range(BANDS)])]
    pallas_call x8 -> x9, Pallas kernels: 8.17 us -> 8.75 us  [call(): pl.pallas_call(kernel, out_shape=outs, in_specs=in_specs or [SCALARS] + [...]
  transfers between devices with their start and end apart: 17 -> 14, of which waited for: 4 -> 5; matrix products, arithmetic and copies ran while one was open for 1% -> 1% of each run, Pallas kernels for 7% -> 7%
where the time goes in v10:
time: 211 us; the launch traced here: 210 us
  blocking collectives  94.9 us (45%)
  starting transfers between devices  67 us (32%)
  Pallas kernels  21.1 us (10%)
  between operations  14.8 us (7%)
  waiting for transfers between devices  9.22 us (4%)
  local copies, waits for them, and re-layouts  2.25 us (1%)
    all_to_all x2, blocking collectives, exchange(): return lax.all_to_all(array, axis, split_axis=0, concat_axis=0, tiled=True)  41 us
    all_to_all x4, starting transfers between devices, exchange(): return lax.all_to_all(array, axis, split_axis=0, concat_axis=0, tiled=True)  39.9 us
    all_gather x1, blocking collectives, body(): grad_band = lax.all_gather(grad_tile, BLK, axis=0, tiled=False)  33.2 us
    all_gather x1, blocking collectives, body(): stat_band = lax.all_gather(stat, BLK, axis=0, tiled=False)  20.7 us
    ppermute x4, starting transfers between devices, shift(): lax.ppermute(array, REP, [(i, (i + step) % BANDS) for i in range(BANDS)])  13.6 us
    ppermute x3, starting transfers between devices, body(): lax.ppermute(chip[step], 'x', [(i, (i + step) % pairs) for i in range(pai...  10.5 us
    pallas_call x9, Pallas kernels, call(): pl.pallas_call(kernel, out_shape=outs, in_specs=in_specs or [SCALARS] + [...  8.75 us
    pallas_call x1, Pallas kernels, newton(): pl.pallas_call(newton_kernel, out_shape=like((home_count, tile, width)),...  7.51 us
  transfers between devices with their start and end apart: 14, of which 5 were waited for; matrix products, arithmetic and copies ran while one was open for 1% of the time, Pallas kernels for 7%

profile of v10, /device:TPU:1, one launch (start us, length us, event | category | flops | bytes accessed | tf_op | source)
XLA Modules:
  0.0 209.8 jit_solution(18381867227515653410)
XLA Ops:
  7.2 0.1 pad_add_fusion.table
  7.3 1.2 copy-done
  8.5 0.6 shard_map.59
  9.1 2.4 %shard_map.63 = bf16[16,160,128]{2,1,0:T(8,128)(2,1)} custom-call(s32[2]{0:T(128)S(1)} %pad_add_fusion.table, bf16[1024,1024]{1,0:T(8,128)(2,1)} %bitcast.20), custom_call_target="tpu_custom_call" | custom-call | tf_op jit(solution)/shard_map/pallas_call | solution.py:87
  11.6 19.4 %all-to-all-start = ((bf16[16,160,128]{2,1,0:T(8,128)(2,1)}), bf16[16,160,128]{2,1,0:T(8,128)(2,1)S(1)}, u32[]{:S(2)}, u32[]{:S(2)}) async-start(bf16[16,160,128]{2,1,0:T(8,128)(2,1)} %shard_map.63), calls=%async_computation | async-start | bytes 1310720 | tf_op jit(solution)/shard_map/all_to_all | solution.py:287
  31.0 2.9 %collective-permute-start = (bf16[4,2,128,256]{3,2,1,0:T(8,128)(2,1)S(1)}, bf16[4,2,128,256]{3,2,1,0:T(8,128)(2,1)S(1)}, u32[]{:S(2)}, u32[]{:S(2)}) collective-permute-start(bf16[4,2,128,256]{3,2,1,0:T(8,128)(2,1)S(1)} %get-tuple-element.17), channel_id=1, source_target_pairs={{0,128},{128,0},{1,129},{129,1},{2,130},{130,2},{3,131},{131,3},{4... | collective-permute-start | bytes 1572872 | tf_op jit(solution)/shard_map/ppermute | solution.py:342
  33.9 0.2 select_reduce_fusion.1
  34.1 0.1 select_reduce_fusion
  34.2 0.1 sub.17
  34.3 1.1 collective-permute-done.came
  35.4 0.7 shard_map.60
  36.0 3.1 %collective-permute-start.1 = (bf16[2,128,256]{2,1,0:T(8,128)(2,1)S(1)}, bf16[2,128,256]{2,1,0:T(8,128)(2,1)S(1)}, u32[]{:S(2)}, u32[]{:S(2)}) collective-permute-start(bf16[2,128,256]{2,1,0:T(8,128)(2,1)S(1)} %get-tuple-element.19), channel_id=1, source_target_pairs={{0,256},{256,512},{512,768},{768,0},{1,257},{257,513},{513,769},{7... | collective-permute-start | bytes 393224 | tf_op jit(solution)/shard_map/ppermute | solution.py:348
  39.2 4.4 %collective-permute-start.2 = (bf16[2,128,256]{2,1,0:T(8,128)(2,1)S(1)}, bf16[2,128,256]{2,1,0:T(8,128)(2,1)S(1)}, u32[]{:S(2)}, u32[]{:S(2)}) collective-permute-start(bf16[2,128,256]{2,1,0:T(8,128)(2,1)S(1)} %get-tuple-element.20), channel_id=1, source_target_pairs={{0,512},{256,768},{512,0},{768,256},{1,513},{257,769},{513,1},{769... | collective-permute-start | bytes 393224 | tf_op jit(solution)/shard_map/ppermute | solution.py:348
  43.5 3.1 %collective-permute-start.3 = (bf16[2,128,256]{2,1,0:T(8,128)(2,1)S(1)}, bf16[2,128,256]{2,1,0:T(8,128)(2,1)S(1)}, u32[]{:S(2)}, u32[]{:S(2)}) collective-permute-start(bf16[2,128,256]{2,1,0:T(8,128)(2,1)S(1)} %get-tuple-element.21), channel_id=1, source_target_pairs={{0,768},{256,0},{512,256},{768,512},{1,769},{257,1},{513,257},{769... | collective-permute-start | bytes 393224 | tf_op jit(solution)/shard_map/ppermute | solution.py:348
  46.6 0.1 and_select_fusion.3
  46.7 0.1 dynamic_slice.22
  46.8 0.1 reshape_squeeze.3
  46.9 0.1 dynamic_slice.25
  47.0 0.6 dynamic_slice.24
  48.1 0.1 concatenate.3.table
  48.2 1.3 collective-permute-done.3.refs_3_
  49.5 1.3 shard_map.61
  50.8 33.2 %all-gather = bf16[8,128,256]{2,1,0:T(8,128)(2,1)S(1)} all-gather(bf16[2,128,256]{2,1,0:T(8,128)(2,1)} %shard_map.61), channel_id=2, replica_groups=mesh['x'=4,'core'=2,'zl'=4,'y'=8,'zh'=4] {'zh'}, dimensions={0}, use_global_device_ids=true | all-gather | bytes 655360 | tf_op jit(solution)/shard_map/all_gather | solution.py:354
  84.0 1.4 shard_map.64
  85.5 6.8 %all-to-all-start.1 = ((bf16[8,2,160,128]{3,2,1,0:T(8,128)(2,1)}), bf16[8,2,160,128]{3,2,1,0:T(8,128)(2,1)S(1)}, u32[]{:S(2)}, u32[]{:S(2)}) async-start(bf16[8,2,160,128]{3,2,1,0:T(8,128)(2,1)} %bitcast.7), calls=%async_computation.1 | async-start | bytes 1310720 | tf_op jit(solution)/shard_map/all_to_all | solution.py:287
  92.3 0.0 all-gather.9.cloned.1.call-start
  92.3 0.7 all-gather.9.cloned.1.call-update
  93.0 5.8 %collective-permute-start.7 = (bf16[4,2,32,256]{3,2,1,0:T(8,128)(2,1)S(1)}, bf16[4,2,32,256]{3,2,1,0:T(8,128)(2,1)S(1)}, u32[]{:S(2)}, u32[]{:S(2)}) collective-permute-start(bf16[4,2,32,256]{3,2,1,0:T(8,128)(2,1)S(1)} %constant_dynamic-slice_fusion), channel_id=1, source_target_pairs={{0,512},{128,640},{256,768},{384,896},{512,0},{640,128},{768,256},... | collective-permute-start | bytes 393224 | tf_op jit(solution)/shard_map/ppermute | solution.py:291
  98.8 5.5 %collective-permute-start.6 = (bf16[4,2,32,256]{3,2,1,0:T(8,128)(2,1)S(1)}, bf16[4,2,32,256]{3,2,1,0:T(8,128)(2,1)S(1)}, u32[]{:S(2)}, u32[]{:S(2)}) collective-permute-start(bf16[4,2,32,256]{3,2,1,0:T(8,128)(2,1)S(1)} %constant_dynamic-slice_fusion), channel_id=1, source_target_pairs={{0,640},{128,768},{256,896},{384,0},{512,128},{640,256},{768,384},... | collective-permute-start | bytes 393224 | tf_op jit(solution)/shard_map/ppermute | solution.py:291
  104.4 1.9 collective-permute-start.5
  106.3 0.4 collective-permute-start.4
  106.7 0.8 collective-permute-done.6.refs_2_
  107.5 4.2 %collective-permute-done.5.refs_1_ = bf16[4,2,32,256]{3,2,1,0:T(8,128)(2,1)S(1)} collective-permute-done((bf16[4,2,32,256]{3,2,1,0:T(8,128)(2,1)S(1)}, bf16[4,2,32,256]{3,2,1,0:T(8,128)(2,1)S(1)}, u32[]{:S(2)}, u32[]{:S(2)}) %collective-permute-start.5) | collective-permute-done | bytes 131104 | tf_op jit(solution)/shard_map/ppermute | solution.py:291
  111.7 1.1 collective-permute-done.4.refs_0_
  112.8 1.8 shard_map.62
  114.6 6.6 %all-to-all-start.2 = ((bf16[8,2,160,128]{3,2,1,0:T(8,128)(2,1)}), bf16[8,2,160,128]{3,2,1,0:T(8,128)(2,1)S(1)}, u32[]{:S(2)}, u32[]{:S(2)}) async-start(bf16[8,2,160,128]{3,2,1,0:T(8,128)(2,1)} %get-tuple-element.25), calls=%async_computation.2 | async-start | bytes 1310720 | tf_op jit(solution)/shard_map/all_to_all | solution.py:287
  121.2 0.0 all-gather.7.cloned.1.call-start
  121.3 0.6 shard_map.65
  121.8 20.7 %all-gather.1 = bf16[8,160,128]{2,1,0:T(8,128)(2,1)} all-gather(bf16[2,160,128]{2,1,0:T(8,128)(2,1)S(1)} %shard_map.65), channel_id=3, replica_groups=mesh['x'=4,'core'=2,'zl'=4,'y'=8,'zh'=4] {'zh'}, dimensions={0}, use_global_device_ids=true | all-gather | bytes 409600 | tf_op jit(solution)/shard_map/all_gather | solution.py:368
  142.5 0.0 all-gather.7.cloned.1.call-update
  142.6 0.6 shard_map.67
  143.1 21.2 %all_to_all.30.came = bf16[16,160,128]{2,1,0:T(8,128)(2,1)S(1)} all-to-all(bf16[16,160,128]{2,1,0:T(8,128)(2,1)S(1)} %shard_map.67), channel_id=1, replica_groups=mesh['x'=4,'core'=2,'zl'=4,'y'=8,'zh'=4] {'zl'}, dimensions={0} | all-to-all | bytes 1310720 | tf_op jit(solution)/shard_map/all_to_all | solution.py:287
  164.4 0.6 shard_map.68
  164.9 19.8 %all_to_all.31.came = bf16[4,160,128]{2,1,0:T(8,128)(2,1)S(1)} all-to-all(bf16[4,160,128]{2,1,0:T(8,128)(2,1)S(1)} %shard_map.68), channel_id=1, replica_groups=mesh['x'=4,'core'=2,'zl'=4,'y'=8,'zh'=4] {'zh'}, dimensions={0} | all-to-all | bytes 327680 | tf_op jit(solution)/shard_map/all_to_all | solution.py:287
  184.7 1.3 shard_map.69
  186.0 7.0 %all-to-all-start.5 = ((bf16[8,128,128]{2,1,0:T(8,128)(2,1)}), bf16[8,128,128]{2,1,0:T(8,128)(2,1)S(1)}, u32[]{:S(2)}, u32[]{:S(2)}) async-start(bf16[8,128,128]{2,1,0:T(8,128)(2,1)} %get-tuple-element.28), calls=%async_computation.5 | async-start | bytes 524288 | tf_op jit(solution)/shard_map/all_to_all | solution.py:287
  193.1 7.5 %shard_map.66 = bf16[2,128,256]{2,1,0:T(8,128)(2,1)} custom-call(s32[43]{0:T(128)S(1)} %concatenate.3.table, bf16[8,4,2,160,128]{4,3,2,1,0:T(8,128)(2,1)} %bitcast.22, bf16[8,2,128,256]{3,2,1,0:T(8,128)(2,1)} %bitcast.24), custom_call_target="tpu_custom_call" | custom-call | tf_op jit(solution)/shard_map/pallas_call | solution.py:269
  200.6 2.4 %shard_map.70 = bf16[128,1024]{1,0:T(8,128)(2,1)} custom-call(s32[43]{0:T(128)S(1)} %concatenate.3.table, bf16[1024,1024]{1,0:T(8,128)(2,1)} %bitcast.21, bf16[640,128]{1,0:T(8,128)(2,1)S(1)} %get-tuple-element.27.band, bf16[8,128,128]{2,1,0:T(8,128)(2,1)S(1)} %all-to-all-done.5.came), custom_call_target="tpu_custom_call" | custom-call | tf_op jit(solution)/shard_map/pallas_call | solution.py:188
  (20 shorter events, 0.1 us)
Async XLA Ops:
  7.2 26.7 %copy-start.1 = (s32[64]{0:T(128)S(1)}, s32[64]{0:T(128)}, u32[]{:S(2)}) copy-start(s32[64]{0:T(128)} %param.5) | copy-start | bytes 772
  7.3 1.2 copy-start
  9.1 37.6 %copy-start.2 = (s32[64]{0:T(128)S(1)}, s32[64]{0:T(128)}, u32[]{:S(2)}) copy-start(s32[64]{0:T(128)} %param.6) | copy-start | bytes 772
  11.6 72.5 %all-to-all-start = ((bf16[16,160,128]{2,1,0:T(8,128)(2,1)}), bf16[16,160,128]{2,1,0:T(8,128)(2,1)S(1)}, u32[]{:S(2)}, u32[]{:S(2)}) async-start(bf16[16,160,128]{2,1,0:T(8,128)(2,1)} %shard_map.63), calls=%async_computation | async-start | bytes 1310720 | tf_op jit(solution)/shard_map/all_to_all | solution.py:287
  31.0 4.4 %collective-permute-start = (bf16[4,2,128,256]{3,2,1,0:T(8,128)(2,1)S(1)}, bf16[4,2,128,256]{3,2,1,0:T(8,128)(2,1)S(1)}, u32[]{:S(2)}, u32[]{:S(2)}) collective-permute-start(bf16[4,2,128,256]{3,2,1,0:T(8,128)(2,1)S(1)} %get-tuple-element.17), channel_id=1, source_target_pairs={{0,128},{128,0},{1,129},{129,1},{2,130},{130,2},{3,131},{131,3},{4... | collective-permute-start | bytes 1572872 | tf_op jit(solution)/shard_map/ppermute | solution.py:342
  36.0 12.2 %collective-permute-start.1 = (bf16[2,128,256]{2,1,0:T(8,128)(2,1)S(1)}, bf16[2,128,256]{2,1,0:T(8,128)(2,1)S(1)}, u32[]{:S(2)}, u32[]{:S(2)}) collective-permute-start(bf16[2,128,256]{2,1,0:T(8,128)(2,1)S(1)} %get-tuple-element.19), channel_id=1, source_target_pairs={{0,256},{256,512},{512,768},{768,0},{1,257},{257,513},{513,769},{7... | collective-permute-start | bytes 393224 | tf_op jit(solution)/shard_map/ppermute | solution.py:348
  39.2 9.1 %collective-permute-start.2 = (bf16[2,128,256]{2,1,0:T(8,128)(2,1)S(1)}, bf16[2,128,256]{2,1,0:T(8,128)(2,1)S(1)}, u32[]{:S(2)}, u32[]{:S(2)}) collective-permute-start(bf16[2,128,256]{2,1,0:T(8,128)(2,1)S(1)} %get-tuple-element.20), channel_id=1, source_target_pairs={{0,512},{256,768},{512,0},{768,256},{1,513},{257,769},{513,1},{769... | collective-permute-start | bytes 393224 | tf_op jit(solution)/shard_map/ppermute | solution.py:348
  43.5 6.0 %collective-permute-start.3 = (bf16[2,128,256]{2,1,0:T(8,128)(2,1)S(1)}, bf16[2,128,256]{2,1,0:T(8,128)(2,1)S(1)}, u32[]{:S(2)}, u32[]{:S(2)}) collective-permute-start(bf16[2,128,256]{2,1,0:T(8,128)(2,1)S(1)} %get-tuple-element.21), channel_id=1, source_target_pairs={{0,768},{256,0},{512,256},{768,512},{1,769},{257,1},{513,257},{769... | collective-permute-start | bytes 393224 | tf_op jit(solution)/shard_map/ppermute | solution.py:348
  85.5 29.1 %all-to-all-start.1 = ((bf16[8,2,160,128]{3,2,1,0:T(8,128)(2,1)}), bf16[8,2,160,128]{3,2,1,0:T(8,128)(2,1)S(1)}, u32[]{:S(2)}, u32[]{:S(2)}) async-start(bf16[8,2,160,128]{3,2,1,0:T(8,128)(2,1)} %bitcast.7), calls=%async_computation.1 | async-start | bytes 1310720 | tf_op jit(solution)/shard_map/all_to_all | solution.py:287
  92.3 100.8 %all-gather.9.cloned.1.call-start = ((), (), s32[]{:S(2)}) async-start(), calls=%async_computation.7 | async-start | bytes 1179648 | tf_op jit(solution)/shard_map/all_gather | solution.py:352
  93.0 13.7 %collective-permute-start.7 = (bf16[4,2,32,256]{3,2,1,0:T(8,128)(2,1)S(1)}, bf16[4,2,32,256]{3,2,1,0:T(8,128)(2,1)S(1)}, u32[]{:S(2)}, u32[]{:S(2)}) collective-permute-start(bf16[4,2,32,256]{3,2,1,0:T(8,128)(2,1)S(1)} %constant_dynamic-slice_fusion), channel_id=1, source_target_pairs={{0,512},{128,640},{256,768},{384,896},{512,0},{640,128},{768,256},... | collective-permute-start | bytes 393224 | tf_op jit(solution)/shard_map/ppermute | solution.py:291
  98.8 8.6 %collective-permute-start.6 = (bf16[4,2,32,256]{3,2,1,0:T(8,128)(2,1)S(1)}, bf16[4,2,32,256]{3,2,1,0:T(8,128)(2,1)S(1)}, u32[]{:S(2)}, u32[]{:S(2)}) collective-permute-start(bf16[4,2,32,256]{3,2,1,0:T(8,128)(2,1)S(1)} %constant_dynamic-slice_fusion), channel_id=1, source_target_pairs={{0,640},{128,768},{256,896},{384,0},{512,128},{640,256},{768,384},... | collective-permute-start | bytes 393224 | tf_op jit(solution)/shard_map/ppermute | solution.py:291
  104.4 7.3 %collective-permute-start.5 = (bf16[4,2,32,256]{3,2,1,0:T(8,128)(2,1)S(1)}, bf16[4,2,32,256]{3,2,1,0:T(8,128)(2,1)S(1)}, u32[]{:S(2)}, u32[]{:S(2)}) collective-permute-start(bf16[4,2,32,256]{3,2,1,0:T(8,128)(2,1)S(1)} %constant_dynamic-slice_fusion), channel_id=1, source_target_pairs={{0,768},{128,896},{256,0},{384,128},{512,256},{640,384},{768,512},... | collective-permute-start | bytes 393224 | tf_op jit(solution)/shard_map/ppermute | solution.py:291
  106.3 6.5 %collective-permute-start.4 = (bf16[4,2,32,256]{3,2,1,0:T(8,128)(2,1)S(1)}, bf16[4,2,32,256]{3,2,1,0:T(8,128)(2,1)S(1)}, u32[]{:S(2)}, u32[]{:S(2)}) collective-permute-start(bf16[4,2,32,256]{3,2,1,0:T(8,128)(2,1)S(1)} %constant_dynamic-slice_fusion), channel_id=1, source_target_pairs={{0,896},{128,0},{256,128},{384,256},{512,384},{640,512},{768,640},... | collective-permute-start | bytes 393224 | tf_op jit(solution)/shard_map/ppermute | solution.py:291
  114.6 27.9 %all-to-all-start.2 = ((bf16[8,2,160,128]{3,2,1,0:T(8,128)(2,1)}), bf16[8,2,160,128]{3,2,1,0:T(8,128)(2,1)S(1)}, u32[]{:S(2)}, u32[]{:S(2)}) async-start(bf16[8,2,160,128]{3,2,1,0:T(8,128)(2,1)} %get-tuple-element.25), calls=%async_computation.2 | async-start | bytes 1310720 | tf_op jit(solution)/shard_map/all_to_all | solution.py:287
  121.2 71.8 %all-gather.7.cloned.1.call-start = ((), (), s32[]{:S(2)}) async-start(), calls=%async_computation.6 | async-start | bytes 2949120 | tf_op jit(solution)/shard_map/all_gather | solution.py:370
  186.0 14.6 %all-to-all-start.5 = ((bf16[8,128,128]{2,1,0:T(8,128)(2,1)}), bf16[8,128,128]{2,1,0:T(8,128)(2,1)S(1)}, u32[]{:S(2)}, u32[]{:S(2)}) async-start(bf16[8,128,128]{2,1,0:T(8,128)(2,1)} %get-tuple-element.28), calls=%async_computation.5 | async-start | bytes 524288 | tf_op jit(solution)/shard_map/all_to_all | solution.py:287
Sparse Core Ops, SparseCore 0:
  96.4 33.6 all-gather.8
  142.7 33.8 all-gather.6

commit v11 on v10

--- a/solution.py
+++ b/solution.py
@@ -16,7 +16,6 @@
 REP = ("x", "core")
 OWN = ("zl", "y")
 BLK = "zh"
-RING = ("zl", "zh")
 
 BIG = pltpu.CompilerParams(vmem_limit_bytes=40 * 1024 * 1024)
 SCALARS = pl.BlockSpec(memory_space=pltpu.SMEM)
@@ -70,20 +69,18 @@
 
 
 def history_kernel(table, column, out):
-    tile = column.shape[1]
-    shards = 4
+    shards, _, tile = out.shape
     size = tile // shards
     for step in range(STEPS):
         start = lax.rem(table[REP_AT] + step, BANDS) * tile
         for shard in range(shards):
             piece = column[ds(start + shard * size, size, size), :]
-            for level in range(out.shape[0] // shards):
-                out[level * shards + shard, step * size : (step + 1) * size] = piece
-
-
-def cut_history(table, history, places, tile, shards):
+            out[shard, step * size : (step + 1) * size] = piece
+
+
+def cut_history(table, history, tile, shards):
     order_full = history.shape[0]
-    shape = (places, STEPS * tile // shards, tile)
+    shape = (shards, STEPS * tile // shards, tile)
     return pl.pallas_call(
         history_kernel,
         out_shape=like(shape),
@@ -326,13 +323,14 @@
 
 def body(partial_grads, owner_map, iterations, slot_history):
     turns, shards = lax.axis_size("y"), lax.axis_size(BLK)
-    ring = lax.axis_size("zl") * shards
+    levels = lax.axis_size("zl")
+    ring = levels * shards
     my_blk = lax.axis_index(BLK)
     _, home_count, order_full, width = partial_grads.shape
     tile = order_full // BANDS
     size = tile // shards
     depth = STEPS * size
-    history = pltpu.with_memory_space_constraint(slot_history[0, 0], pltpu.HBM)
+    history = slot_history[0, 0]
     table = tables(owner_map, iterations, home_count)
     place = jnp.stack([lax.axis_index(REP), my_blk]).astype(jnp.int32)
 
@@ -341,7 +339,8 @@
     kept, sent = call(fan_kernel, [place, partial_grads[0]], [half, half])
     came = lax.ppermute(sent, "core", [(0, 1), (1, 0)])
 
-    history_ring = exchange(cut_history(after(place, sent), history, ring, tile, shards), RING)
+    history_there = pltpu.with_memory_space_constraint(history, pltpu.HBM)
+    history_parts = exchange(cut_history(place, history_there, tile, shards), BLK)
 
     chip = call(pair_kernel, [place, kept, came], [like((home_count, tile, width))] * pairs)
     partials = [chip[0]] + [
@@ -349,11 +348,16 @@
         for step in range(1, pairs)
     ]
     grad_tile = call(sum_kernel, [place, *partials], like((home_count, tile, width)))
+
+    history_parts = after(history_parts, grad_tile)
+    history_sent = jnp.broadcast_to(history_parts[None], (levels,) + history_parts.shape)
+    history_level = exchange(history_sent.reshape(ring, depth, tile), "zl")
+
     grad_cols = lax.all_gather(grad_tile, REP, axis=0, tiled=False)
 
     grad_band = lax.all_gather(grad_tile, BLK, axis=0, tiled=False)
 
-    history_sent = take(table, after(history_ring, grad_band), HISTORY_AT)
+    history_sent = take(table, after(history_level, grad_band), HISTORY_AT)
     history_sent = history_sent.reshape(turns, home_count, depth, tile)
     history_came = exchange(history_sent, "y")
 

time: 211 us -> 216 us (1.024)
  starting transfers between devices: 67 us -> 75.7 us
    ppermute x1, starting transfers between devices: 2.86 us -> 16.1 us  [body(): came = lax.ppermute(sent, 'core', [(0, 1), (1, 0)])]
    all_to_all x2, blocking collectives: 41 us -> 51.4 us  [exchange(): return lax.all_to_all(array, axis, split_axis=0, concat_axis=0, tiled=True)]
    all_to_all x4 -> x5, starting transfers between devices: 39.9 us -> 30.7 us  [exchange(): return lax.all_to_all(array, axis, split_axis=0, concat_axis=0, tiled=True)]
    all_gather x1, blocking collectives: 33.2 us -> 24 us  [body(): grad_band = lax.all_gather(grad_tile, BLK, axis=0, tiled=False)]
    ppermute x4, starting transfers between devices: 13.6 us -> 18.4 us  [shift(): lax.ppermute(array, REP, [(i, (i + step) % BANDS) for i in range(BANDS)])]
    all_gather x1, blocking collectives: 20.7 us -> 17.5 us  [body(): stat_band = lax.all_gather(stat, BLK, axis=0, tiled=False)]
  transfers between devices with their start and end apart: 14 -> 15, of which waited for: 5 -> 5; matrix products, arithmetic and copies ran while one was open for 1% -> 1% of each run, Pallas kernels for 7% -> 8%
where the time goes in v11:
time: 216 us
  blocking collectives  92.9 us (43%)
  starting transfers between devices  75.7 us (35%)
  Pallas kernels  19.9 us (9%)
  between operations  14.9 us (7%)
  waiting for transfers between devices  8.49 us (4%)
  local copies, waits for them, and re-layouts  3.2 us (1%)
    all_to_all x2, blocking collectives, exchange(): return lax.all_to_all(array, axis, split_axis=0, concat_axis=0, tiled=True)  51.4 us
    all_to_all x5, starting transfers between devices, exchange(): return lax.all_to_all(array, axis, split_axis=0, concat_axis=0, tiled=True)  30.7 us
    all_gather x1, blocking collectives, body(): grad_band = lax.all_gather(grad_tile, BLK, axis=0, tiled=False)  24 us
    ppermute x4, starting transfers between devices, shift(): lax.ppermute(array, REP, [(i, (i + step) % BANDS) for i in range(BANDS)])  18.4 us
    all_gather x1, blocking collectives, body(): stat_band = lax.all_gather(stat, BLK, axis=0, tiled=False)  17.5 us
    ppermute x1, starting transfers between devices, body(): came = lax.ppermute(sent, 'core', [(0, 1), (1, 0)])  16.1 us
    ppermute x3, starting transfers between devices, body(): lax.ppermute(chip[step], 'x', [(i, (i + step) % pairs) for i in range(pai...  10.5 us
    pallas_call x9, Pallas kernels, call(): pl.pallas_call(kernel, out_shape=outs, in_specs=in_specs or [SCALARS] + [...  8.76 us
  transfers between devices with their start and end apart: 15, of which 5 were waited for; matrix products, arithmetic and copies ran while one was open for 1% of the time, Pallas kernels for 8%

profile of v11, /device:TPU:1, one launch (start us, length us, event | category | flops | bytes accessed | tf_op | source)
XLA Modules:
  0.0 215.6 jit_solution(244859147347040189)
XLA Ops:
  7.2 0.1 pad_add_fusion.table
  7.3 1.2 copy-done.1
  8.5 0.6 shard_map.59
  9.1 16.1 %collective-permute-start = (bf16[4,2,128,256]{3,2,1,0:T(8,128)(2,1)S(1)}, bf16[4,2,128,256]{3,2,1,0:T(8,128)(2,1)S(1)}, u32[]{:S(2)}, u32[]{:S(2)}) collective-permute-start(bf16[4,2,128,256]{3,2,1,0:T(8,128)(2,1)S(1)} %get-tuple-element.17), channel_id=1, source_target_pairs={{0,128},{128,0},{1,129},{129,1},{2,130},{130,2},{3,131},{131,3},{4... | collective-permute-start | bytes 1572872 | tf_op jit(solution)/shard_map/ppermute | solution.py:340
  25.2 2.2 %shard_map.63 = bf16[4,160,128]{2,1,0:T(8,128)(2,1)} custom-call(s32[2]{0:T(128)S(1)} %pad_add_fusion.table, bf16[1024,1024]{1,0:T(8,128)(2,1)} %bitcast.17), custom_call_target="tpu_custom_call" | custom-call | tf_op jit(solution)/shard_map/pallas_call | solution.py:84
  27.4 5.9 %all-to-all-start = ((bf16[4,160,128]{2,1,0:T(8,128)(2,1)}), bf16[4,160,128]{2,1,0:T(8,128)(2,1)S(1)}, u32[]{:S(2)}, u32[]{:S(2)}) async-start(bf16[4,160,128]{2,1,0:T(8,128)(2,1)} %shard_map.63), calls=%async_computation | async-start | bytes 327680 | tf_op jit(solution)/shard_map/all_to_all | solution.py:284
  33.3 0.7 shard_map.60
  34.0 3.1 %collective-permute-start.1 = (bf16[2,128,256]{2,1,0:T(8,128)(2,1)S(1)}, bf16[2,128,256]{2,1,0:T(8,128)(2,1)S(1)}, u32[]{:S(2)}, u32[]{:S(2)}) collective-permute-start(bf16[2,128,256]{2,1,0:T(8,128)(2,1)S(1)} %get-tuple-element.19), channel_id=1, source_target_pairs={{0,256},{256,512},{512,768},{768,0},{1,257},{257,513},{513,769},{7... | collective-permute-start | bytes 393224 | tf_op jit(solution)/shard_map/ppermute | solution.py:347
  37.1 4.4 %collective-permute-start.2 = (bf16[2,128,256]{2,1,0:T(8,128)(2,1)S(1)}, bf16[2,128,256]{2,1,0:T(8,128)(2,1)S(1)}, u32[]{:S(2)}, u32[]{:S(2)}) collective-permute-start(bf16[2,128,256]{2,1,0:T(8,128)(2,1)S(1)} %get-tuple-element.20), channel_id=1, source_target_pairs={{0,512},{256,768},{512,0},{768,256},{1,513},{257,769},{513,1},{769... | collective-permute-start | bytes 393224 | tf_op jit(solution)/shard_map/ppermute | solution.py:347
  41.4 3.1 %collective-permute-start.3 = (bf16[2,128,256]{2,1,0:T(8,128)(2,1)S(1)}, bf16[2,128,256]{2,1,0:T(8,128)(2,1)S(1)}, u32[]{:S(2)}, u32[]{:S(2)}) collective-permute-start(bf16[2,128,256]{2,1,0:T(8,128)(2,1)S(1)} %get-tuple-element.21), channel_id=1, source_target_pairs={{0,768},{256,0},{512,256},{768,512},{1,769},{257,1},{513,257},{769... | collective-permute-start | bytes 393224 | tf_op jit(solution)/shard_map/ppermute | solution.py:347
  44.5 1.2 collective-permute-done.2.refs_2_
  45.7 1.8 collective-permute-done.3.refs_3_
  47.5 1.3 shard_map.61
  48.8 0.9 broadcast_in_dim.44
  49.7 4.3 %all-to-all-start.1 = ((bf16[16,160,128]{2,1,0:T(8,128)(2,1)}), bf16[16,160,128]{2,1,0:T(8,128)(2,1)S(1)}, u32[]{:S(2)}, u32[]{:S(2)}) async-start(bf16[16,160,128]{2,1,0:T(8,128)(2,1)} %bitcast.7), calls=%async_computation.1 | async-start | bytes 1310720 | tf_op jit(solution)/shard_map/all_to_all | solution.py:284
  54.0 0.2 select_reduce_fusion.1
  54.2 0.1 select_reduce_fusion
  54.3 0.1 sub.17
  54.4 0.1 reshape_squeeze.3
  54.5 0.6 dynamic_slice.24
  55.8 0.1 dynamic_slice.22
  55.9 0.1 dynamic_slice.25
  56.0 0.1 and_select_fusion.3
  56.0 0.1 concatenate.3.table
  56.1 24.0 %all-gather = bf16[8,128,256]{2,1,0:T(8,128)(2,1)S(1)} all-gather(bf16[2,128,256]{2,1,0:T(8,128)(2,1)} %shard_map.61), channel_id=2, replica_groups=mesh['x'=4,'core'=2,'zl'=4,'y'=8,'zh'=4] {'zh'}, dimensions={0}, use_global_device_ids=true | all-gather | bytes 655360 | tf_op jit(solution)/shard_map/all_gather | solution.py:358
  80.1 1.5 shard_map.64
  81.6 6.8 %all-to-all-start.2 = ((bf16[8,2,160,128]{3,2,1,0:T(8,128)(2,1)}), bf16[8,2,160,128]{3,2,1,0:T(8,128)(2,1)S(1)}, u32[]{:S(2)}, u32[]{:S(2)}) async-start(bf16[8,2,160,128]{3,2,1,0:T(8,128)(2,1)} %bitcast.8), calls=%async_computation.2 | async-start | bytes 1310720 | tf_op jit(solution)/shard_map/all_to_all | solution.py:284
  88.5 0.7 all-gather.9.cloned.1.call-update
  89.2 9.0 %collective-permute-start.4 = (bf16[4,2,32,256]{3,2,1,0:T(8,128)(2,1)S(1)}, bf16[4,2,32,256]{3,2,1,0:T(8,128)(2,1)S(1)}, u32[]{:S(2)}, u32[]{:S(2)}) collective-permute-start(bf16[4,2,32,256]{3,2,1,0:T(8,128)(2,1)S(1)} %constant_dynamic-slice_fusion), channel_id=1, source_target_pairs={{0,896},{128,0},{256,128},{384,256},{512,384},{640,512},{768,640},... | collective-permute-start | bytes 393224 | tf_op jit(solution)/shard_map/ppermute | solution.py:288
  98.2 4.3 %collective-permute-start.5 = (bf16[4,2,32,256]{3,2,1,0:T(8,128)(2,1)S(1)}, bf16[4,2,32,256]{3,2,1,0:T(8,128)(2,1)S(1)}, u32[]{:S(2)}, u32[]{:S(2)}) collective-permute-start(bf16[4,2,32,256]{3,2,1,0:T(8,128)(2,1)S(1)} %constant_dynamic-slice_fusion), channel_id=1, source_target_pairs={{0,768},{128,896},{256,0},{384,128},{512,256},{640,384},{768,512},... | collective-permute-start | bytes 393224 | tf_op jit(solution)/shard_map/ppermute | solution.py:288
  102.4 2.5 %collective-permute-start.6 = (bf16[4,2,32,256]{3,2,1,0:T(8,128)(2,1)S(1)}, bf16[4,2,32,256]{3,2,1,0:T(8,128)(2,1)S(1)}, u32[]{:S(2)}, u32[]{:S(2)}) collective-permute-start(bf16[4,2,32,256]{3,2,1,0:T(8,128)(2,1)S(1)} %constant_dynamic-slice_fusion), channel_id=1, source_target_pairs={{0,640},{128,768},{256,896},{384,0},{512,128},{640,256},{768,384},... | collective-permute-start | bytes 393224 | tf_op jit(solution)/shard_map/ppermute | solution.py:288
  105.0 2.6 %collective-permute-start.7 = (bf16[4,2,32,256]{3,2,1,0:T(8,128)(2,1)S(1)}, bf16[4,2,32,256]{3,2,1,0:T(8,128)(2,1)S(1)}, u32[]{:S(2)}, u32[]{:S(2)}) collective-permute-start(bf16[4,2,32,256]{3,2,1,0:T(8,128)(2,1)S(1)} %constant_dynamic-slice_fusion), channel_id=1, source_target_pairs={{0,512},{128,640},{256,768},{384,896},{512,0},{640,128},{768,256},... | collective-permute-start | bytes 393224 | tf_op jit(solution)/shard_map/ppermute | solution.py:288
  107.6 2.9 %collective-permute-done.6.refs_2_ = bf16[4,2,32,256]{3,2,1,0:T(8,128)(2,1)S(1)} collective-permute-done((bf16[4,2,32,256]{3,2,1,0:T(8,128)(2,1)S(1)}, bf16[4,2,32,256]{3,2,1,0:T(8,128)(2,1)S(1)}, u32[]{:S(2)}, u32[]{:S(2)}) %collective-permute-start.6) | collective-permute-done | bytes 131104 | tf_op jit(solution)/shard_map/ppermute | solution.py:288
  110.5 1.7 collective-permute-done.7.refs_3_
  112.2 1.7 shard_map.62
  114.0 6.9 %all-to-all-start.3 = ((bf16[8,2,160,128]{3,2,1,0:T(8,128)(2,1)}), bf16[8,2,160,128]{3,2,1,0:T(8,128)(2,1)S(1)}, u32[]{:S(2)}, u32[]{:S(2)}) async-start(bf16[8,2,160,128]{3,2,1,0:T(8,128)(2,1)} %get-tuple-element.25), calls=%async_computation.3 | async-start | bytes 1310720 | tf_op jit(solution)/shard_map/all_to_all | solution.py:284
  120.9 0.0 all-gather.7.cloned.1.call-start
  120.9 0.6 shard_map.65
  121.5 17.5 %all-gather.1 = bf16[8,160,128]{2,1,0:T(8,128)(2,1)} all-gather(bf16[2,160,128]{2,1,0:T(8,128)(2,1)S(1)} %shard_map.65), channel_id=3, replica_groups=mesh['x'=4,'core'=2,'zl'=4,'y'=8,'zh'=4] {'zh'}, dimensions={0}, use_global_device_ids=true | all-gather | bytes 409600 | tf_op jit(solution)/shard_map/all_gather | solution.py:372
  139.0 0.2 all-to-all-done.3
  139.2 0.6 shard_map.67
  139.8 31.3 %all_to_all.35.came = bf16[16,160,128]{2,1,0:T(8,128)(2,1)S(1)} all-to-all(bf16[16,160,128]{2,1,0:T(8,128)(2,1)S(1)} %shard_map.67), channel_id=1, replica_groups=mesh['x'=4,'core'=2,'zl'=4,'y'=8,'zh'=4] {'zl'}, dimensions={0} | all-to-all | bytes 1310720 | tf_op jit(solution)/shard_map/all_to_all | solution.py:284
  171.1 0.6 shard_map.68
  171.6 20.1 %all_to_all.36.came = bf16[4,160,128]{2,1,0:T(8,128)(2,1)S(1)} all-to-all(bf16[4,160,128]{2,1,0:T(8,128)(2,1)S(1)} %shard_map.68), channel_id=1, replica_groups=mesh['x'=4,'core'=2,'zl'=4,'y'=8,'zh'=4] {'zh'}, dimensions={0} | all-to-all | bytes 327680 | tf_op jit(solution)/shard_map/all_to_all | solution.py:284
  191.8 1.3 shard_map.69
  193.1 6.7 %all-to-all-start.6 = ((bf16[8,128,128]{2,1,0:T(8,128)(2,1)}), bf16[8,128,128]{2,1,0:T(8,128)(2,1)S(1)}, u32[]{:S(2)}, u32[]{:S(2)}) async-start(bf16[8,128,128]{2,1,0:T(8,128)(2,1)} %get-tuple-element.28), calls=%async_computation.6 | async-start | bytes 524288 | tf_op jit(solution)/shard_map/all_to_all | solution.py:284
  199.8 7.5 %shard_map.66 = bf16[2,128,256]{2,1,0:T(8,128)(2,1)} custom-call(s32[43]{0:T(128)S(1)} %concatenate.3.table, bf16[8,4,2,160,128]{4,3,2,1,0:T(8,128)(2,1)} %bitcast.23, bf16[8,2,128,256]{3,2,1,0:T(8,128)(2,1)} %bitcast.25), custom_call_target="tpu_custom_call" | custom-call | tf_op jit(solution)/shard_map/pallas_call | solution.py:266
  207.3 1.4 shard_map.70
  (25 shorter events, 0.2 us)
Async XLA Ops:
  7.2 1.2 copy-start.1
  9.1 24.2 %collective-permute-start = (bf16[4,2,128,256]{3,2,1,0:T(8,128)(2,1)S(1)}, bf16[4,2,128,256]{3,2,1,0:T(8,128)(2,1)S(1)}, u32[]{:S(2)}, u32[]{:S(2)}) collective-permute-start(bf16[4,2,128,256]{3,2,1,0:T(8,128)(2,1)S(1)} %get-tuple-element.17), channel_id=1, source_target_pairs={{0,128},{128,0},{1,129},{129,1},{2,130},{130,2},{3,131},{131,3},{4... | collective-permute-start | bytes 1572872 | tf_op jit(solution)/shard_map/ppermute | solution.py:340
  27.4 26.6 %copy-start.2 = (s32[64]{0:T(128)S(1)}, s32[64]{0:T(128)}, u32[]{:S(2)}) copy-start(s32[64]{0:T(128)} %param.5) | copy-start | bytes 772
  27.4 28.4 %copy-start.3 = (s32[64]{0:T(128)S(1)}, s32[64]{0:T(128)}, u32[]{:S(2)}) copy-start(s32[64]{0:T(128)} %param.6) | copy-start | bytes 772
  27.4 21.4 %all-to-all-start = ((bf16[4,160,128]{2,1,0:T(8,128)(2,1)}), bf16[4,160,128]{2,1,0:T(8,128)(2,1)S(1)}, u32[]{:S(2)}, u32[]{:S(2)}) async-start(bf16[4,160,128]{2,1,0:T(8,128)(2,1)} %shard_map.63), calls=%async_computation | async-start | bytes 327680 | tf_op jit(solution)/shard_map/all_to_all | solution.py:284
  34.0 10.6 %collective-permute-start.1 = (bf16[2,128,256]{2,1,0:T(8,128)(2,1)S(1)}, bf16[2,128,256]{2,1,0:T(8,128)(2,1)S(1)}, u32[]{:S(2)}, u32[]{:S(2)}) collective-permute-start(bf16[2,128,256]{2,1,0:T(8,128)(2,1)S(1)} %get-tuple-element.19), channel_id=1, source_target_pairs={{0,256},{256,512},{512,768},{768,0},{1,257},{257,513},{513,769},{7... | collective-permute-start | bytes 393224 | tf_op jit(solution)/shard_map/ppermute | solution.py:347
  37.1 8.6 %collective-permute-start.2 = (bf16[2,128,256]{2,1,0:T(8,128)(2,1)S(1)}, bf16[2,128,256]{2,1,0:T(8,128)(2,1)S(1)}, u32[]{:S(2)}, u32[]{:S(2)}) collective-permute-start(bf16[2,128,256]{2,1,0:T(8,128)(2,1)S(1)} %get-tuple-element.20), channel_id=1, source_target_pairs={{0,512},{256,768},{512,0},{768,256},{1,513},{257,769},{513,1},{769... | collective-permute-start | bytes 393224 | tf_op jit(solution)/shard_map/ppermute | solution.py:347
  41.4 6.1 %collective-permute-start.3 = (bf16[2,128,256]{2,1,0:T(8,128)(2,1)S(1)}, bf16[2,128,256]{2,1,0:T(8,128)(2,1)S(1)}, u32[]{:S(2)}, u32[]{:S(2)}) collective-permute-start(bf16[2,128,256]{2,1,0:T(8,128)(2,1)S(1)} %get-tuple-element.21), channel_id=1, source_target_pairs={{0,768},{256,0},{512,256},{768,512},{1,769},{257,1},{513,257},{769... | collective-permute-start | bytes 393224 | tf_op jit(solution)/shard_map/ppermute | solution.py:347
  49.7 30.4 %all-to-all-start.1 = ((bf16[16,160,128]{2,1,0:T(8,128)(2,1)}), bf16[16,160,128]{2,1,0:T(8,128)(2,1)S(1)}, u32[]{:S(2)}, u32[]{:S(2)}) async-start(bf16[16,160,128]{2,1,0:T(8,128)(2,1)} %bitcast.7), calls=%async_computation.1 | async-start | bytes 1310720 | tf_op jit(solution)/shard_map/all_to_all | solution.py:284
  81.6 32.4 %all-to-all-start.2 = ((bf16[8,2,160,128]{3,2,1,0:T(8,128)(2,1)}), bf16[8,2,160,128]{3,2,1,0:T(8,128)(2,1)S(1)}, u32[]{:S(2)}, u32[]{:S(2)}) async-start(bf16[8,2,160,128]{3,2,1,0:T(8,128)(2,1)} %bitcast.8), calls=%async_computation.2 | async-start | bytes 1310720 | tf_op jit(solution)/shard_map/all_to_all | solution.py:284
  88.4 111.4 %all-gather.9.cloned.1.call-start = ((), (), s32[]{:S(2)}) async-start(), calls=%async_computation.8 | async-start | bytes 1179648 | tf_op jit(solution)/shard_map/all_gather | solution.py:356
  89.2 18.4 %collective-permute-start.4 = (bf16[4,2,32,256]{3,2,1,0:T(8,128)(2,1)S(1)}, bf16[4,2,32,256]{3,2,1,0:T(8,128)(2,1)S(1)}, u32[]{:S(2)}, u32[]{:S(2)}) collective-permute-start(bf16[4,2,32,256]{3,2,1,0:T(8,128)(2,1)S(1)} %constant_dynamic-slice_fusion), channel_id=1, source_target_pairs={{0,896},{128,0},{256,128},{384,256},{512,384},{640,512},{768,640},... | collective-permute-start | bytes 393224 | tf_op jit(solution)/shard_map/ppermute | solution.py:288
  98.2 9.4 %collective-permute-start.5 = (bf16[4,2,32,256]{3,2,1,0:T(8,128)(2,1)S(1)}, bf16[4,2,32,256]{3,2,1,0:T(8,128)(2,1)S(1)}, u32[]{:S(2)}, u32[]{:S(2)}) collective-permute-start(bf16[4,2,32,256]{3,2,1,0:T(8,128)(2,1)S(1)} %constant_dynamic-slice_fusion), channel_id=1, source_target_pairs={{0,768},{128,896},{256,0},{384,128},{512,256},{640,384},{768,512},... | collective-permute-start | bytes 393224 | tf_op jit(solution)/shard_map/ppermute | solution.py:288
  102.4 8.1 %collective-permute-start.6 = (bf16[4,2,32,256]{3,2,1,0:T(8,128)(2,1)S(1)}, bf16[4,2,32,256]{3,2,1,0:T(8,128)(2,1)S(1)}, u32[]{:S(2)}, u32[]{:S(2)}) collective-permute-start(bf16[4,2,32,256]{3,2,1,0:T(8,128)(2,1)S(1)} %constant_dynamic-slice_fusion), channel_id=1, source_target_pairs={{0,640},{128,768},{256,896},{384,0},{512,128},{640,256},{768,384},... | collective-permute-start | bytes 393224 | tf_op jit(solution)/shard_map/ppermute | solution.py:288
  105.0 7.2 %collective-permute-start.7 = (bf16[4,2,32,256]{3,2,1,0:T(8,128)(2,1)S(1)}, bf16[4,2,32,256]{3,2,1,0:T(8,128)(2,1)S(1)}, u32[]{:S(2)}, u32[]{:S(2)}) collective-permute-start(bf16[4,2,32,256]{3,2,1,0:T(8,128)(2,1)S(1)} %constant_dynamic-slice_fusion), channel_id=1, source_target_pairs={{0,512},{128,640},{256,768},{384,896},{512,0},{640,128},{768,256},... | collective-permute-start | bytes 393224 | tf_op jit(solution)/shard_map/ppermute | solution.py:288
  114.0 25.2 %all-to-all-start.3 = ((bf16[8,2,160,128]{3,2,1,0:T(8,128)(2,1)}), bf16[8,2,160,128]{3,2,1,0:T(8,128)(2,1)S(1)}, u32[]{:S(2)}, u32[]{:S(2)}) async-start(bf16[8,2,160,128]{3,2,1,0:T(8,128)(2,1)} %get-tuple-element.25), calls=%async_computation.3 | async-start | bytes 1310720 | tf_op jit(solution)/shard_map/all_to_all | solution.py:284
  120.9 78.9 %all-gather.7.cloned.1.call-start = ((), (), s32[]{:S(2)}) async-start(), calls=%async_computation.7 | async-start | bytes 2949120 | tf_op jit(solution)/shard_map/all_gather | solution.py:374
  171.1 36.3 %copy-start = (bf16[1,1,1024,1024]{3,2,1,0:T(8,128)(2,1)S(1)}, bf16[1,1,1024,1024]{3,2,1,0:T(8,128)(2,1)}, u32[]{:S(2)}) copy-start(bf16[1,1,1024,1024]{3,2,1,0:T(8,128)(2,1)} %param.7) | copy-start | bytes 6291460
  193.1 14.3 %all-to-all-start.6 = ((bf16[8,128,128]{2,1,0:T(8,128)(2,1)}), bf16[8,128,128]{2,1,0:T(8,128)(2,1)S(1)}, u32[]{:S(2)}, u32[]{:S(2)}) async-start(bf16[8,128,128]{2,1,0:T(8,128)(2,1)} %get-tuple-element.28), calls=%async_computation.6 | async-start | bytes 524288 | tf_op jit(solution)/shard_map/all_to_all | solution.py:284
Sparse Core Ops, SparseCore 0:
  92.6 48.6 all-gather.8
  143.9 42.2 all-gather.6

commit v12 on v10

--- a/solution.py
+++ b/solution.py
@@ -332,7 +332,8 @@
     tile = order_full // BANDS
     size = tile // shards
     depth = STEPS * size
-    history = pltpu.with_memory_space_constraint(slot_history[0, 0], pltpu.HBM)
+    history = slot_history[0, 0]
+    history_there = pltpu.with_memory_space_constraint(history, pltpu.HBM)
     table = tables(owner_map, iterations, home_count)
     place = jnp.stack([lax.axis_index(REP), my_blk]).astype(jnp.int32)
 
@@ -341,7 +342,7 @@
     kept, sent = call(fan_kernel, [place, partial_grads[0]], [half, half])
     came = lax.ppermute(sent, "core", [(0, 1), (1, 0)])
 
-    history_ring = exchange(cut_history(after(place, sent), history, ring, tile, shards), RING)
+    history_ring = exchange(cut_history(place, history_there, ring, tile, shards), RING)
 
     chip = call(pair_kernel, [place, kept, came], [like((home_count, tile, width))] * pairs)
     partials = [chip[0]] + [

time: 211 us -> 204 us (0.967)
    all_to_all x2, blocking collectives: 41 us -> 38.3 us  [exchange(): return lax.all_to_all(array, axis, split_axis=0, concat_axis=0, tiled=True)]
  transfers between devices with their start and end apart: 14 -> 14, of which waited for: 5 -> 4; matrix products, arithmetic and copies ran while one was open for 1% -> 1% of each run, Pallas kernels for 7% -> 7%
where the time goes in v12:
time: 204 us; the launch traced here: 203 us
  blocking collectives  93.1 us (46%)
  starting transfers between devices  66 us (32%)
  Pallas kernels  20.1 us (10%)
  between operations  15 us (7%)
  waiting for transfers between devices  7.35 us (4%)
    all_to_all x4, starting transfers between devices, exchange(): return lax.all_to_all(array, axis, split_axis=0, concat_axis=0, tiled=True)  40.7 us
    all_to_all x2, blocking collectives, exchange(): return lax.all_to_all(array, axis, split_axis=0, concat_axis=0, tiled=True)  38.3 us
    all_gather x1, blocking collectives, body(): grad_band = lax.all_gather(grad_tile, BLK, axis=0, tiled=False)  33.8 us
    all_gather x1, blocking collectives, body(): stat_band = lax.all_gather(stat, BLK, axis=0, tiled=False)  21 us
    ppermute x4, starting transfers between devices, shift(): lax.ppermute(array, REP, [(i, (i + step) % BANDS) for i in range(BANDS)])  11.8 us
    ppermute x3, starting transfers between devices, body(): lax.ppermute(chip[step], 'x', [(i, (i + step) % pairs) for i in range(pai...  10.5 us
    pallas_call x9, Pallas kernels, call(): pl.pallas_call(kernel, out_shape=outs, in_specs=in_specs or [SCALARS] + [...  8.76 us
    pallas_call x1, Pallas kernels, newton(): pl.pallas_call(newton_kernel, out_shape=like((home_count, tile, width)),...  7.5 us
  transfers between devices with their start and end apart: 14, of which 4 were waited for; matrix products, arithmetic and copies ran while one was open for 1% of the time, Pallas kernels for 7%

profile of v12, /device:TPU:1, one launch (start us, length us, event | category | flops | bytes accessed | tf_op | source)
XLA Modules:
  0.0 203.1 jit_solution(9019057806045607326)
XLA Ops:
  7.2 0.1 pad_add_fusion.table
  7.3 2.4 %shard_map.63 = bf16[16,160,128]{2,1,0:T(8,128)(2,1)} custom-call(s32[2]{0:T(128)S(1)} %pad_add_fusion.table, bf16[1024,1024]{1,0:T(8,128)(2,1)} %bitcast.16), custom_call_target="tpu_custom_call" | custom-call | tf_op jit(solution)/shard_map/pallas_call | solution.py:87
  9.7 19.4 %all-to-all-start = ((bf16[16,160,128]{2,1,0:T(8,128)(2,1)}), bf16[16,160,128]{2,1,0:T(8,128)(2,1)S(1)}, u32[]{:S(2)}, u32[]{:S(2)}) async-start(bf16[16,160,128]{2,1,0:T(8,128)(2,1)} %shard_map.63), calls=%async_computation | async-start | bytes 1310720 | tf_op jit(solution)/shard_map/all_to_all | solution.py:287
  29.2 0.6 shard_map.59
  29.8 2.9 %collective-permute-start = (bf16[4,2,128,256]{3,2,1,0:T(8,128)(2,1)S(1)}, bf16[4,2,128,256]{3,2,1,0:T(8,128)(2,1)S(1)}, u32[]{:S(2)}, u32[]{:S(2)}) collective-permute-start(bf16[4,2,128,256]{3,2,1,0:T(8,128)(2,1)S(1)} %get-tuple-element.16), channel_id=1, source_target_pairs={{0,128},{128,0},{1,129},{129,1},{2,130},{130,2},{3,131},{131,3},{4... | collective-permute-start | bytes 1572872 | tf_op jit(solution)/shard_map/ppermute | solution.py:343
  32.7 0.2 select_reduce_fusion.1
  32.9 0.1 select_reduce_fusion
  33.0 0.1 sub.17
  33.1 1.1 collective-permute-done.came
  34.2 0.7 shard_map.60
  34.8 3.1 %collective-permute-start.1 = (bf16[2,128,256]{2,1,0:T(8,128)(2,1)S(1)}, bf16[2,128,256]{2,1,0:T(8,128)(2,1)S(1)}, u32[]{:S(2)}, u32[]{:S(2)}) collective-permute-start(bf16[2,128,256]{2,1,0:T(8,128)(2,1)S(1)} %get-tuple-element.18), channel_id=1, source_target_pairs={{0,256},{256,512},{512,768},{768,0},{1,257},{257,513},{513,769},{7... | collective-permute-start | bytes 393224 | tf_op jit(solution)/shard_map/ppermute | solution.py:349
  38.0 4.4 %collective-permute-start.2 = (bf16[2,128,256]{2,1,0:T(8,128)(2,1)S(1)}, bf16[2,128,256]{2,1,0:T(8,128)(2,1)S(1)}, u32[]{:S(2)}, u32[]{:S(2)}) collective-permute-start(bf16[2,128,256]{2,1,0:T(8,128)(2,1)S(1)} %get-tuple-element.19), channel_id=1, source_target_pairs={{0,512},{256,768},{512,0},{768,256},{1,513},{257,769},{513,1},{769... | collective-permute-start | bytes 393224 | tf_op jit(solution)/shard_map/ppermute | solution.py:349
  42.3 3.1 %collective-permute-start.3 = (bf16[2,128,256]{2,1,0:T(8,128)(2,1)S(1)}, bf16[2,128,256]{2,1,0:T(8,128)(2,1)S(1)}, u32[]{:S(2)}, u32[]{:S(2)}) collective-permute-start(bf16[2,128,256]{2,1,0:T(8,128)(2,1)S(1)} %get-tuple-element.20), channel_id=1, source_target_pairs={{0,768},{256,0},{512,256},{768,512},{1,769},{257,1},{513,257},{769... | collective-permute-start | bytes 393224 | tf_op jit(solution)/shard_map/ppermute | solution.py:349
  45.4 0.7 dynamic_slice.24
  46.1 0.1 reshape_squeeze.3
  46.9 0.1 dynamic_slice.22
  47.0 0.1 dynamic_slice.25
  47.1 0.1 and_select_fusion.3
  47.2 0.1 concatenate.3.table
  47.2 0.0 collective-permute-done.2.refs_2_
  47.3 1.1 collective-permute-done.3.refs_3_
  48.3 1.3 shard_map.61
  49.6 33.8 %all-gather = bf16[8,128,256]{2,1,0:T(8,128)(2,1)S(1)} all-gather(bf16[2,128,256]{2,1,0:T(8,128)(2,1)} %shard_map.61), channel_id=2, replica_groups=mesh['x'=4,'core'=2,'zl'=4,'y'=8,'zh'=4] {'zh'}, dimensions={0}, use_global_device_ids=true | all-gather | bytes 655360 | tf_op jit(solution)/shard_map/all_gather | solution.py:355
  83.4 0.0 all-to-all-done.tiles
  83.4 1.4 shard_map.64
  84.9 6.8 %all-to-all-start.1 = ((bf16[8,2,160,128]{3,2,1,0:T(8,128)(2,1)}), bf16[8,2,160,128]{3,2,1,0:T(8,128)(2,1)S(1)}, u32[]{:S(2)}, u32[]{:S(2)}) async-start(bf16[8,2,160,128]{3,2,1,0:T(8,128)(2,1)} %bitcast.7), calls=%async_computation.1 | async-start | bytes 1310720 | tf_op jit(solution)/shard_map/all_to_all | solution.py:287
  91.7 0.0 all-gather.9.cloned.1.call-start
  91.7 0.7 all-gather.9.cloned.1.call-update
  92.5 2.3 %collective-permute-start.4 = (bf16[4,2,32,256]{3,2,1,0:T(8,128)(2,1)S(1)}, bf16[4,2,32,256]{3,2,1,0:T(8,128)(2,1)S(1)}, u32[]{:S(2)}, u32[]{:S(2)}) collective-permute-start(bf16[4,2,32,256]{3,2,1,0:T(8,128)(2,1)S(1)} %constant_dynamic-slice_fusion), channel_id=1, source_target_pairs={{0,896},{128,0},{256,128},{384,256},{512,384},{640,512},{768,640},... | collective-permute-start | bytes 393224 | tf_op jit(solution)/shard_map/ppermute | solution.py:291
  94.8 3.7 %collective-permute-start.5 = (bf16[4,2,32,256]{3,2,1,0:T(8,128)(2,1)S(1)}, bf16[4,2,32,256]{3,2,1,0:T(8,128)(2,1)S(1)}, u32[]{:S(2)}, u32[]{:S(2)}) collective-permute-start(bf16[4,2,32,256]{3,2,1,0:T(8,128)(2,1)S(1)} %constant_dynamic-slice_fusion), channel_id=1, source_target_pairs={{0,768},{128,896},{256,0},{384,128},{512,256},{640,384},{768,512},... | collective-permute-start | bytes 393224 | tf_op jit(solution)/shard_map/ppermute | solution.py:291
  98.5 2.2 %collective-permute-start.6 = (bf16[4,2,32,256]{3,2,1,0:T(8,128)(2,1)S(1)}, bf16[4,2,32,256]{3,2,1,0:T(8,128)(2,1)S(1)}, u32[]{:S(2)}, u32[]{:S(2)}) collective-permute-start(bf16[4,2,32,256]{3,2,1,0:T(8,128)(2,1)S(1)} %constant_dynamic-slice_fusion), channel_id=1, source_target_pairs={{0,640},{128,768},{256,896},{384,0},{512,128},{640,256},{768,384},... | collective-permute-start | bytes 393224 | tf_op jit(solution)/shard_map/ppermute | solution.py:291
  100.7 3.5 %collective-permute-start.7 = (bf16[4,2,32,256]{3,2,1,0:T(8,128)(2,1)S(1)}, bf16[4,2,32,256]{3,2,1,0:T(8,128)(2,1)S(1)}, u32[]{:S(2)}, u32[]{:S(2)}) collective-permute-start(bf16[4,2,32,256]{3,2,1,0:T(8,128)(2,1)S(1)} %constant_dynamic-slice_fusion), channel_id=1, source_target_pairs={{0,512},{128,640},{256,768},{384,896},{512,0},{640,128},{768,256},... | collective-permute-start | bytes 393224 | tf_op jit(solution)/shard_map/ppermute | solution.py:291
  104.3 2.4 %collective-permute-done.6.refs_2_ = bf16[4,2,32,256]{3,2,1,0:T(8,128)(2,1)S(1)} collective-permute-done((bf16[4,2,32,256]{3,2,1,0:T(8,128)(2,1)S(1)}, bf16[4,2,32,256]{3,2,1,0:T(8,128)(2,1)S(1)}, u32[]{:S(2)}, u32[]{:S(2)}) %collective-permute-start.6) | collective-permute-done | bytes 131104 | tf_op jit(solution)/shard_map/ppermute | solution.py:291
  106.6 2.1 %collective-permute-done.7.refs_3_ = bf16[4,2,32,256]{3,2,1,0:T(8,128)(2,1)S(1)} collective-permute-done((bf16[4,2,32,256]{3,2,1,0:T(8,128)(2,1)S(1)}, bf16[4,2,32,256]{3,2,1,0:T(8,128)(2,1)S(1)}, u32[]{:S(2)}, u32[]{:S(2)}) %collective-permute-start.7) | collective-permute-done | bytes 131104 | tf_op jit(solution)/shard_map/ppermute | solution.py:291
  108.7 1.8 shard_map.62
  110.5 6.9 %all-to-all-start.2 = ((bf16[8,2,160,128]{3,2,1,0:T(8,128)(2,1)}), bf16[8,2,160,128]{3,2,1,0:T(8,128)(2,1)S(1)}, u32[]{:S(2)}, u32[]{:S(2)}) async-start(bf16[8,2,160,128]{3,2,1,0:T(8,128)(2,1)} %get-tuple-element.23), calls=%async_computation.2 | async-start | bytes 1310720 | tf_op jit(solution)/shard_map/all_to_all | solution.py:287
  117.4 0.0 all-gather.7.cloned.1.call-start
  117.5 0.6 shard_map.65
  118.0 21.0 %all-gather.1 = bf16[8,160,128]{2,1,0:T(8,128)(2,1)} all-gather(bf16[2,160,128]{2,1,0:T(8,128)(2,1)S(1)} %shard_map.65), channel_id=3, replica_groups=mesh['x'=4,'core'=2,'zl'=4,'y'=8,'zh'=4] {'zh'}, dimensions={0}, use_global_device_ids=true | all-gather | bytes 409600 | tf_op jit(solution)/shard_map/all_gather | solution.py:369
  139.0 0.0 all-gather.7.cloned.1.call-update
  139.0 0.6 shard_map.67
  139.6 18.3 %all_to_all.30.came = bf16[16,160,128]{2,1,0:T(8,128)(2,1)S(1)} all-to-all(bf16[16,160,128]{2,1,0:T(8,128)(2,1)S(1)} %shard_map.67), channel_id=1, replica_groups=mesh['x'=4,'core'=2,'zl'=4,'y'=8,'zh'=4] {'zl'}, dimensions={0} | all-to-all | bytes 1310720 | tf_op jit(solution)/shard_map/all_to_all | solution.py:287
  158.0 0.6 shard_map.68
  158.5 20.0 %all_to_all.31.came = bf16[4,160,128]{2,1,0:T(8,128)(2,1)S(1)} all-to-all(bf16[4,160,128]{2,1,0:T(8,128)(2,1)S(1)} %shard_map.68), channel_id=1, replica_groups=mesh['x'=4,'core'=2,'zl'=4,'y'=8,'zh'=4] {'zh'}, dimensions={0} | all-to-all | bytes 327680 | tf_op jit(solution)/shard_map/all_to_all | solution.py:287
  178.5 1.3 shard_map.69
  179.8 7.6 %all-to-all-start.5 = ((bf16[8,128,128]{2,1,0:T(8,128)(2,1)}), bf16[8,128,128]{2,1,0:T(8,128)(2,1)S(1)}, u32[]{:S(2)}, u32[]{:S(2)}) async-start(bf16[8,128,128]{2,1,0:T(8,128)(2,1)} %get-tuple-element.26), calls=%async_computation.5 | async-start | bytes 524288 | tf_op jit(solution)/shard_map/all_to_all | solution.py:287
  187.4 7.5 %shard_map.66 = bf16[2,128,256]{2,1,0:T(8,128)(2,1)} custom-call(s32[43]{0:T(128)S(1)} %concatenate.3.table, bf16[8,4,2,160,128]{4,3,2,1,0:T(8,128)(2,1)} %bitcast.22, bf16[8,2,128,256]{3,2,1,0:T(8,128)(2,1)} %bitcast.24), custom_call_target="tpu_custom_call" | custom-call | tf_op jit(solution)/shard_map/pallas_call | solution.py:269
  194.9 1.4 shard_map.70
  (22 shorter events, 0.1 us)
Async XLA Ops:
  7.2 22.0 %copy-start.1 = (bf16[1,2,1024,256]{3,2,1,0:T(8,128)(2,1)S(1)}, bf16[1,2,1024,256]{3,2,1,0:T(8,128)(2,1)}, u32[]{:S(2)}) copy-start(bf16[1,2,1024,256]{3,2,1,0:T(8,128)(2,1)} %param.4) | copy-start | bytes 3145732
  7.2 25.5 %copy-start.2 = (s32[64]{0:T(128)S(1)}, s32[64]{0:T(128)}, u32[]{:S(2)}) copy-start(s32[64]{0:T(128)} %param.5) | copy-start | bytes 772
  7.3 39.6 %copy-start.3 = (s32[64]{0:T(128)S(1)}, s32[64]{0:T(128)}, u32[]{:S(2)}) copy-start(s32[64]{0:T(128)} %param.6) | copy-start | bytes 772
  9.7 73.7 %all-to-all-start = ((bf16[16,160,128]{2,1,0:T(8,128)(2,1)}), bf16[16,160,128]{2,1,0:T(8,128)(2,1)S(1)}, u32[]{:S(2)}, u32[]{:S(2)}) async-start(bf16[16,160,128]{2,1,0:T(8,128)(2,1)} %shard_map.63), calls=%async_computation | async-start | bytes 1310720 | tf_op jit(solution)/shard_map/all_to_all | solution.py:287
  29.8 4.4 %collective-permute-start = (bf16[4,2,128,256]{3,2,1,0:T(8,128)(2,1)S(1)}, bf16[4,2,128,256]{3,2,1,0:T(8,128)(2,1)S(1)}, u32[]{:S(2)}, u32[]{:S(2)}) collective-permute-start(bf16[4,2,128,256]{3,2,1,0:T(8,128)(2,1)S(1)} %get-tuple-element.16), channel_id=1, source_target_pairs={{0,128},{128,0},{1,129},{129,1},{2,130},{130,2},{3,131},{131,3},{4... | collective-permute-start | bytes 1572872 | tf_op jit(solution)/shard_map/ppermute | solution.py:343
  34.8 12.4 %collective-permute-start.1 = (bf16[2,128,256]{2,1,0:T(8,128)(2,1)S(1)}, bf16[2,128,256]{2,1,0:T(8,128)(2,1)S(1)}, u32[]{:S(2)}, u32[]{:S(2)}) collective-permute-start(bf16[2,128,256]{2,1,0:T(8,128)(2,1)S(1)} %get-tuple-element.18), channel_id=1, source_target_pairs={{0,256},{256,512},{512,768},{768,0},{1,257},{257,513},{513,769},{7... | collective-permute-start | bytes 393224 | tf_op jit(solution)/shard_map/ppermute | solution.py:349
  38.0 9.3 %collective-permute-start.2 = (bf16[2,128,256]{2,1,0:T(8,128)(2,1)S(1)}, bf16[2,128,256]{2,1,0:T(8,128)(2,1)S(1)}, u32[]{:S(2)}, u32[]{:S(2)}) collective-permute-start(bf16[2,128,256]{2,1,0:T(8,128)(2,1)S(1)} %get-tuple-element.19), channel_id=1, source_target_pairs={{0,512},{256,768},{512,0},{768,256},{1,513},{257,769},{513,1},{769... | collective-permute-start | bytes 393224 | tf_op jit(solution)/shard_map/ppermute | solution.py:349
  42.3 6.0 %collective-permute-start.3 = (bf16[2,128,256]{2,1,0:T(8,128)(2,1)S(1)}, bf16[2,128,256]{2,1,0:T(8,128)(2,1)S(1)}, u32[]{:S(2)}, u32[]{:S(2)}) collective-permute-start(bf16[2,128,256]{2,1,0:T(8,128)(2,1)S(1)} %get-tuple-element.20), channel_id=1, source_target_pairs={{0,768},{256,0},{512,256},{768,512},{1,769},{257,1},{513,257},{769... | collective-permute-start | bytes 393224 | tf_op jit(solution)/shard_map/ppermute | solution.py:349
  84.9 25.6 %all-to-all-start.1 = ((bf16[8,2,160,128]{3,2,1,0:T(8,128)(2,1)}), bf16[8,2,160,128]{3,2,1,0:T(8,128)(2,1)S(1)}, u32[]{:S(2)}, u32[]{:S(2)}) async-start(bf16[8,2,160,128]{3,2,1,0:T(8,128)(2,1)} %bitcast.7), calls=%async_computation.1 | async-start | bytes 1310720 | tf_op jit(solution)/shard_map/all_to_all | solution.py:287
  91.7 95.7 %all-gather.9.cloned.1.call-start = ((), (), s32[]{:S(2)}) async-start(), calls=%async_computation.7 | async-start | bytes 1179648 | tf_op jit(solution)/shard_map/all_gather | solution.py:353
  92.5 11.8 %collective-permute-start.4 = (bf16[4,2,32,256]{3,2,1,0:T(8,128)(2,1)S(1)}, bf16[4,2,32,256]{3,2,1,0:T(8,128)(2,1)S(1)}, u32[]{:S(2)}, u32[]{:S(2)}) collective-permute-start(bf16[4,2,32,256]{3,2,1,0:T(8,128)(2,1)S(1)} %constant_dynamic-slice_fusion), channel_id=1, source_target_pairs={{0,896},{128,0},{256,128},{384,256},{512,384},{640,512},{768,640},... | collective-permute-start | bytes 393224 | tf_op jit(solution)/shard_map/ppermute | solution.py:291
  94.8 9.5 %collective-permute-start.5 = (bf16[4,2,32,256]{3,2,1,0:T(8,128)(2,1)S(1)}, bf16[4,2,32,256]{3,2,1,0:T(8,128)(2,1)S(1)}, u32[]{:S(2)}, u32[]{:S(2)}) collective-permute-start(bf16[4,2,32,256]{3,2,1,0:T(8,128)(2,1)S(1)} %constant_dynamic-slice_fusion), channel_id=1, source_target_pairs={{0,768},{128,896},{256,0},{384,128},{512,256},{640,384},{768,512},... | collective-permute-start | bytes 393224 | tf_op jit(solution)/shard_map/ppermute | solution.py:291
  98.5 8.1 %collective-permute-start.6 = (bf16[4,2,32,256]{3,2,1,0:T(8,128)(2,1)S(1)}, bf16[4,2,32,256]{3,2,1,0:T(8,128)(2,1)S(1)}, u32[]{:S(2)}, u32[]{:S(2)}) collective-permute-start(bf16[4,2,32,256]{3,2,1,0:T(8,128)(2,1)S(1)} %constant_dynamic-slice_fusion), channel_id=1, source_target_pairs={{0,640},{128,768},{256,896},{384,0},{512,128},{640,256},{768,384},... | collective-permute-start | bytes 393224 | tf_op jit(solution)/shard_map/ppermute | solution.py:291
  100.7 8.0 %collective-permute-start.7 = (bf16[4,2,32,256]{3,2,1,0:T(8,128)(2,1)S(1)}, bf16[4,2,32,256]{3,2,1,0:T(8,128)(2,1)S(1)}, u32[]{:S(2)}, u32[]{:S(2)}) collective-permute-start(bf16[4,2,32,256]{3,2,1,0:T(8,128)(2,1)S(1)} %constant_dynamic-slice_fusion), channel_id=1, source_target_pairs={{0,512},{128,640},{256,768},{384,896},{512,0},{640,128},{768,256},... | collective-permute-start | bytes 393224 | tf_op jit(solution)/shard_map/ppermute | solution.py:291
  110.5 28.5 %all-to-all-start.2 = ((bf16[8,2,160,128]{3,2,1,0:T(8,128)(2,1)}), bf16[8,2,160,128]{3,2,1,0:T(8,128)(2,1)S(1)}, u32[]{:S(2)}, u32[]{:S(2)}) async-start(bf16[8,2,160,128]{3,2,1,0:T(8,128)(2,1)} %get-tuple-element.23), calls=%async_computation.2 | async-start | bytes 1310720 | tf_op jit(solution)/shard_map/all_to_all | solution.py:287
  117.4 69.9 %all-gather.7.cloned.1.call-start = ((), (), s32[]{:S(2)}) async-start(), calls=%async_computation.6 | async-start | bytes 2949120 | tf_op jit(solution)/shard_map/all_gather | solution.py:371
  158.0 36.9 %copy-start = (bf16[1,1,1024,1024]{3,2,1,0:T(8,128)(2,1)S(1)}, bf16[1,1,1024,1024]{3,2,1,0:T(8,128)(2,1)}, u32[]{:S(2)}) copy-start(bf16[1,1,1024,1024]{3,2,1,0:T(8,128)(2,1)} %param.7) | copy-start | bytes 6291460
  179.8 15.1 %all-to-all-start.5 = ((bf16[8,128,128]{2,1,0:T(8,128)(2,1)}), bf16[8,128,128]{2,1,0:T(8,128)(2,1)S(1)}, u32[]{:S(2)}, u32[]{:S(2)}) async-start(bf16[8,128,128]{2,1,0:T(8,128)(2,1)} %get-tuple-element.26), calls=%async_computation.5 | async-start | bytes 524288 | tf_op jit(solution)/shard_map/all_to_all | solution.py:287
Sparse Core Ops, SparseCore 0:
  95.8 31.7 all-gather.8
  139.2 34.3 all-gather.6
